TPU v7x, 32 devices: a whole 2x2x4 slice. The times are simulated.
32 devices in a mesh: parts: 2 (over y), win: 16 (over z, x, core).
Axes of the slice: x: 2, y: 2, z: 4, core: 2. Of those that a mesh axis runs over, the one named last changes fastest.
Arguments:
- records: bfloat16 [2048, 8192], P('win', 'parts'), parts along dimension 1, may hold values from -45 to 45
- templates: bfloat16 [2, 64, 128, 512], P(None, None, 'win'), may hold values from -16 to 16
- panel_start: int32 [4], P('parts'), parts along dimension 0, may hold values from 0 to 1920
Outputs:
- traces: float32 [8192, 128], P(('parts', 'win')), parts along dimension 0
There are 2 independent parts, one for each index of `parts`. A program takes and returns all parts, laid end to end along the dimension named above; an argument that names none is the same for every part. Nothing has to cross between parts.
Inputs may be any that keep to these rules, and one draw needn't show every extreme that they name: Each panel covers channels panel_start to panel_start + 127; panels may share channels.
All inputs are finite; a program needn't handle non-finite values.
Results may differ from a plain program's by a relative error of at most 0.0003.
Values may be sent and summed in bfloat16 or wider, within the bound.
No kernel may reach another device: no remote copies, remote signals or barrier semaphores. Data moves between devices by JAX's collectives and lax.ppermute only.
A program may use at most 128 MiB of HBM per device.

v0:
```python
import math

import jax
import jax.numpy as jnp
from jax import lax
from jax.sharding import PartitionSpec as P

P_SIZE = 2
G = 64
CT = 128
L = 512


epsilon = 1e-06


def from_behind(value, axis, steps):
    count = lax.axis_size(axis)
    first, last = (max(0, -steps), min(count, count - steps))
    return lax.ppermute(value, axis, [(source, source + steps) for source in range(first, last)])


def correlate(strip, kernels):
    panels, rows, length = strip.shape
    groups = kernels.shape[1]
    inputs = strip.reshape(1, panels * rows, length)
    filters = kernels.reshape(panels * groups, rows, kernels.shape[3])
    result = lax.conv_general_dilated(
        inputs,
        filters,
        (1,),
        "VALID",
        dimension_numbers=("NCH", "OIH", "NCH"),
        feature_group_count=panels,
        preferred_element_type=jnp.float32,
    )
    return result.reshape(panels, groups, result.shape[2])


def extend(segment, sender, local_len):
    portions = [segment]
    hop_count = (L - 2) // local_len + 1
    for distance in range(1, hop_count + 1):
        amount = min(local_len, L - 1 - (distance - 1) * local_len)
        portions.append(sender(segment[..., :amount], distance))
    return jnp.concatenate(portions, axis=-1)


def pick_panels(window, panel_start):
    return jnp.stack(
        [lax.dynamic_slice_in_dim(window, panel_start[panel], CT, 0) for panel in range(P_SIZE)]
    )


def local(records, templates, panel_start):
    window = lax.all_to_all(records, "win", split_axis=1, concat_axis=0, tiled=True)
    local_len = window.shape[1]

    def sender(portion, distance):
        return from_behind(portion, "win", -distance)

    chosen = pick_panels(extend(window, sender, local_len), panel_start)
    squares = jnp.sum(jnp.square(chosen.astype(jnp.float32)), axis=1)
    energy = lax.reduce_window(squares, jnp.float32(0.0), lax.add, (1, L), (1, 1), "VALID")
    own_norm = jnp.sum(jnp.square(templates.astype(jnp.float32)), axis=(2, 3))
    template_norm = lax.psum(own_norm, "win")
    initial = jnp.zeros((P_SIZE, G, local_len), jnp.float32)
    summed = initial + correlate(chosen, lax.all_gather(templates, "win", axis=2, tiled=True))
    correlation = jnp.transpose(summed, (2, 0, 1))
    scaled = math.sqrt(CT * L) * correlation * lax.rsqrt(template_norm)[None, :, :]
    traces = scaled * lax.rsqrt(energy + epsilon).T[:, :, None]
    return traces.reshape(local_len, P_SIZE * G)


def solution(mesh):
    placed = (P("win", "parts"), P(None, None, "win", None), P("parts"))
    return jax.shard_map(
        local, mesh=mesh, in_specs=placed, out_specs=P(("parts", "win"), None), check_vma=False
    )
```

profile of v0, /device:TPU:0, one launch (start us, length us, event | category | flops | bytes accessed | tf_op | source)
XLA Modules:
  0.0 419.5 jit_solution(6883028820602811246)
XLA Ops:
  6.5 0.0 copy-start
  6.5 0.0 copy-start.3
  6.5 0.0 all-gather.2.cloned.1.call-start
  6.5 4.9 %copy.8 = bf16[2,64,8,512]{1,2,0,3:T(8,128)(2,1)} copy(bf16[2,64,8,512]{3,2,1,0:T(8,128)(2,1)} %param.4) | data formatting | bytes 2097152 | tf_op args[1]
  11.5 0.0 all-gather.2.cloned.1.call-update
  11.5 1.3 copy.15
  12.8 46.6 %all_to_all.19 = bf16[128,16,256]{2,0,1:T(8,128)(2,1)S(1)} all-to-all(bf16[128,16,256]{2,0,1:T(8,128)(2,1)S(1)} %bitcast.24), channel_id=1, replica_groups=mesh['parts'=2,'win'=16] {'win'}, dimensions={1} | all-to-all | bytes 2097152 | tf_op jit(solution)/shard_map/all_to_all | solution.py:56
  59.4 1.3 collective-permute-start
  60.7 1.3 collective-permute-start.1
  62.0 0.0 copy-done.3
  62.0 0.6 fusion.1
  66.5 0.0 copy-done
  66.5 0.6 multiply_reduce_fusion
  67.1 89.9 %psum.7 = f32[2,64]{1,0:T(2,128)S(1)} all-reduce(f32[2,64]{1,0:T(2,128)S(1)} %multiply_reduce_fusion), channel_id=1, replica_groups=mesh['parts'=2,'win'=16] {'win'}, use_global_device_ids=true, to_apply=%region_1.0 | all-reduce | flops 128 | bytes 1024 | tf_op jit(solution)/shard_map/psum | solution.py:66
  157.0 0.6 rsqrt_multiply_fusion
  157.5 0.0 collective-permute-done.1
  157.5 0.0 collective-permute-done
  157.5 1.6 pad_maximum_fusion
  159.2 0.1 dynamic-slice_bitcast_fusion.1
  159.3 0.1 multiply_reduce_fusion.1
  159.4 17.8 %reduce_window.7 = f32[2,256]{1,0:T(2,128)S(1)} reduce-window(f32[2,767]{1,0:T(2,128)S(1)} %multiply_reduce_fusion.1, f32[]{:T(128)} %constant.4.clone.1), window={size=1x512}, to_apply=%region_3.0 | reduce-window | flops 261632 | bytes 8188 | tf_op jit(solution)/shard_map/reduce_window | solution.py:64
  177.2 0.8 copy.10
  178.1 1.0 copy.9
  179.1 66.8 %all-gather.2.cloned.1.call-done = bf16[2,64,128,512]{1,2,0,3:T(8,128)(2,1)} async-done(((bf16[2,64,8,512]{1,2,0,3:T(8,128)(2,1)}), bf16[2,64,128,512]{1,2,0,3:T(8,128)(2,1)}) %all-gather.2.cloned.1.call-update) | async-done | bytes 16777232 | tf_op jit(solution)/shard_map/all_gather | solution.py:68
  245.8 0.0 copy-start.1
  245.8 0.0 copy-start.2
  245.8 165.2 %fusion.2 = f32[1,2,64,256]{2,0,1,3:T(1,128)S(1)} fusion(bf16[1,2,128,767]{2,0,1,3:T(2,128)(2,1)S(1)} %copy.9, bf16[2,64,128,512]{1,2,0,3:T(8,128)(2,1)} %all-gather.2.cloned.1.call-done), kind=kOutput, calls=%fused_computation.12 | convolution fusion | flops 4294967296 | bytes 17300992 | tf_op jit(solution)/shard_map/conv_general_dilated | solution.py:28
  411.1 0.0 copy-done.1
  411.1 0.0 copy-done.2
  411.1 0.3 bitcast_multiply_fusion
  411.4 0.1 copy.11
  411.5 0.8 copy.12
  (2 shorter events, 0.0 us)
Async XLA Ops:
  6.5 60.0 %copy-start = (bf16[2,64,8,512]{3,2,1,0:T(8,128)(2,1)S(1)}, bf16[2,64,8,512]{3,2,1,0:T(8,128)(2,1)}, u32[]{:S(2)}) copy-start(bf16[2,64,8,512]{3,2,1,0:T(8,128)(2,1)} %param.4) | copy-start | bytes 3145732
  6.5 55.5 %copy-start.3 = (s32[2]{0:T(128)S(1)}, s32[2]{0:T(128)}, u32[]{:S(2)}) copy-start(s32[2]{0:T(128)} %param.5) | copy-start | bytes 28
  6.5 239.3 %all-gather.2.cloned.1.call-start = ((), (), s32[]{:S(2)}) async-start(), calls=%async_computation.1 | async-start | bytes 35651584 | tf_op jit(solution)/shard_map/all_gather | solution.py:68
  59.4 98.1 %collective-permute-start = (bf16[2048,256]{1,0:T(8,128)(2,1)S(1)}, bf16[2048,256]{1,0:T(8,128)(2,1)S(1)}, u32[]{:S(2)}, u32[]{:S(2)}) collective-permute-start(bf16[2048,256]{1,0:T(8,128)(2,1)S(1)} %bitcast.25), channel_id=1, source_target_pairs={{1,0},{2,1},{3,2},{4,3},{5,4},{6,5},{7,6},{8,7},{9,8},{10,9},{11,1... | collective-permute-start | bytes 3145736 | tf_op jit(solution)/shard_map/ppermute | solution.py:20
  60.7 96.8 %collective-permute-start.1 = (bf16[2048,255]{1,0:T(8,128)(2,1)S(1)}, bf16[2048,255]{1,0:T(8,128)(2,1)}, u32[]{:S(2)}, u32[]{:S(2)}) collective-permute-start(bf16[2048,255]{1,0:T(8,128)(2,1)S(1)} %bitcast.26), channel_id=1, source_target_pairs={{2,0},{3,1},{4,2},{5,3},{6,4},{7,5},{8,6},{9,7},{10,8},{11,9},{12,... | collective-permute-start | bytes 3133448 | tf_op jit(solution)/shard_map/ppermute | solution.py:20
  245.8 165.2 %copy-start.1 = (f32[256,2]{1,0:T(8,128)S(1)}, f32[256,2]{1,0:T(8,128)}, u32[]{:S(2)}) copy-start(f32[256,2]{1,0:T(8,128)} %copy.10) | copy-start | bytes 6148
  245.8 165.2 %copy-start.2 = (f32[2,64]{1,0:T(2,128)S(1)}, f32[2,64]{1,0:T(2,128)}, u32[]{:S(2)}) copy-start(f32[2,64]{1,0:T(2,128)} %rsqrt_multiply_fusion) | copy-start | bytes 1540
Sparse Core Ops, SparseCore 0:
  11.6 234.1 all-gather.1
where the time goes:
time: 422 us; the launch traced here: 420 us
  matrix products  165 us (39%)
  blocking collectives  136 us (32%)
  waiting for transfers between devices  66.8 us (16%)
  other arithmetic  21.1 us (5%)
  between operations  17.8 us (4%)
  local copies, waits for them, and re-layouts  9.66 us (2%)
    conv_general_dilated x1, matrix products, correlate(): lax.conv_general_dilated(inputs, filters, (1,), 'VALID', dimension_number...  165 us
    psum x1, blocking collectives, local(): template_norm = lax.psum(own_norm, 'win')  89.9 us
    all_gather x1, waiting for transfers between devices, local(): lax.all_gather(templates, 'win', axis=2, tiled=True)  66.8 us
    all_to_all x1, blocking collectives, local(): lax.all_to_all(records, 'win', split_axis=1, concat_axis=0, tiled=True)  46.6 us
    another operation x1, other arithmetic, local(): lax.reduce_window(squares, jnp.float32(0.0), lax.add, (1, L), (1, 1), 'VA...  17.8 us
  transfers between devices with their start and end apart: 3, of which 1 were waited for; matrix products, arithmetic and copies ran while one was open for 6% of the time, Pallas kernels for 0%

commit v1 on v0

v1 whole, which is shorter than its diff:
```python
import math

import jax
import jax.numpy as jnp
from jax import lax
from jax.experimental import pallas as pl
from jax.experimental.pallas import tpu as pltpu
from jax.sharding import PartitionSpec as P

CT = 128
L = 512
LANES = 128
epsilon = 1e-06
f32 = jnp.float32
bf16 = jnp.bfloat16
VMEM_BYTES = 60 * 2**20


def iota(shape, dim):
    return lax.broadcasted_iota(jnp.int32, shape, dim)


def dot(a, b, dims=(((1,), (0,)), ((), ()))):
    return lax.dot_general(a, b, dims, preferred_element_type=f32)


def split3(v):
    high = v.astype(bf16)
    rest = v - high.astype(f32)
    middle = rest.astype(bf16)
    return high, middle, (rest - middle.astype(f32)).astype(bf16)


def pick(v, m):
    return sum(dot(part, m) for part in split3(v))


def picked(m, v):
    return sum(dot(m, part) for part in split3(v))


def shift_kernel(own_ref, other_ref, w_ref, norm_ref, rows_ref, *, phases):
    gc = own_ref.shape[0]
    groups = LANES // 2
    each = gc // groups
    channels = 2 * each
    pad = channels * phases
    total = rows_ref.shape[0]
    rows_ref[pl.ds(0, pad), :] = jnp.zeros((pad, LANES), f32)
    rows_ref[pl.ds(pad + L * channels, total - pad - L * channels), :] = jnp.zeros(
        (total - pad - L * channels, LANES), f32
    )
    norm = jnp.zeros((1, LANES), f32)
    row, lane = iota((gc, LANES), 0), iota((gc, LANES), 1)
    for side, ref in enumerate((own_ref, other_ref)):
        for c in range(each):
            choose = (row == (lane % groups) * each + c).astype(f32).astype(bf16)
            piece = dot(ref[...], choose, (((0,), (0,)), ((), ())))
            norm = norm + jnp.sum(piece * piece, axis=0, keepdims=True)
            rows_ref[pl.ds(pad + side * each + c, L, stride=channels), :] = piece
    norm_ref[...] = jnp.broadcast_to(norm, norm_ref.shape)
    low = iota((256, LANES), 1) < groups
    for q in range(w_ref.shape[0]):
        for tile in range(phases // 2):
            start = pad + 256 * q - 2 * tile * channels
            even = rows_ref[pl.ds(start, 256), :]
            odd = rows_ref[pl.ds(start - channels, 256), :]
            w_ref[q, :, tile * LANES : (tile + 1) * LANES] = jnp.where(low, even, odd).astype(bf16)


def shifted(own, other, phases, pairs):
    channels = 2 * own.shape[1]
    rows = 256 * pairs + channels * phases
    gc = own.shape[0] * own.shape[1]
    return pl.pallas_call(
        lambda *refs: shift_kernel(*refs, phases=phases),
        out_shape=(
            jax.ShapeDtypeStruct((pairs, 256, phases * 64), bf16),
            jax.ShapeDtypeStruct((8, LANES), f32),
        ),
        scratch_shapes=[pltpu.VMEM((rows, LANES), f32)],
        compiler_params=pltpu.CompilerParams(vmem_limit_bytes=VMEM_BYTES),
        cost_estimate=pl.CostEstimate(flops=2**30, bytes_accessed=2**24, transcendentals=0),
        name="shift_templates",
    )(own.reshape(gc, L), other.reshape(gc, L))


def correlate_kernel(*refs, phases, za, zb, n_early, n_late):
    ix_ref = refs[0]
    early = refs[1 : 1 + n_early]
    late = refs[1 + n_early : 1 + n_early + n_late]
    w_ref, norm_ref = refs[1 + n_early + n_late : 3 + n_early + n_late]
    zs = n_early
    outs = refs[3 + n_early + n_late :]
    keep_a, send_a, keep_b = outs[:3]
    send_b = outs[3 : 2 + zs]
    spread_ref, rows_ref, slide_ref, acc_ref, wbuf_ref, sem = outs[2 + zs :]

    pairs = w_ref.shape[0]
    for q in range(pairs):
        pltpu.make_async_copy(w_ref.at[q], wbuf_ref.at[q], sem.at[q]).start()

    channels = LANES // phases
    first, second = sum(r[...] for r in early[1:]) + early[0][...], late[0][...] + late[1][...]
    repeat = (iota((channels, LANES), 0) == iota((channels, LANES), 1) % channels).astype(f32).astype(bf16)
    ta, tb = first.shape[1], second.shape[1]
    spread_ref[pl.ds(0, ta), :] = dot(first, repeat, (((0,), (0,)), ((), ())))
    spread_ref[pl.ds(ta, tb), :] = dot(second, repeat, (((0,), (0,)), ((), ())))
    count = (ta + tb) // phases
    phase = iota((count, LANES), 1) // channels
    rows = jnp.zeros((count, LANES), f32)
    for k in range(phases):
        rows = jnp.where(phase == k, spread_ref[pl.ds(k, count, stride=phases), :], rows)
    total = rows_ref.shape[0]
    rows_ref[pl.ds(0, count), :] = rows
    rows_ref[pl.ds(count, total - count), :] = jnp.zeros((total - count, LANES), f32)

    span = slide_ref.shape[1]
    for k in range(min(8, pairs)):
        slide_ref[k, :, 0:LANES] = rows_ref[pl.ds(2 * k, span), :].astype(bf16)
        slide_ref[k, :, LANES:] = rows_ref[pl.ds(2 * k + 1, span), :].astype(bf16)

    per = L // phases
    left, right = iota((LANES, LANES), 0) // channels, iota((LANES, LANES), 1) % (2 * phases)
    inside = right < phases
    tail = (inside & (left >= right)).astype(f32).astype(bf16)
    head = (inside & (left < right)).astype(f32).astype(bf16)
    squares = rows * rows
    sums = jnp.broadcast_to(jnp.sum(squares, axis=1, keepdims=True), squares.shape)
    distance = iota((count, count), 1) - iota((count, count), 0)
    band = ((distance >= 1) & (distance < per)).astype(f32).astype(bf16)
    begin = pick(squares, head)
    begin = jnp.concatenate([begin[per:], jnp.zeros((per, LANES), f32)], axis=0)
    energy = pick(squares, tail) + picked(band, sums) + begin

    for q in range(pairs):
        pltpu.make_async_copy(w_ref.at[q], wbuf_ref.at[q], sem.at[q]).wait()
        window = slide_ref[q % 8, pl.ds(16 * (q // 8), count), :]
        term = dot(window, wbuf_ref[q])
        if q == 0:
            acc_ref[...] = term
        else:
            acc_ref[...] += term

    groups = LANES // 2
    sub = per // 8
    place = iota((LANES, LANES), 1)
    wanted = (place // (2 * phases)) * phases + place % (2 * phases) - phases
    scatter = ((place % (2 * phases) >= phases) & (iota((LANES, LANES), 0) == wanted)).astype(f32).astype(bf16)
    norm = pick(norm_ref[...], scatter)
    rows_ref[pl.ds(0, count), :] = energy
    lane_group = iota((8, LANES), 1) // (2 * phases)
    x, z = ix_ref[0], ix_ref[1]
    tiles = phases // 2

    def extras(chip):
        at = pl.multiple_of(chip * per, 8)
        e = jnp.zeros((8, LANES), f32)
        for k in range(sub):
            e = jnp.where(lane_group == k, rows_ref[pl.ds(at + 8 * k, 8), :], e)
        valid = iota((8, LANES), 1) % (2 * phases) < phases
        return jnp.where(valid, e, norm)

    def write(ref, slot, chip, lo, hi):
        at = pl.multiple_of(chip * per, 8)
        for tile in range(tiles):
            a, b = max(lo, tile * per), min(hi, (tile + 1) * per)
            if a < b:
                ref[slot, a - lo : b - lo, :] = acc_ref[
                    pl.ds(pl.multiple_of(at + a - tile * per, 8), b - a), tile * LANES : (tile + 1) * LANES
                ]
        if hi > 256:
            ref[slot, 256 - lo : 264 - lo, :] = extras(chip)

    for k in range(zs):
        zk = jnp.bitwise_xor(z, k)
        write(send_a, k, zk * 2 + 1 - x, 0, za)
        write(keep_a, k, zk * 2 + x, 0, za)
        ref = keep_b if k == 0 else send_b[k - 1]
        write(ref, 0, zk * 2 + x, za, za + zb)
        write(ref, 1, zk * 2 + 1 - x, za, za + zb)


def correlate(ix, early, late, w, norm, za, zb):
    zs = len(early)
    phases = w.shape[2] // 64
    t = early[0].shape[1] + late[0].shape[1]
    count = t // phases
    pairs = w.shape[0]
    span = count + 16 * ((pairs - 1) // 8)
    vmem = pl.BlockSpec(memory_space=pltpu.VMEM)
    return pl.pallas_call(
        lambda *refs: correlate_kernel(
            *refs, phases=phases, za=za, zb=zb, n_early=len(early), n_late=len(late)
        ),
        out_shape=tuple(
            [jax.ShapeDtypeStruct((zs, za, LANES), f32)] * 2 + [jax.ShapeDtypeStruct((2, zb, LANES), f32)] * zs
        ),
        in_specs=[pl.BlockSpec(memory_space=pltpu.SMEM)]
        + [vmem] * (len(early) + len(late))
        + [pl.BlockSpec(memory_space=pl.ANY), vmem],
        out_specs=tuple([vmem] * (2 + zs)),
        scratch_shapes=[
            pltpu.VMEM((t, LANES), f32),
            pltpu.VMEM((span + 16, LANES), f32),
            pltpu.VMEM((min(8, pairs), span, 256), bf16),
            pltpu.VMEM((count, w.shape[2]), f32),
            pltpu.VMEM(w.shape, bf16),
            pltpu.SemaphoreType.DMA((pairs,)),
        ],
        compiler_params=pltpu.CompilerParams(vmem_limit_bytes=VMEM_BYTES),
        cost_estimate=pl.CostEstimate(flops=2**33, bytes_accessed=2**24, transcendentals=0),
        name="correlate",
    )(ix, *early, *late, w, norm)


def scale_kernel(*refs, phases, na, nb):
    ix_ref = refs[0]
    a = sum(r[0] for r in refs[1 : 1 + na])
    b = sum(r[0] for r in refs[1 + na : 1 + na + nb])
    mine_ref, other_ref = refs[1 + na + nb :]
    groups = LANES // 2
    per = L // phases
    sub = per // 8
    block = jnp.concatenate([a, b], axis=0)
    extra = block[256:264]
    place = iota((LANES, LANES), 0)
    wanted = (place // (2 * phases)) * phases + place % (2 * phases) - phases
    gather = (
        ((place % (2 * phases) >= phases) & (iota((LANES, LANES), 1) % groups == wanted)).astype(f32).astype(bf16)
    )
    norm = math.sqrt(CT * L) * lax.rsqrt(pick(extra, gather))
    energy = lax.rsqrt(extra + epsilon)
    low = iota((8, LANES), 1) < groups
    first = ix_ref[2] == 0
    half = per // 2
    for tile in range(phases // 2):
        parts = []
        for k in range(sub):
            at = 2 * phases * k + 2 * tile
            scale = jnp.where(low, energy[:, at : at + 1], energy[:, at + 1 : at + 2]) * norm
            parts.append(block[tile * per + 8 * k : tile * per + 8 * k + 8] * scale)
        whole = jnp.concatenate(parts, axis=0) if sub > 1 else parts[0]
        lower, upper = whole[:half], whole[half:]
        mine_ref[tile] = jnp.where(first, lower, upper)
        other_ref[tile] = jnp.where(first, upper, lower)


def scaled(ix, a, b, phases):
    vmem = pl.BlockSpec(memory_space=pltpu.VMEM)
    half = jax.ShapeDtypeStruct((phases // 2, L // phases // 2, LANES), f32)
    return pl.pallas_call(
        lambda *refs: scale_kernel(*refs, phases=phases, na=len(a), nb=len(b)),
        out_shape=(half, half),
        in_specs=[pl.BlockSpec(memory_space=pltpu.SMEM)] + [vmem] * (len(a) + len(b)),
        out_specs=(vmem, vmem),
        cost_estimate=pl.CostEstimate(flops=2**18, bytes_accessed=2**20, transcendentals=0),
        name="scale",
    )(ix, *a, *b)


def weave_kernel(ix_ref, mine_ref, got_ref, out_ref):
    tiles, half, _ = mine_ref.shape
    low = iota((half, LANES), 1) < LANES // 2
    first = ix_ref[2] == 0
    for tile in range(tiles):
        mine, got = mine_ref[tile], got_ref[tile]
        zero, one = jnp.where(first, mine, got), jnp.where(first, got, mine)
        out_ref[pl.ds(2 * tile, half, stride=2 * tiles), :] = jnp.where(low, zero, pltpu.roll(one, LANES // 2, 1))
        out_ref[pl.ds(2 * tile + 1, half, stride=2 * tiles), :] = jnp.where(low, pltpu.roll(zero, LANES // 2, 1), one)


def weave(ix, mine, got):
    vmem = pl.BlockSpec(memory_space=pltpu.VMEM)
    tiles, half, _ = mine.shape
    return pl.pallas_call(
        weave_kernel,
        out_shape=jax.ShapeDtypeStruct((2 * tiles * half, LANES), f32),
        in_specs=[pl.BlockSpec(memory_space=pltpu.SMEM), vmem, vmem],
        out_specs=vmem,
        cost_estimate=pl.CostEstimate(flops=2**16, bytes_accessed=2**18, transcendentals=0),
        name="weave",
    )(ix, mine, got)


def local(records, templates, panel_start):
    devices = lax.axis_size("win")
    me = lax.axis_index("win")
    chips = devices // 2
    zs = chips // 2
    core, chip = me % 2, me // 2
    x, z = chip % 2, chip // 2
    ix = jnp.stack([x, z, core]).astype(jnp.int32)
    held, t = records.shape
    own = CT // devices
    per_chip = 2 * own
    phases = LANES // per_chip
    pairs = (L // phases + 2) // 2

    def swap(value, bit):
        return lax.ppermute(value, "win", [(d, d ^ bit) for d in range(devices)])

    kx = jnp.arange(2)[:, None, None]
    kz = jnp.arange(zs)[None, :, None]
    k = jnp.arange(per_chip)[None, None, :]

    def routed(panel):
        target = jnp.bitwise_xor(z, kz) * 2 + jnp.bitwise_xor(x, kx)
        channel = target * per_chip + (k + own * panel) % per_chip
        row = (panel_start[panel] + channel - me * held).reshape(CT, 1)
        return (row == jnp.arange(held)[None, :]).astype(bf16)

    away = jnp.dot(routed(1 - core), records, preferred_element_type=f32).astype(bf16)
    home = jnp.dot(routed(core), records, preferred_element_type=f32).astype(bf16)
    home = home + swap(away, 1)
    wanted = lax.dynamic_index_in_dim(templates, core, 0, keepdims=False)
    given = lax.dynamic_index_in_dim(templates, 1 - core, 0, keepdims=False)
    w, norm = shifted(wanted, swap(given, 1), phases, pairs)

    ta = t * 5 // 8 // LANES * LANES
    home = home.reshape(2, zs, per_chip, t)
    a, b = home[..., :ta], home[..., ta:]
    a = a[0] + swap(a[1], 2)
    b = b[:, 0] + sum(swap(b[:, i], 4 * i) for i in range(1, zs))
    early = [a[0]] + [swap(a[i], 4 * i) for i in range(1, zs)]
    late = [b[0], swap(b[1], 2)]

    za, zb = 168, 96
    keep_a, send_a, keep_b, *send_b = correlate(ix, early, late, w, norm, za, zb)
    a = keep_a + swap(send_a, 2)
    b = keep_b + sum(swap(v, 4 * (i + 1)) for i, v in enumerate(send_b))
    a = [a[0:1]] + [swap(a[i : i + 1], 4 * i) for i in range(1, zs)]
    b = [b[0:1], swap(b[1:2], 2)]
    mine, other = scaled(ix, a, b, phases)
    return weave(ix, mine, swap(other, 1))


def solution(mesh):
    placed = (P("win", "parts"), P(None, None, "win", None), P("parts"))
    return jax.shard_map(
        local, mesh=mesh, in_specs=placed, out_specs=P(("parts", "win"), None), check_vma=False
    )
```

time: 422 us -> 82.2 us (0.19)
  matrix products: 165 us -> 0.96 us
  blocking collectives: 136 us -> 0 us
  waiting for transfers between devices: 66.8 us -> 17 us
  Pallas kernels: 0 us -> 26.9 us
  starting transfers between devices: 2.57 us -> 25.4 us
  between operations: 17.8 us -> 0.17 us
  other arithmetic: 21.1 us -> 4.05 us
    conv_general_dilated x1 -> x0, matrix products: 165 us -> none  [correlate(): lax.conv_general_dilated(inputs, filters, (1,), 'VALID', dimension_number...]
    psum x1 -> x0, blocking collectives: 89.9 us -> none  [local(): template_norm = lax.psum(own_norm, 'win')]
    all_gather x1 -> x0, waiting for transfers between devices: 66.8 us -> none  [local(): lax.all_gather(templates, 'win', axis=2, tiled=True)]
    all_to_all x1 -> x0, blocking collectives: 46.6 us -> none  [local(): lax.all_to_all(records, 'win', split_axis=1, concat_axis=0, tiled=True)]
    pallas_call x0 -> x4, Pallas kernels: none -> 26.9 us  [the longest x1 14.8 us: correlate(): pl.pallas_call(lambda *refs: correlate_kernel(*refs, phases=phases, za=za...]
    ppermute x2 -> x19, starting transfers between devices: 2.57 us -> 25.4 us  [swap(): return lax.ppermute(value, 'win', [(d, d ^ bit) for d in range(devices)])]
    another operation x1, other arithmetic: 17.8 us -> 0.62 us  [local(): ix = jnp.stack([x, z, core]).astype(jnp.int32)]
    ppermute x2 -> x19, waiting for transfers between devices: 0.01 us -> 17 us  [swap(): return lax.ppermute(value, 'win', [(d, d ^ bit) for d in range(devices)])]
  transfers between devices with their start and end apart: 3 -> 19, of which waited for: 1 -> 8; matrix products, arithmetic and copies ran while one was open for 6% -> 6% of each run, Pallas kernels for 0% -> 11%
where the time goes in v1:
time: 82.2 us; the launch traced here: 81.7 us
  Pallas kernels  26.9 us (33%)
  starting transfers between devices  25.4 us (31%)
  waiting for transfers between devices  17 us (21%)
  local copies, waits for them, and re-layouts  7.34 us (9%)
  other arithmetic  4.05 us (5%)
  matrix products  0.96 us (1%)
    ppermute x19, starting transfers between devices, swap(): return lax.ppermute(value, 'win', [(d, d ^ bit) for d in range(devices)])  25.4 us
    ppermute x19, waiting for transfers between devices, swap(): return lax.ppermute(value, 'win', [(d, d ^ bit) for d in range(devices)])  17 us
    pallas_call x1, Pallas kernels, correlate(): pl.pallas_call(lambda *refs: correlate_kernel(*refs, phases=phases, za=za...  14.8 us
    pallas_call x1, Pallas kernels, shifted(): pl.pallas_call(lambda *refs: shift_kernel(*refs, phases=phases), out_shap...  8.58 us
    unnamed x22, local copies, waits for them, and re-layouts  2.19 us
    pallas_call x1, Pallas kernels, scaled(): pl.pallas_call(lambda *refs: scale_kernel(*refs, phases=phases, na=len(a)...  1.88 us
  transfers between devices with their start and end apart: 19, of which 8 were waited for; matrix products, arithmetic and copies ran while one was open for 6% of the time, Pallas kernels for 11%

profile of v1, /device:TPU:0, one launch (start us, length us, event | category | flops | bytes accessed | tf_op | source)
XLA Modules:
  0.0 81.7 jit_solution(2909186635902574005)
XLA Ops:
  0.0 0.1 add_multiply_fusion
  0.1 1.4 %fusion.9 = (s32[1]{0:T(128)}, s32[1]{0:T(128)}) fusion(s32[2]{0:T(128)} %param.5, s32[]{:T(128)S(6)} %select_n.51, s32[]{:T(128)S(6)} %select_n.53), kind=kLoop, calls=%fused_computation.40 | loop fusion | bytes 24 | tf_op jit(solution)/shard_map/dynamic_slice | solution.py:310
  1.5 1.3 %add_subtract_fusion.1 = (s32[2,4,16]{2,1,0:T(4,128)S(1)}, s32[2,4,16]{2,1,0:T(4,128)S(1)}) fusion(s32[]{:T(128)S(6)} %mul.31, s32[16]{0:T(128)S(1)} %get-tuple-element.47, s32[2,4]{1,0:T(2,128)S(1)} %add_multiply_fusion, s32[]{:T(128)} %bitcast.3, s32[16]{0:T(128)S(1)} %get-tuple-element.46, s32[]{:T(128)} %bitcast.4), kind=kLoop, calls=%fused_computation.25 | loop fusion | flops 768 | bytes 1196 | tf_op jit(solution)/shard_map/sub | solution.py:310
  2.8 0.1 sub.42
  2.9 0.5 convolution_convert_fusion
  3.4 0.5 collective-permute-start
  3.9 0.2 copy-done.1
  4.1 1.0 %dynamic-slice_bitcast_fusion = (bf16[64,8,512]{2,1,0:T(8,128)(2,1)}, bf16[512,512]{1,0:T(8,128)(2,1)}) fusion(bf16[2,64,8,512]{3,2,1,0:T(8,128)(2,1)S(1)} %copy-done.1, s32[]{:T(128)S(6)} %select_n.53, s32[]{:T(128)S(6)} %select_n.51), kind=kLoop, calls=%fused_computation.3 | loop fusion | bytes 2097160 | tf_op jit(solution)/shard_map/jit(dynamic_index_in_dim)/squeeze | solution.py:317
  5.1 0.5 collective-permute-start.9
  5.6 0.1 sub.39
  5.7 0.6 pad_add_fusion.refs_0_.ix_ref
  6.3 0.5 fusion
  6.8 3.9 %collective-permute-start.6 = (bf16[2,16,1536]{2,1,0:T(8,128)(2,1)S(1)}, bf16[2,16,1536]{2,1,0:T(8,128)(2,1)S(1)}, u32[]{:S(2)}, u32[]{:S(2)}) collective-permute-start(bf16[2,16,1536]{2,1,0:T(8,128)(2,1)S(1)} %get-tuple-element.27), channel_id=1, source_target_pairs={{0,8},{1,9},{2,10},{3,11},{4,12},{5,13},{6,14},{7,15},{8,0},{9,1},... | collective-permute-start | bytes 294920 | tf_op jit(solution)/shard_map/ppermute | solution.py:301
  10.7 1.6 %collective-permute-start.5 = (bf16[2,16,1536]{2,1,0:T(8,128)(2,1)S(1)}, bf16[2,16,1536]{2,1,0:T(8,128)(2,1)S(1)}, u32[]{:S(2)}, u32[]{:S(2)}) collective-permute-start(bf16[2,16,1536]{2,1,0:T(8,128)(2,1)S(1)} %get-tuple-element.28), channel_id=1, source_target_pairs={{0,4},{1,5},{2,6},{3,7},{4,0},{5,1},{6,2},{7,3},{8,12},{9,13},{10,... | collective-permute-start | bytes 294920 | tf_op jit(solution)/shard_map/ppermute | solution.py:301
  12.3 1.8 %collective-permute-start.1 = (bf16[4,16,2560]{2,1,0:T(8,128)(2,1)S(1)}, bf16[4,16,2560]{2,1,0:T(8,128)(2,1)S(1)}, u32[]{:S(2)}, u32[]{:S(2)}) collective-permute-start(bf16[4,16,2560]{2,1,0:T(8,128)(2,1)S(1)} %slice_bitcast_fusion), channel_id=1, source_target_pairs={{0,2},{1,3},{2,0},{3,1},{4,6},{5,7},{6,4},{7,5},{8,10},{9,11},{10,... | collective-permute-start | bytes 983048 | tf_op jit(solution)/shard_map/ppermute | solution.py:301
  14.1 2.3 %collective-permute-done.6 = bf16[2,16,1536]{2,1,0:T(8,128)(2,1)S(1)} collective-permute-done((bf16[2,16,1536]{2,1,0:T(8,128)(2,1)S(1)}, bf16[2,16,1536]{2,1,0:T(8,128)(2,1)S(1)}, u32[]{:S(2)}, u32[]{:S(2)}) %collective-permute-start.6) | collective-permute-done | bytes 98336 | tf_op jit(solution)/shard_map/ppermute | solution.py:301
  16.4 3.0 %collective-permute-done.7 = bf16[2,16,1536]{2,1,0:T(8,128)(2,1)S(1)} collective-permute-done((bf16[2,16,1536]{2,1,0:T(8,128)(2,1)S(1)}, bf16[2,16,1536]{2,1,0:T(8,128)(2,1)S(1)}, u32[]{:S(2)}, u32[]{:S(2)}) %collective-permute-start.7) | collective-permute-done | bytes 98336 | tf_op jit(solution)/shard_map/ppermute | solution.py:301
  19.4 0.6 slice_bitcast_fusion.10
  20.0 1.5 %collective-permute-start.8 = (bf16[16,1536]{1,0:T(8,128)(2,1)S(1)}, bf16[16,1536]{1,0:T(8,128)(2,1)S(1)}, u32[]{:S(2)}, u32[]{:S(2)}) collective-permute-start(bf16[16,1536]{1,0:T(8,128)(2,1)S(1)} %get-tuple-element.40), channel_id=1, source_target_pairs={{0,2},{1,3},{2,0},{3,1},{4,6},{5,7},{6,4},{7,5},{8,10},{9,11},{10,... | collective-permute-start | bytes 147464 | tf_op jit(solution)/shard_map/ppermute | solution.py:301
  21.5 0.2 collective-permute-done.1
  21.8 0.6 slice_bitcast_fusion.6
  22.4 4.1 %collective-permute-start.4 = (bf16[16,2560]{1,0:T(8,128)(2,1)S(1)}, bf16[16,2560]{1,0:T(8,128)(2,1)S(1)}, u32[]{:S(2)}, u32[]{:S(2)}) collective-permute-start(bf16[16,2560]{1,0:T(8,128)(2,1)S(1)} %get-tuple-element.34), channel_id=1, source_target_pairs={{0,12},{1,13},{2,14},{3,15},{4,8},{5,9},{6,10},{7,11},{8,4},{9,5},... | collective-permute-start | bytes 245768 | tf_op jit(solution)/shard_map/ppermute | solution.py:301
  26.5 0.6 collective-permute-start.2
  27.0 8.6 %shift_templates.1 = (bf16[33,256,512]{2,1,0:T(8,128)(2,1)}, f32[8,128]{1,0:T(8,128)}) custom-call(bf16[512,512]{1,0:T(8,128)(2,1)} %get-tuple-element.26.refs_0_, bf16[512,512]{1,0:T(8,128)(2,1)} %bitcast.20.refs_1_), custom_call_target="tpu_custom_call" | custom-call | flops 1073741824 | bytes 16777216 | tf_op jit(solution)/shard_map/shift_templates/pallas_call | solution.py:75
  35.7 0.6 copy-done.10
  36.3 0.0 copy-done.9
  36.4 14.8 %correlate.1 = (f32[4,168,128]{2,1,0:T(8,128)}, f32[4,168,128]{2,1,0:T(8,128)}, f32[2,96,128]{2,1,0:T(8,128)}, f32[2,96,128]{2,1,0:T(8,128)}, f32[2,96,128]{2,1,0:T(8,128)}, /*index=5*/f32[2,96,128]{2,1,0:T(8,128)}) custom-call(s32[3]{0:T(128)} %pad_add_fusion.refs_0_.ix_ref, bf16[16,2560]{1,0:T(8,128)(2,1)} %get-tuple-element.37.refs_1_, ...), custom_call_target="tpu_custom_call" | custom-call | flops 8589934592 | bytes 16777216 | tf_op jit(solution)/shard_map/correlate/pallas_call | solution.py:192
  51.1 1.6 %collective-permute-start.10 = (f32[4,168,128]{2,1,0:T(8,128)}, f32[4,168,128]{2,1,0:T(8,128)S(1)}, u32[]{:S(2)}, u32[]{:S(2)}) collective-permute-start(f32[4,168,128]{2,1,0:T(8,128)} %get-tuple-element.18), channel_id=1, source_target_pairs={{0,2},{1,3},{2,0},{3,1},{4,6},{5,7},{6,4},{7,5},{8,10},{9,11},{10,... | collective-permute-start | bytes 1032200 | tf_op jit(solution)/shard_map/ppermute | solution.py:301
  52.7 1.5 %collective-permute-start.14 = (f32[2,96,128]{2,1,0:T(8,128)}, f32[2,96,128]{2,1,0:T(8,128)S(1)}, u32[]{:S(2)}, u32[]{:S(2)}) collective-permute-start(f32[2,96,128]{2,1,0:T(8,128)} %get-tuple-element.20), channel_id=1, source_target_pairs={{0,4},{1,5},{2,6},{3,7},{4,0},{5,1},{6,2},{7,3},{8,12},{9,13},{10,... | collective-permute-start | bytes 294920 | tf_op jit(solution)/shard_map/ppermute | solution.py:301
  54.2 2.9 %collective-permute-start.15 = (f32[2,96,128]{2,1,0:T(8,128)}, f32[2,96,128]{2,1,0:T(8,128)S(1)}, u32[]{:S(2)}, u32[]{:S(2)}) collective-permute-start(f32[2,96,128]{2,1,0:T(8,128)} %get-tuple-element.21), channel_id=1, source_target_pairs={{0,8},{1,9},{2,10},{3,11},{4,12},{5,13},{6,14},{7,15},{8,0},{9,1},... | collective-permute-start | bytes 294920 | tf_op jit(solution)/shard_map/ppermute | solution.py:301
  57.1 0.4 collective-permute-done.14
  57.5 3.9 %collective-permute-done.15 = f32[2,96,128]{2,1,0:T(8,128)S(1)} collective-permute-done((f32[2,96,128]{2,1,0:T(8,128)}, f32[2,96,128]{2,1,0:T(8,128)S(1)}, u32[]{:S(2)}, u32[]{:S(2)}) %collective-permute-start.15) | collective-permute-done | bytes 98336 | tf_op jit(solution)/shard_map/ppermute | solution.py:301
  61.4 2.3 %collective-permute-done.16 = f32[2,96,128]{2,1,0:T(8,128)S(1)} collective-permute-done((f32[2,96,128]{2,1,0:T(8,128)}, f32[2,96,128]{2,1,0:T(8,128)S(1)}, u32[]{:S(2)}, u32[]{:S(2)}) %collective-permute-start.16) | collective-permute-done | bytes 98336 | tf_op jit(solution)/shard_map/ppermute | solution.py:301
  63.7 0.9 %add_add_fusion = f32[2,96,128]{2,1,0:T(8,128)S(1)} fusion(f32[2,96,128]{2,1,0:T(8,128)} %get-tuple-element.19, f32[2,96,128]{2,1,0:T(8,128)S(1)} %collective-permute-done.16, f32[2,96,128]{2,1,0:T(8,128)S(1)} %collective-permute-done.14, f32[2,96,128]{2,1,0:T(8,128)S(1)} %collective-permute-done.15), kind=kLoop, calls=%fused_computation.13 | loop fusion | flops 73728 | bytes 491520 | tf_op jit(solution)/shard_map/add | solution.py:331
  64.6 1.0 %add.196 = f32[4,168,128]{2,1,0:T(8,128)S(1)} add(f32[4,168,128]{2,1,0:T(8,128)} %get-tuple-element.17, f32[4,168,128]{2,1,0:T(8,128)S(1)} %collective-permute-done.10) | non-fusion elementwise | flops 86016 | bytes 1032192 | tf_op jit(solution)/shard_map/add | solution.py:330
  65.7 0.7 fusion.7
  66.3 1.2 %collective-permute-start.13 = (f32[1,168,128]{2,1,0:T(8,128)S(1)}, f32[1,168,128]{2,1,0:T(8,128)S(1)}, u32[]{:S(2)}, u32[]{:S(2)}) collective-permute-start(f32[1,168,128]{2,1,0:T(8,128)S(1)} %get-tuple-element.30), channel_id=1, source_target_pairs={{0,12},{1,13},{2,14},{3,15},{4,8},{5,9},{6,10},{7,11},{8,4},{9,5},... | collective-permute-start | bytes 258056 | tf_op jit(solution)/shard_map/ppermute | solution.py:301
  67.5 0.1 collective-permute-start.12
  67.6 3.1 %collective-permute-start.11 = (f32[1,168,128]{2,1,0:T(8,128)S(1)}, f32[1,168,128]{2,1,0:T(8,128)S(1)}, u32[]{:S(2)}, u32[]{:S(2)}) collective-permute-start(f32[1,168,128]{2,1,0:T(8,128)S(1)} %get-tuple-element.32), channel_id=1, source_target_pairs={{0,4},{1,5},{2,6},{3,7},{4,0},{5,1},{6,2},{7,3},{8,12},{9,13},{10,... | collective-permute-start | bytes 258056 | tf_op jit(solution)/shard_map/ppermute | solution.py:301
  70.7 0.6 fusion.8
  71.3 0.6 collective-permute-start.17
  72.0 3.4 %collective-permute-done.17.refs_6_ = f32[1,96,128]{2,1,0:T(8,128)S(1)} collective-permute-done((f32[1,96,128]{2,1,0:T(8,128)S(1)}, f32[1,96,128]{2,1,0:T(8,128)S(1)}, u32[]{:S(2)}, u32[]{:S(2)}) %collective-permute-start.17) | collective-permute-done | bytes 49184 | tf_op jit(solution)/shard_map/ppermute | solution.py:301
  75.5 0.6 copy-done.6
  76.0 0.1 copy-done.2
  76.1 1.9 %scale.1 = (f32[4,32,128]{2,1,0:T(8,128)}, f32[4,32,128]{2,1,0:T(8,128)}) custom-call(s32[3]{0:T(128)} %pad_add_fusion.refs_0_.ix_ref, f32[1,168,128]{2,1,0:T(8,128)} %get-tuple-element.33.refs_1_, f32[1,168,128]{2,1,0:T(8,128)} %copy-done.4, f32[1,168,128]{2,1,0:T(8,128)} %copy-done.3, f32[1,168,128]{2,1,0:T(8,128)} %copy-done.2, ...), custom_call_target="tpu_custom_call" | custom-call | flops 262144 | bytes 1048576 | tf_op jit(solution)/shard_map/scale/pallas_call | solution.py:252
  78.0 1.5 %collective-permute-done.18.got_ref = f32[4,32,128]{2,1,0:T(8,128)S(1)} collective-permute-done((f32[4,32,128]{2,1,0:T(8,128)}, f32[4,32,128]{2,1,0:T(8,128)S(1)}, u32[]{:S(2)}, u32[]{:S(2)}) %collective-permute-start.18) | collective-permute-done | bytes 65568 | tf_op jit(solution)/shard_map/ppermute | solution.py:301
  79.5 0.6 copy-done.5
  80.1 1.6 %weave.1 = f32[256,128]{1,0:T(8,128)} custom-call(s32[3]{0:T(128)} %pad_add_fusion.refs_0_.ix_ref, f32[4,32,128]{2,1,0:T(8,128)} %get-tuple-element.23.mine_ref, f32[4,32,128]{2,1,0:T(8,128)} %copy-done.5), custom_call_target="tpu_custom_call" | custom-call | flops 65536 | bytes 262144 | tf_op jit(solution)/shard_map/weave/pallas_call | solution.py:276
  (38 shorter events, 0.3 us)
Async XLA Ops:
  0.0 2.9 %copy-start = (bf16[128,4096]{1,0:T(8,128)(2,1)S(1)}, bf16[128,4096]{1,0:T(8,128)(2,1)}, u32[]{:S(2)}) copy-start(bf16[128,4096]{1,0:T(8,128)(2,1)} %param.3) | copy-start | bytes 3145732
  2.9 1.2 %copy-start.1 = (bf16[2,64,8,512]{3,2,1,0:T(8,128)(2,1)S(1)}, bf16[2,64,8,512]{3,2,1,0:T(8,128)(2,1)}, u32[]{:S(2)}) copy-start(bf16[2,64,8,512]{3,2,1,0:T(8,128)(2,1)} %param.4) | copy-start | bytes 3145732
  3.4 2.9 %collective-permute-start = (bf16[128,4096]{1,0:T(8,128)(2,1)S(1)}, bf16[128,4096]{1,0:T(8,128)(2,1)S(1)}, u32[]{:S(2)}, u32[]{:S(2)}) collective-permute-start(bf16[128,4096]{1,0:T(8,128)(2,1)S(1)} %convolution_convert_fusion), channel_id=1, source_target_pairs={{0,1},{1,0},{2,3},{3,2},{4,5},{5,4},{6,7},{7,6},{8,9},{9,8},{10,11... | collective-permute-start | bytes 3145736 | tf_op jit(solution)/shard_map/ppermute | solution.py:301
  5.1 21.9 %collective-permute-start.9 = (bf16[64,8,512]{2,1,0:T(8,128)(2,1)}, bf16[64,8,512]{2,1,0:T(8,128)(2,1)}, u32[]{:S(2)}, u32[]{:S(2)}) collective-permute-start(bf16[64,8,512]{2,1,0:T(8,128)(2,1)} %get-tuple-element.25), channel_id=1, source_target_pairs={{0,1},{1,0},{2,3},{3,2},{4,5},{5,4},{6,7},{7,6},{8,9},{9,8},{10,11... | collective-permute-start | bytes 1572872 | tf_op jit(solution)/shard_map/ppermute | solution.py:301
  6.8 9.6 %collective-permute-start.6 = (bf16[2,16,1536]{2,1,0:T(8,128)(2,1)S(1)}, bf16[2,16,1536]{2,1,0:T(8,128)(2,1)S(1)}, u32[]{:S(2)}, u32[]{:S(2)}) collective-permute-start(bf16[2,16,1536]{2,1,0:T(8,128)(2,1)S(1)} %get-tuple-element.27), channel_id=1, source_target_pairs={{0,8},{1,9},{2,10},{3,11},{4,12},{5,13},{6,14},{7,15},{8,0},{9,1},... | collective-permute-start | bytes 294920 | tf_op jit(solution)/shard_map/ppermute | solution.py:301
  10.7 5.7 %collective-permute-start.5 = (bf16[2,16,1536]{2,1,0:T(8,128)(2,1)S(1)}, bf16[2,16,1536]{2,1,0:T(8,128)(2,1)S(1)}, u32[]{:S(2)}, u32[]{:S(2)}) collective-permute-start(bf16[2,16,1536]{2,1,0:T(8,128)(2,1)S(1)} %get-tuple-element.28), channel_id=1, source_target_pairs={{0,4},{1,5},{2,6},{3,7},{4,0},{5,1},{6,2},{7,3},{8,12},{9,13},{10,... | collective-permute-start | bytes 294920 | tf_op jit(solution)/shard_map/ppermute | solution.py:301
  12.3 7.1 %collective-permute-start.7 = (bf16[2,16,1536]{2,1,0:T(8,128)(2,1)S(1)}, bf16[2,16,1536]{2,1,0:T(8,128)(2,1)S(1)}, u32[]{:S(2)}, u32[]{:S(2)}) collective-permute-start(bf16[2,16,1536]{2,1,0:T(8,128)(2,1)S(1)} %get-tuple-element.29), channel_id=1, source_target_pairs={{0,12},{1,13},{2,14},{3,15},{4,8},{5,9},{6,10},{7,11},{8,4},{9,5},... | collective-permute-start | bytes 294920 | tf_op jit(solution)/shard_map/ppermute | solution.py:301
  12.3 9.4 %collective-permute-start.1 = (bf16[4,16,2560]{2,1,0:T(8,128)(2,1)S(1)}, bf16[4,16,2560]{2,1,0:T(8,128)(2,1)S(1)}, u32[]{:S(2)}, u32[]{:S(2)}) collective-permute-start(bf16[4,16,2560]{2,1,0:T(8,128)(2,1)S(1)} %slice_bitcast_fusion), channel_id=1, source_target_pairs={{0,2},{1,3},{2,0},{3,1},{4,6},{5,7},{6,4},{7,5},{8,10},{9,11},{10,... | collective-permute-start | bytes 983048 | tf_op jit(solution)/shard_map/ppermute | solution.py:301
  20.0 15.6 %collective-permute-start.8 = (bf16[16,1536]{1,0:T(8,128)(2,1)S(1)}, bf16[16,1536]{1,0:T(8,128)(2,1)S(1)}, u32[]{:S(2)}, u32[]{:S(2)}) collective-permute-start(bf16[16,1536]{1,0:T(8,128)(2,1)S(1)} %get-tuple-element.40), channel_id=1, source_target_pairs={{0,2},{1,3},{2,0},{3,1},{4,6},{5,7},{6,4},{7,5},{8,10},{9,11},{10,... | collective-permute-start | bytes 147464 | tf_op jit(solution)/shard_map/ppermute | solution.py:301
  22.4 13.2 %collective-permute-start.4 = (bf16[16,2560]{1,0:T(8,128)(2,1)S(1)}, bf16[16,2560]{1,0:T(8,128)(2,1)S(1)}, u32[]{:S(2)}, u32[]{:S(2)}) collective-permute-start(bf16[16,2560]{1,0:T(8,128)(2,1)S(1)} %get-tuple-element.34), channel_id=1, source_target_pairs={{0,12},{1,13},{2,14},{3,15},{4,8},{5,9},{6,10},{7,11},{8,4},{9,5},... | collective-permute-start | bytes 245768 | tf_op jit(solution)/shard_map/ppermute | solution.py:301
  26.5 9.2 %collective-permute-start.3 = (bf16[16,2560]{1,0:T(8,128)(2,1)S(1)}, bf16[16,2560]{1,0:T(8,128)(2,1)S(1)}, u32[]{:S(2)}, u32[]{:S(2)}) collective-permute-start(bf16[16,2560]{1,0:T(8,128)(2,1)S(1)} %get-tuple-element.35), channel_id=1, source_target_pairs={{0,8},{1,9},{2,10},{3,11},{4,12},{5,13},{6,14},{7,15},{8,0},{9,1},... | collective-permute-start | bytes 245768 | tf_op jit(solution)/shard_map/ppermute | solution.py:301
  26.5 9.2 %collective-permute-start.2 = (bf16[16,2560]{1,0:T(8,128)(2,1)S(1)}, bf16[16,2560]{1,0:T(8,128)(2,1)S(1)}, u32[]{:S(2)}, u32[]{:S(2)}) collective-permute-start(bf16[16,2560]{1,0:T(8,128)(2,1)S(1)} %get-tuple-element.36), channel_id=1, source_target_pairs={{0,4},{1,5},{2,6},{3,7},{4,0},{5,1},{6,2},{7,3},{8,12},{9,13},{10,... | collective-permute-start | bytes 245768 | tf_op jit(solution)/shard_map/ppermute | solution.py:301
  35.6 0.6 copy-start.10
  35.6 0.6 copy-start.7
  35.7 0.7 copy-start.8
  35.7 0.7 copy-start.9
  51.1 13.5 %collective-permute-start.10 = (f32[4,168,128]{2,1,0:T(8,128)}, f32[4,168,128]{2,1,0:T(8,128)S(1)}, u32[]{:S(2)}, u32[]{:S(2)}) collective-permute-start(f32[4,168,128]{2,1,0:T(8,128)} %get-tuple-element.18), channel_id=1, source_target_pairs={{0,2},{1,3},{2,0},{3,1},{4,6},{5,7},{6,4},{7,5},{8,10},{9,11},{10,... | collective-permute-start | bytes 1032200 | tf_op jit(solution)/shard_map/ppermute | solution.py:301
  52.7 4.8 %collective-permute-start.14 = (f32[2,96,128]{2,1,0:T(8,128)}, f32[2,96,128]{2,1,0:T(8,128)S(1)}, u32[]{:S(2)}, u32[]{:S(2)}) collective-permute-start(f32[2,96,128]{2,1,0:T(8,128)} %get-tuple-element.20), channel_id=1, source_target_pairs={{0,4},{1,5},{2,6},{3,7},{4,0},{5,1},{6,2},{7,3},{8,12},{9,13},{10,... | collective-permute-start | bytes 294920 | tf_op jit(solution)/shard_map/ppermute | solution.py:301
  54.2 7.3 %collective-permute-start.15 = (f32[2,96,128]{2,1,0:T(8,128)}, f32[2,96,128]{2,1,0:T(8,128)S(1)}, u32[]{:S(2)}, u32[]{:S(2)}) collective-permute-start(f32[2,96,128]{2,1,0:T(8,128)} %get-tuple-element.21), channel_id=1, source_target_pairs={{0,8},{1,9},{2,10},{3,11},{4,12},{5,13},{6,14},{7,15},{8,0},{9,1},... | collective-permute-start | bytes 294920 | tf_op jit(solution)/shard_map/ppermute | solution.py:301
  57.1 6.6 %collective-permute-start.16 = (f32[2,96,128]{2,1,0:T(8,128)}, f32[2,96,128]{2,1,0:T(8,128)S(1)}, u32[]{:S(2)}, u32[]{:S(2)}) collective-permute-start(f32[2,96,128]{2,1,0:T(8,128)} %get-tuple-element.22), channel_id=1, source_target_pairs={{0,12},{1,13},{2,14},{3,15},{4,8},{5,9},{6,10},{7,11},{8,4},{9,5},... | collective-permute-start | bytes 294920 | tf_op jit(solution)/shard_map/ppermute | solution.py:301
  66.3 9.1 %collective-permute-start.13 = (f32[1,168,128]{2,1,0:T(8,128)S(1)}, f32[1,168,128]{2,1,0:T(8,128)S(1)}, u32[]{:S(2)}, u32[]{:S(2)}) collective-permute-start(f32[1,168,128]{2,1,0:T(8,128)S(1)} %get-tuple-element.30), channel_id=1, source_target_pairs={{0,12},{1,13},{2,14},{3,15},{4,8},{5,9},{6,10},{7,11},{8,4},{9,5},... | collective-permute-start | bytes 258056 | tf_op jit(solution)/shard_map/ppermute | solution.py:301
  67.5 7.9 %collective-permute-start.12 = (f32[1,168,128]{2,1,0:T(8,128)S(1)}, f32[1,168,128]{2,1,0:T(8,128)S(1)}, u32[]{:S(2)}, u32[]{:S(2)}) collective-permute-start(f32[1,168,128]{2,1,0:T(8,128)S(1)} %get-tuple-element.31), channel_id=1, source_target_pairs={{0,8},{1,9},{2,10},{3,11},{4,12},{5,13},{6,14},{7,15},{8,0},{9,1},... | collective-permute-start | bytes 258056 | tf_op jit(solution)/shard_map/ppermute | solution.py:301
  67.6 7.8 %collective-permute-start.11 = (f32[1,168,128]{2,1,0:T(8,128)S(1)}, f32[1,168,128]{2,1,0:T(8,128)S(1)}, u32[]{:S(2)}, u32[]{:S(2)}) collective-permute-start(f32[1,168,128]{2,1,0:T(8,128)S(1)} %get-tuple-element.32), channel_id=1, source_target_pairs={{0,4},{1,5},{2,6},{3,7},{4,0},{5,1},{6,2},{7,3},{8,12},{9,13},{10,... | collective-permute-start | bytes 258056 | tf_op jit(solution)/shard_map/ppermute | solution.py:301
  71.3 4.1 %collective-permute-start.17 = (f32[1,96,128]{2,1,0:T(8,128)S(1)}, f32[1,96,128]{2,1,0:T(8,128)S(1)}, u32[]{:S(2)}, u32[]{:S(2)}) collective-permute-start(f32[1,96,128]{2,1,0:T(8,128)S(1)} %get-tuple-element.38), channel_id=1, source_target_pairs={{0,2},{1,3},{2,0},{3,1},{4,6},{5,7},{6,4},{7,5},{8,10},{9,11},{10,... | collective-permute-start | bytes 147464 | tf_op jit(solution)/shard_map/ppermute | solution.py:301
  75.4 0.6 copy-start.6
  75.4 0.7 copy-start.2
  75.4 0.7 copy-start.3
  75.4 0.7 copy-start.4
  78.0 1.5 %collective-permute-start.18 = (f32[4,32,128]{2,1,0:T(8,128)}, f32[4,32,128]{2,1,0:T(8,128)S(1)}, u32[]{:S(2)}, u32[]{:S(2)}) collective-permute-start(f32[4,32,128]{2,1,0:T(8,128)} %get-tuple-element.24), channel_id=1, source_target_pairs={{0,1},{1,0},{2,3},{3,2},{4,5},{5,4},{6,7},{7,6},{8,9},{9,8},{10,11... | collective-permute-start | bytes 196616 | tf_op jit(solution)/shard_map/ppermute | solution.py:301
  79.5 0.6 copy-start.5

commit v2 on v0

v2 whole, which is shorter than its diff:
```python
import math

import jax
import jax.numpy as jnp
from jax import lax
from jax.experimental import pallas as pl
from jax.experimental.pallas import tpu as pltpu
from jax.sharding import PartitionSpec as P

CT = 128
L = 512
LANES = 128
epsilon = 1e-06
f32 = jnp.float32
bf16 = jnp.bfloat16
SPARE = 12 * 2**20
IN_VMEM = pl.BlockSpec(memory_space=pltpu.VMEM)
SMALL = pltpu.CompilerParams(vmem_limit_bytes=8 * 2**20)


def iota(shape, dim):
    return lax.broadcasted_iota(jnp.int32, shape, dim)


def dot(a, b, dims=(((1,), (0,)), ((), ()))):
    return lax.dot_general(a, b, dims, preferred_element_type=f32)


def split3(v):
    high = v.astype(bf16)
    rest = v - high.astype(f32)
    middle = rest.astype(bf16)
    return high, middle, (rest - middle.astype(f32)).astype(bf16)


def pick(v, m):
    return sum(dot(part, m) for part in split3(v))


def picked(m, v):
    return sum(dot(m, part) for part in split3(v))


def shift_kernel(own_ref, other_ref, w_ref, norm_ref, rows_ref, *, phases):
    gc = own_ref.shape[0]
    groups = LANES // 2
    each = gc // groups
    channels = 2 * each
    versions, total, _ = w_ref.shape
    pad = channels * phases
    front = rows_ref.shape[0] - total
    rows_ref[pl.ds(0, front + pad), :] = jnp.zeros((front + pad, LANES), f32)
    rows_ref[pl.ds(front + pad + L * channels, total - pad - L * channels), :] = jnp.zeros(
        (total - pad - L * channels, LANES), f32
    )
    norm = jnp.zeros((1, LANES), f32)
    width = min(2, each) * LANES
    row, lane = iota((gc, width), 0), iota((gc, width), 1)
    for side, ref in enumerate((own_ref, other_ref)):
        for c in range(0, each, width // LANES):
            choose = (row == (lane % groups) * each + c + lane // LANES).astype(f32).astype(bf16)
            piece = dot(ref[...], choose, (((0,), (0,)), ((), ())))
            for i in range(width // LANES):
                one = piece[:, i * LANES : (i + 1) * LANES]
                norm = norm + jnp.sum(one * one, axis=0, keepdims=True)
                rows_ref[pl.ds(front + pad + side * each + c + i, L, stride=channels), :] = one
    norm_ref[...] = jnp.broadcast_to(norm, norm_ref.shape)
    low = iota((256, LANES), 1) < groups
    for v in range(versions):
        for at in range(0, total, 256):
            size = min(256, total - at)
            start = front + at - 2 * channels * v
            even = rows_ref[pl.ds(start, size), :]
            odd = rows_ref[pl.ds(start - channels, size), :]
            w_ref[v, at : at + size, :] = jnp.where(low[:size], even, odd).astype(bf16)


def shifted(own, other, phases, pairs):
    channels = 2 * own.shape[1]
    versions = max(1, 8 // channels)
    total = 256 * pairs + channels * phases
    front = (2 * versions - 1) * channels + 8
    front = (front + 7) // 8 * 8
    gc = own.shape[0] * own.shape[1]
    return pl.pallas_call(
        lambda *refs: shift_kernel(*refs, phases=phases),
        out_shape=(
            jax.ShapeDtypeStruct((versions, total, LANES), bf16),
            jax.ShapeDtypeStruct((8, LANES), f32),
        ),
        scratch_shapes=[pltpu.VMEM((front + total, LANES), f32)],
        compiler_params=pltpu.CompilerParams(vmem_limit_bytes=512 * (front + total) + SPARE),
        cost_estimate=pl.CostEstimate(flops=2**30, bytes_accessed=2**24, transcendentals=0),
        name="shift_templates",
    )(own.reshape(gc, L), other.reshape(gc, L))


def bits_of(devices):
    x, z, *rest = [1 << i for i in range(1, devices.bit_length() - 1)]
    return [x, z] + rest, [z, x] + rest


def panel_of(device, devices):
    return sum(device >> i & 1 for i in range(devices.bit_length() - 1)) % 2


def target_of(slot, panel, devices):
    mine, theirs = bits_of(devices)
    chip = jnp.zeros_like(slot)
    for i, (p, q) in enumerate(zip(mine, theirs)):
        chip += (slot >> (len(mine) - 1 - i) & 1) * jnp.where(panel == 0, p, q)
    return chip // 2


def spread(pieces, spread_ref, phases):
    value = sum(r[...] for r in pieces[1:]) + pieces[0][...]
    channels, t = value.shape
    repeat = (iota((channels, LANES), 0) == iota((channels, LANES), 1) % channels).astype(f32).astype(bf16)
    spread_ref[...] = dot(value, repeat, (((0,), (0,)), ((), ())))
    count = t // phases
    phase = iota((count, LANES), 1) // channels
    rows = jnp.zeros((count, LANES), f32)
    for k in range(phases):
        rows = jnp.where(phase == k, spread_ref[pl.ds(k, count, stride=phases), :], rows)
    return rows


def fill_slide(rows_ref, slide_ref):
    span = slide_ref.shape[1]
    for k in range(slide_ref.shape[0]):
        slide_ref[k, :, 0:LANES] = rows_ref[pl.ds(2 * k, span), :].astype(bf16)
        slide_ref[k, :, LANES:] = rows_ref[pl.ds(2 * k + 1, span), :].astype(bf16)


def energies(squares, m, phases):
    n = squares.shape[0]
    channels = LANES // phases
    per = L // phases
    left, right = iota((LANES, LANES), 0) // channels, iota((LANES, LANES), 1) % (2 * phases)
    inside = right < phases
    tail = (inside & (left >= right)).astype(f32).astype(bf16)
    head = (inside & (left < right)).astype(f32).astype(bf16)
    sums = jnp.broadcast_to(jnp.sum(squares, axis=1, keepdims=True), squares.shape)
    distance = iota((m, n), 1) - iota((m, n), 0)
    band = ((distance >= 1) & (distance < per)).astype(f32).astype(bf16)
    begin = pick(squares[per : min(n, per + m)], head)
    if per + m > n:
        begin = jnp.concatenate([begin, jnp.zeros((per + m - n, LANES), f32)], axis=0)
    return pick(squares[:m], tail) + picked(band, sums) + begin


def correlate_tiles(slide_ref, w_ref, acc_ref, m, tiles, phases):
    versions = w_ref.shape[0]
    channels = LANES // phases
    pairs = (w_ref.shape[1] - LANES) // 256

    def shifts(q, tile):
        v = tile % versions
        return w_ref[v, pl.ds(LANES + 256 * q - 2 * channels * (tile - v), 256), :]

    for q in range(pairs):
        window = slide_ref[q % 8, pl.ds(16 * (q // 8), m), :]
        term = dot(window, jnp.concatenate([shifts(q, tile) for tile in tiles], axis=1))
        if q == 0:
            acc_ref[pl.ds(0, m), :] = term
        else:
            acc_ref[pl.ds(0, m), :] += term


def late_kernel(*refs, phases):
    *pieces, w_ref, out_rows, out_energy, out_acc, spread_ref, rows_ref, slide_ref = refs
    rows = spread(pieces, spread_ref, phases)
    count = rows.shape[0]
    out_rows[...] = rows
    rows_ref[pl.ds(0, count), :] = rows
    rows_ref[pl.ds(count, rows_ref.shape[0] - count), :] = jnp.zeros((rows_ref.shape[0] - count, LANES), f32)
    fill_slide(rows_ref, slide_ref)
    out_energy[...] = energies(rows * rows, count, phases)
    correlate_tiles(slide_ref, w_ref, out_acc, count, range(phases // 2), phases)


def write_blocks(send_ref, keep_ref, acc_ref, lead, per, devices):
    me = lax.axis_index("win")
    kept = keep_ref.shape[0]
    for slot in range(2 * kept):
        chip = jnp.bitwise_xor(me // 2, target_of(jnp.int32(slot), panel_of(me, devices), devices))
        at = pl.multiple_of(chip * per, 8)
        ref = keep_ref if slot < kept else send_ref
        for tile in range(acc_ref.shape[1] // LANES):
            ref[slot % kept, tile * per : (tile + 1) * per, :] = acc_ref[
                pl.ds(at, per), tile * LANES : (tile + 1) * LANES
            ]
        if lead is not None:
            ref[slot % kept, LANES:, :] = lead(at)


def early_kernel(*refs, phases, devices):
    *pieces, w_ref, rest_rows, rest_acc, send_ref, keep_ref, rows_ref, slide_ref, spread_ref, acc_ref = refs
    rows = spread(pieces, spread_ref, phases)
    m = rows.shape[0]
    n = m + rest_rows.shape[0]
    rows_ref[pl.ds(0, m), :] = rows
    rows_ref[pl.ds(m, n - m), :] = rest_rows[...]
    fill_slide(rows_ref, slide_ref)
    acc_ref[pl.ds(m, n - m), :] = rest_acc[:, : acc_ref.shape[1]]
    correlate_tiles(slide_ref, w_ref, acc_ref, m, range(phases // 4), phases)
    write_blocks(send_ref, keep_ref, acc_ref, None, L // phases, devices)


def middle_kernel(rows_ref, slide_ref, w_ref, norm_ref, rest_energy, rest_acc, send_ref, keep_ref, energy_ref, acc_ref, *, phases, devices):
    n = rows_ref.shape[0]
    m = n - rest_energy.shape[0]
    squares = rows_ref[...]
    energy_ref[pl.ds(0, m), :] = energies(squares * squares, m, phases)
    energy_ref[pl.ds(m, n - m), :] = rest_energy[...]
    acc_ref[pl.ds(m, n - m), :] = rest_acc[:, acc_ref.shape[1] :]
    correlate_tiles(slide_ref, w_ref, acc_ref, m, range(phases // 4, phases // 2), phases)

    per = L // phases
    place = iota((LANES, LANES), 1)
    wanted = (place // (2 * phases)) * phases + place % (2 * phases) - phases
    scatter = ((place % (2 * phases) >= phases) & (iota((LANES, LANES), 0) == wanted)).astype(f32).astype(bf16)
    norm = pick(norm_ref[...], scatter)
    lane = iota((8, LANES), 1)

    def extras(at):
        e = norm
        for k in range(per // 8):
            e = jnp.where(
                (lane // (2 * phases) == k) & (lane % (2 * phases) < phases), energy_ref[pl.ds(at + 8 * k, 8), :], e
            )
        return e

    write_blocks(send_ref, keep_ref, acc_ref, extras, per, devices)


def grant(shapes):
    return pltpu.CompilerParams(vmem_limit_bytes=sum(math.prod(s.shape) * 4 for s in shapes) + SPARE)


def slide_shape(m, phases):
    pairs = (L // phases + 2) // 2
    return (min(8, pairs), m + 16 * ((pairs - 1) // 8), 256)


def correlate_late(pieces, w, phases):
    t = pieces[0].shape[1]
    count = t // phases
    slide = slide_shape(count, phases)
    shapes = [
        pltpu.VMEM((t, LANES), f32),
        pltpu.VMEM((slide[1] + 16, LANES), f32),
        pltpu.VMEM(slide, bf16),
    ]
    return pl.pallas_call(
        lambda *refs: late_kernel(*refs, phases=phases),
        out_shape=(
            jax.ShapeDtypeStruct((count, LANES), f32),
            jax.ShapeDtypeStruct((count, LANES), f32),
            jax.ShapeDtypeStruct((count, phases * 64), f32),
        ),
        in_specs=[IN_VMEM] * (len(pieces) + 1),
        out_specs=(IN_VMEM, IN_VMEM, IN_VMEM),
        scratch_shapes=shapes,
        compiler_params=grant(shapes),
        cost_estimate=pl.CostEstimate(flops=2**31, bytes_accessed=2**22, transcendentals=0),
        name="correlate_late",
    )(*pieces, w)


def correlate_early(pieces, w, rest_rows, rest_acc, phases, devices):
    t = pieces[0].shape[1]
    m = t // phases
    n = m + rest_rows.shape[0]
    kept = devices // 4
    shapes = [pltpu.VMEM((t, LANES), f32), pltpu.VMEM((n, phases * 32), f32)]
    block = jax.ShapeDtypeStruct((kept, LANES, LANES), f32)
    return pl.pallas_call(
        lambda *refs: early_kernel(*refs, phases=phases, devices=devices),
        out_shape=(
            block,
            block,
            jax.ShapeDtypeStruct((n, LANES), f32),
            jax.ShapeDtypeStruct(slide_shape(m, phases), bf16),
        ),
        in_specs=[IN_VMEM] * (len(pieces) + 3),
        out_specs=(IN_VMEM,) * 4,
        scratch_shapes=shapes,
        compiler_params=grant(shapes),
        cost_estimate=pl.CostEstimate(flops=2**32, bytes_accessed=2**24, transcendentals=0),
        name="correlate_early",
    )(*pieces, w, rest_rows, rest_acc)


def correlate_middle(rows, slide, w, norm, rest_energy, rest_acc, phases, devices):
    n = rows.shape[0]
    kept = devices // 4
    shapes = [pltpu.VMEM((n, LANES), f32), pltpu.VMEM((n, phases * 32), f32)]
    block = jax.ShapeDtypeStruct((kept, LANES + 8, LANES), f32)
    return pl.pallas_call(
        lambda *refs: middle_kernel(*refs, phases=phases, devices=devices),
        out_shape=(block, block),
        in_specs=[IN_VMEM] * 6,
        out_specs=(IN_VMEM, IN_VMEM),
        scratch_shapes=shapes,
        compiler_params=grant(shapes),
        cost_estimate=pl.CostEstimate(flops=2**33, bytes_accessed=2**24, transcendentals=0),
        name="correlate_middle",
    )(rows, slide, w, norm, rest_energy, rest_acc)


def halves_kernel(*refs, phases, na, nb):
    mine_ref, other_ref = refs[na + nb :]
    a = sum(r[0] for r in refs[:na])
    b = sum(r[0] for r in refs[na : na + nb])
    block = jnp.concatenate([a, b], axis=0)
    per = L // phases
    half = per // 2
    first = lax.axis_index("win") % 2 == 0
    for tile in range(phases // 2):
        lower = block[tile * per : tile * per + half]
        upper = block[tile * per + half : (tile + 1) * per]
        mine_ref[tile * half : (tile + 1) * half] = jnp.where(first, lower, upper)
        other_ref[tile * half : (tile + 1) * half] = jnp.where(first, upper, lower)
    mine_ref[128:136] = block[256:264]
    other_ref[128:136] = block[256:264]


def halves(a, b, phases):
    half = jax.ShapeDtypeStruct((136, LANES), f32)
    return pl.pallas_call(
        lambda *refs: halves_kernel(*refs, phases=phases, na=len(a), nb=len(b)),
        out_shape=(half, half),
        in_specs=[IN_VMEM] * (len(a) + len(b)),
        out_specs=(IN_VMEM, IN_VMEM),
        compiler_params=SMALL,
        cost_estimate=pl.CostEstimate(flops=2**18, bytes_accessed=2**20, transcendentals=0),
        name="halves",
    )(*a, *b)


def finish_kernel(mine_ref, got_ref, out_ref, *, phases, devices):
    groups = LANES // 2
    per = L // phases
    half = per // 2
    me = lax.axis_index("win")
    first = me % 2 == 0
    straight = panel_of(me, devices) == 0
    place = iota((LANES, LANES), 0)
    wanted = (place // (2 * phases)) * phases + place % (2 * phases) - phases
    gather = (
        ((place % (2 * phases) >= phases) & (iota((LANES, LANES), 1) % groups == wanted)).astype(f32).astype(bf16)
    )
    low = iota((half, LANES), 1) < groups
    sides = []
    for ref in (mine_ref, got_ref):
        extra = ref[128:136]
        norm = math.sqrt(CT * L) * lax.rsqrt(pick(extra, gather))[:1]
        scale = lax.rsqrt(extra + epsilon)
        sides.append((ref, norm, scale))
    for tile in range(phases // 2):
        scaled = []
        for ref, norm, scale in sides:
            columns = []
            for phase in (2 * tile, 2 * tile + 1):
                if half >= 8:
                    count = half // 8
                    at = [2 * phases * k + phase for k in range(2 * count)]
                    pieces = [scale[:, i : i + 1] for i in at]
                    columns.append(
                        jnp.concatenate(
                            [jnp.where(first, pieces[k], pieces[k + count]) for k in range(count)], axis=0
                        )
                    )
                else:
                    columns.append(
                        jnp.where(first, scale[:half, phase : phase + 1], scale[half : 2 * half, phase : phase + 1])
                    )
            rows = ref[tile * half : (tile + 1) * half]
            scaled.append(rows * (jnp.where(low, columns[0], columns[1]) * norm))
        mine, got = scaled
        zero, one = jnp.where(straight, mine, got), jnp.where(straight, got, mine)
        out_ref[pl.ds(2 * tile, half, stride=phases), :] = jnp.where(low, zero, pltpu.roll(one, groups, 1))
        out_ref[pl.ds(2 * tile + 1, half, stride=phases), :] = jnp.where(low, pltpu.roll(zero, groups, 1), one)


def finish(mine, got, phases, devices):
    return pl.pallas_call(
        lambda *refs: finish_kernel(*refs, phases=phases, devices=devices),
        out_shape=jax.ShapeDtypeStruct((L // 2, LANES), f32),
        in_specs=[IN_VMEM, IN_VMEM],
        out_specs=IN_VMEM,
        compiler_params=SMALL,
        cost_estimate=pl.CostEstimate(flops=2**18, bytes_accessed=2**18, transcendentals=0),
        name="finish",
    )(mine, got)


def route_kernel(start_ref, records_ref, early_ref, late_ref, *, for_sibling, devices):
    me = lax.axis_index("win")
    panel = panel_of(me, devices)
    if for_sibling:
        panel = 1 - panel
    held = records_ref.shape[0]
    per_chip = 2 * CT // devices
    row = iota((CT, held), 0)
    target = jnp.bitwise_xor(target_of(row // per_chip, panel, devices), me // 2)
    core = jnp.bitwise_xor(panel, panel_of(2 * target, devices))
    channel = target * per_chip + (row % per_chip + per_chip // 2 * core) % per_chip
    routed = (channel + start_ref[panel] - me * held == iota((CT, held), 1)).astype(f32).astype(bf16)
    half = early_ref.shape[1]
    late_ref[...] = dot(routed, records_ref[:, half:]).astype(bf16)
    early_ref[...] = dot(routed, records_ref[:, :half]).astype(bf16)


def route(panel_start, records, for_sibling, devices):
    half = jax.ShapeDtypeStruct((CT, records.shape[1] // 2), bf16)
    return pl.pallas_call(
        lambda *refs: route_kernel(*refs, for_sibling=for_sibling, devices=devices),
        out_shape=(half, half),
        in_specs=[pl.BlockSpec(memory_space=pltpu.SMEM), IN_VMEM],
        out_specs=(IN_VMEM, IN_VMEM),
        compiler_params=pltpu.CompilerParams(vmem_limit_bytes=SPARE),
        cost_estimate=pl.CostEstimate(flops=2**27, bytes_accessed=2**21, transcendentals=0),
        name="route_away" if for_sibling else "route_home",
    )(panel_start, records)


def add_kernel(kept_ref, got_ref, keep_ref, send_ref):
    half = keep_ref.shape[0]
    keep_ref[...] = kept_ref[:half] + got_ref[:half]
    send_ref[...] = kept_ref[half:] + got_ref[half:]


def sum_kernel(kept_ref, got_ref, sum_ref):
    sum_ref[...] = kept_ref[...] + got_ref[...]


def summed(kept, got):
    return pl.pallas_call(
        sum_kernel,
        out_shape=jax.ShapeDtypeStruct(kept.shape, kept.dtype),
        in_specs=[IN_VMEM, IN_VMEM],
        out_specs=IN_VMEM,
        compiler_params=SMALL,
        cost_estimate=pl.CostEstimate(flops=2**33, bytes_accessed=2**20, transcendentals=0),
        name="sum",
    )(kept, got)


def added(kept, got):
    half = kept.shape[0] // 2
    if kept.dtype == bf16 and half % 16:
        whole = kept + got
        return whole[:half], whole[half:]
    part = jax.ShapeDtypeStruct((half, *kept.shape[1:]), kept.dtype)
    return pl.pallas_call(
        add_kernel,
        out_shape=(part, part),
        in_specs=[IN_VMEM, IN_VMEM],
        out_specs=(IN_VMEM, IN_VMEM),
        compiler_params=SMALL,
        cost_estimate=pl.CostEstimate(flops=2**32, bytes_accessed=2**20, transcendentals=0),
        name="add",
    )(kept, got)


def local(records, templates, panel_start):
    devices = lax.axis_size("win")
    panel = panel_of(lax.axis_index("win"), devices)
    phases = devices // 2
    pairs = (L // phases + 2) // 2
    orders = bits_of(devices)

    def sibling(value):
        return lax.ppermute(value, "win", [(d, d ^ 1) for d in range(devices)])

    def exchange(value, step):
        return lax.ppermute(value, "win", [(d, d ^ 1 ^ orders[panel_of(d, devices)][step]) for d in range(devices)])

    def scattered(keep, send, step):
        got = exchange(send, step)
        if step == len(orders[0]) - 1:
            return keep, got
        return scattered(*added(keep, got), step + 1)

    away_early, away_late = route(panel_start, records, True, devices)
    got_late, got_early = sibling(away_late), sibling(away_early)
    home_early, home_late = route(panel_start, records, False, devices)
    wanted = lax.dynamic_index_in_dim(templates, panel, 0, keepdims=False)
    given = lax.dynamic_index_in_dim(templates, 1 - panel, 0, keepdims=False)
    w, norm = shifted(wanted, sibling(given), phases, pairs)

    late = scattered(*added(home_late, got_late), 0)
    early = scattered(*added(home_early, got_early), 0)
    rest_rows, rest_energy, rest_acc = correlate_late(late, w, phases)
    send_a, keep_a, rows, slide = correlate_early(early, w, rest_rows, rest_acc, phases, devices)
    send_b, keep_b = correlate_middle(rows, slide, w, norm, rest_energy, rest_acc, phases, devices)
    a = scattered(keep_a, send_a, 0)
    b = scattered(keep_b, send_b, 0)
    mine, other = halves([summed(*a)], b, phases)
    return finish(mine, sibling(other), phases, devices)


def solution(mesh):
    placed = (P("win", "parts"), P(None, None, "win", None), P("parts"))
    return jax.shard_map(
        local, mesh=mesh, in_specs=placed, out_specs=P(("parts", "win"), None), check_vma=False
    )
```

time: 422 us -> 55.2 us (0.13)
  matrix products: 165 us -> 0 us
  blocking collectives: 136 us -> 0 us
  waiting for transfers between devices: 66.8 us -> 11.1 us
  starting transfers between devices: 2.57 us -> 27.1 us
  other arithmetic: 21.1 us -> 0 us
  between operations: 17.8 us -> 0.13 us
  Pallas kernels: 0 us -> 12.7 us
  local copies, waits for them, and re-layouts: 9.66 us -> 3.15 us
    conv_general_dilated x1 -> x0, matrix products: 165 us -> none  [correlate(): lax.conv_general_dilated(inputs, filters, (1,), 'VALID', dimension_number...]
    psum x1 -> x0, blocking collectives: 89.9 us -> none  [local(): template_norm = lax.psum(own_norm, 'win')]
    all_gather x1 -> x0, waiting for transfers between devices: 66.8 us -> none  [local(): lax.all_gather(templates, 'win', axis=2, tiled=True)]
    all_to_all x1 -> x0, blocking collectives: 46.6 us -> none  [local(): lax.all_to_all(records, 'win', split_axis=1, concat_axis=0, tiled=True)]
    ppermute x2 -> x16, starting transfers between devices: 2.57 us -> 27.1 us  [the longest x12 25.9 us: exchange(): lax.ppermute(value, 'win', [(d, d ^ 1 ^ orders[panel_of(d, devices)][step...]
    another operation x1 -> x0, other arithmetic: 17.8 us -> none  [local(): lax.reduce_window(squares, jnp.float32(0.0), lax.add, (1, L), (1, 1), 'VA...]
    pallas_call x0 -> x19, Pallas kernels: none -> 12.7 us  [the longest x1 3.26 us: correlate_late(): pl.pallas_call(lambda *refs: late_kernel(*refs, phases=phases), out_shape...]
    ppermute x2 -> x16, waiting for transfers between devices: 0.01 us -> 11.1 us  [the longest x12 9.88 us: exchange(): lax.ppermute(value, 'win', [(d, d ^ 1 ^ orders[panel_of(d, devices)][step...]
  transfers between devices with their start and end apart: 3 -> 16, of which waited for: 1 -> 8; matrix products, arithmetic and copies ran while one was open for 6% -> 2% of each run, Pallas kernels for 0% -> 16%
where the time goes in v2:
time: 55.2 us; the launch traced here: 54.2 us
  starting transfers between devices  27.1 us (49%)
  Pallas kernels  12.7 us (23%)
  waiting for transfers between devices  11.1 us (20%)
  local copies, waits for them, and re-layouts  3.15 us (6%)
    ppermute x12, starting transfers between devices, exchange(): lax.ppermute(value, 'win', [(d, d ^ 1 ^ orders[panel_of(d, devices)][step...  25.9 us
    ppermute x12, waiting for transfers between devices, exchange(): lax.ppermute(value, 'win', [(d, d ^ 1 ^ orders[panel_of(d, devices)][step...  9.88 us
    pallas_call x1, Pallas kernels, correlate_late(): pl.pallas_call(lambda *refs: late_kernel(*refs, phases=phases), out_shape...  3.26 us
    pallas_call x1, Pallas kernels, shifted(): pl.pallas_call(lambda *refs: shift_kernel(*refs, phases=phases), out_shap...  2.25 us
    pallas_call x2, Pallas kernels, route(): pl.pallas_call(lambda *refs: route_kernel(*refs, for_sibling=for_sibling,...  2.2 us
    pallas_call x1, Pallas kernels, correlate_early(): pl.pallas_call(lambda *refs: early_kernel(*refs, phases=phases, devices=d...  1.93 us
    unnamed x8, local copies, waits for them, and re-layouts  1.89 us
    pallas_call x1, Pallas kernels, correlate_middle(): pl.pallas_call(lambda *refs: middle_kernel(*refs, phases=phases, devices=...  1.74 us
  transfers between devices with their start and end apart: 16, of which 8 were waited for; matrix products, arithmetic and copies ran while one was open for 2% of the time, Pallas kernels for 16%

profile of v2, /device:TPU:0, one launch (start us, length us, event | category | flops | bytes accessed | tf_op | source)
XLA Modules:
  0.0 54.2 jit_solution(9071271969672551166)
XLA Ops:
  0.0 0.0 copy-start
  0.0 1.2 %copy-done = bf16[128,4096]{1,0:T(8,128)(2,1)S(1)} copy-done((bf16[128,4096]{1,0:T(8,128)(2,1)S(1)}, bf16[128,4096]{1,0:T(8,128)(2,1)}, u32[]{:S(2)}) %copy-start) | copy-done | bytes 1048600
  1.2 0.0 copy-start.2
  1.2 0.7 %copy-done.2 = s32[2]{0:T(128)S(1)} copy-done((s32[2]{0:T(128)S(1)}, s32[2]{0:T(128)}, u32[]{:S(2)}) %copy-start.2) | copy-done | bytes 32
  1.9 1.1 %route_away.1 = (bf16[128,2048]{1,0:T(8,128)(2,1)S(1)}, bf16[128,2048]{1,0:T(8,128)(2,1)S(1)}) custom-call(s32[2]{0:T(128)S(1)} %copy-done.2, bf16[128,4096]{1,0:T(8,128)(2,1)S(1)} %copy-done), custom_call_target="tpu_custom_call" | custom-call | flops 134217728 | bytes 2097152 | tf_op jit(solution)/shard_map/route_away/pallas_call | solution.py:418
  3.0 0.5 collective-permute-start.5
  3.5 0.1 collective-permute-start
  3.6 1.3 %dynamic-slice_bitcast_fusion = (bf16[64,8,512]{2,1,0:T(8,128)(2,1)S(1)}, bf16[512,512]{1,0:T(8,128)(2,1)S(1)}) fusion(bf16[2,64,8,512]{3,2,1,0:T(8,128)(2,1)} %param.4, s32[]{:T(128)S(6)} %select_n.16, s32[]{:T(128)S(6)} %select_n.15), kind=kLoop, calls=%fused_computation | loop fusion | bytes 2097160 | tf_op jit(solution)/shard_map/jit(dynamic_index_in_dim)/squeeze | solution.py:491
  4.9 0.5 collective-permute-start.4
  5.4 0.0 copy-done.1
  5.4 0.0 copy-done.3
  5.4 1.1 %route_home.1 = (bf16[128,2048]{1,0:T(8,128)(2,1)S(1)}, bf16[128,2048]{1,0:T(8,128)(2,1)S(1)}) custom-call(s32[2]{0:T(128)S(1)} %copy-done.3, bf16[128,4096]{1,0:T(8,128)(2,1)S(1)} %copy-done.1), custom_call_target="tpu_custom_call" | custom-call | flops 134217728 | bytes 2097152 | tf_op jit(solution)/shard_map/route_home/pallas_call | solution.py:418
  6.5 0.0 collective-permute-done.5.got_ref
  6.5 0.1 add.40
  6.5 2.7 %collective-permute-start.6 = (bf16[64,2048]{1,0:T(8,128)(2,1)S(1)}, bf16[64,2048]{1,0:T(8,128)(2,1)S(1)}, u32[]{:S(2)}, u32[]{:S(2)}) collective-permute-start(bf16[64,2048]{1,0:T(8,128)(2,1)S(1)} %get-tuple-element.54), channel_id=1, source_target_pairs={{0,3},{1,4},{2,7},{3,0},{4,1},{5,6},{6,5},{7,2},{8,13},{9,10},{10,... | collective-permute-start | bytes 786440 | tf_op jit(solution)/shard_map/ppermute | solution.py:479
  9.2 0.0 collective-permute-done.got_ref
  9.2 0.1 add.37
  9.3 0.1 collective-permute-start.1
  9.4 0.0 collective-permute-done.4
  9.4 2.2 %shift_templates.1 = (bf16[1,8576,128]{2,1,0:T(8,128)(2,1)S(1)}, f32[8,128]{1,0:T(8,128)S(1)}) custom-call(bf16[512,512]{1,0:T(8,128)(2,1)S(1)} %get-tuple-element.80.refs_0_, bf16[512,512]{1,0:T(8,128)(2,1)S(1)} %bitcast.5), custom_call_target="tpu_custom_call" | custom-call | flops 1073741824 | bytes 16777216 | tf_op jit(solution)/shard_map/shift_templates/pallas_call | solution.py:85
  11.6 1.6 %collective-permute-done.6.got_ref = bf16[64,2048]{1,0:T(8,128)(2,1)S(1)} collective-permute-done((bf16[64,2048]{1,0:T(8,128)(2,1)S(1)}, bf16[64,2048]{1,0:T(8,128)(2,1)S(1)}, u32[]{:S(2)}, u32[]{:S(2)}) %collective-permute-start.6) | collective-permute-done | bytes 262176 | tf_op jit(solution)/shard_map/ppermute | solution.py:479
  13.3 2.2 %collective-permute-start.7 = (bf16[32,2048]{1,0:T(8,128)(2,1)S(1)}, bf16[32,2048]{1,0:T(8,128)(2,1)S(1)}, u32[]{:S(2)}, u32[]{:S(2)}) collective-permute-start(bf16[32,2048]{1,0:T(8,128)(2,1)S(1)} %get-tuple-element.56), channel_id=1, source_target_pairs={{0,5},{1,2},{2,1},{3,6},{4,7},{5,0},{6,3},{7,4},{8,11},{9,12},{10,... | collective-permute-start | bytes 393224 | tf_op jit(solution)/shard_map/ppermute | solution.py:479
  15.5 0.7 %collective-permute-done.1.got_ref = bf16[64,2048]{1,0:T(8,128)(2,1)S(1)} collective-permute-done((bf16[64,2048]{1,0:T(8,128)(2,1)S(1)}, bf16[64,2048]{1,0:T(8,128)(2,1)S(1)}, u32[]{:S(2)}, u32[]{:S(2)}) %collective-permute-start.1) | collective-permute-done | bytes 262176 | tf_op jit(solution)/shard_map/ppermute | solution.py:479
  16.2 2.3 %collective-permute-start.2 = (bf16[32,2048]{1,0:T(8,128)(2,1)S(1)}, bf16[32,2048]{1,0:T(8,128)(2,1)S(1)}, u32[]{:S(2)}, u32[]{:S(2)}) collective-permute-start(bf16[32,2048]{1,0:T(8,128)(2,1)S(1)} %get-tuple-element.47), channel_id=1, source_target_pairs={{0,5},{1,2},{2,1},{3,6},{4,7},{5,0},{6,3},{7,4},{8,11},{9,12},{10,... | collective-permute-start | bytes 393224 | tf_op jit(solution)/shard_map/ppermute | solution.py:479
  18.5 0.0 collective-permute-done.7.got_ref
  18.5 2.5 %collective-permute-start.8 = (bf16[16,2048]{1,0:T(8,128)(2,1)S(1)}, bf16[16,2048]{1,0:T(8,128)(2,1)S(1)}, u32[]{:S(2)}, u32[]{:S(2)}) collective-permute-start(bf16[16,2048]{1,0:T(8,128)(2,1)S(1)} %get-tuple-element.58), channel_id=1, source_target_pairs={{0,9},{1,8},{2,11},{3,10},{4,13},{5,12},{6,15},{7,14},{8,1},{9,0},... | collective-permute-start | bytes 196616 | tf_op jit(solution)/shard_map/ppermute | solution.py:479
  21.0 0.2 collective-permute-done.2.got_ref
  21.1 3.3 %collective-permute-start.3 = (bf16[16,2048]{1,0:T(8,128)(2,1)S(1)}, bf16[16,2048]{1,0:T(8,128)(2,1)S(1)}, u32[]{:S(2)}, u32[]{:S(2)}) collective-permute-start(bf16[16,2048]{1,0:T(8,128)(2,1)S(1)} %get-tuple-element.49), channel_id=1, source_target_pairs={{0,9},{1,8},{2,11},{3,10},{4,13},{5,12},{6,15},{7,14},{8,1},{9,0},... | collective-permute-start | bytes 196616 | tf_op jit(solution)/shard_map/ppermute | solution.py:479
  24.4 0.0 collective-permute-done.8.refs_1_
  24.4 3.3 %correlate_late.1 = (f32[256,128]{1,0:T(8,128)S(1)}, f32[256,128]{1,0:T(8,128)S(1)}, f32[256,512]{1,0:T(8,128)S(1)}) custom-call(bf16[16,2048]{1,0:T(8,128)(2,1)S(1)} %get-tuple-element.57.refs_0_, bf16[16,2048]{1,0:T(8,128)(2,1)S(1)} %collective-permute-done.8.refs_1_, bf16[1,8576,128]{2,1,0:T(8,128)(2,1)S(1)} %get-tuple-element.50.refs_2_), custom_call_target="tpu_custom_call" | custom-call | flops 2147483648 | bytes 4194304 | tf_op jit(solution)/shard_map/correlate_late/pallas_call | solution.py:255
  27.7 0.4 collective-permute-done.3.refs_1_
  28.1 1.9 %correlate_early.1 = (f32[4,128,128]{2,1,0:T(8,128)S(1)}, f32[4,128,128]{2,1,0:T(8,128)S(1)}, f32[512,128]{1,0:T(8,128)S(1)}, bf16[8,320,256]{2,1,0:T(8,128)(2,1)S(1)}) custom-call(bf16[16,2048]{1,0:T(8,128)(2,1)S(1)} %get-tuple-element.48.refs_0_, bf16[16,2048]{1,0:T(8,128)(2,1)S(1)} %collective-permute-done.3.refs_1_, ...), custom_call_target="tpu_custom_call" | custom-call | flops 4294967296 | bytes 16777216 | tf_op jit(solution)/shard_map/correlate_early/pallas_call | solution.py:278
  30.0 1.3 %collective-permute-start.9 = (f32[4,128,128]{2,1,0:T(8,128)S(1)}, f32[4,128,128]{2,1,0:T(8,128)S(1)}, u32[]{:S(2)}, u32[]{:S(2)}) collective-permute-start(f32[4,128,128]{2,1,0:T(8,128)S(1)} %get-tuple-element.62), channel_id=1, source_target_pairs={{0,3},{1,4},{2,7},{3,0},{4,1},{5,6},{6,5},{7,2},{8,13},{9,10},{10,... | collective-permute-start | bytes 786440 | tf_op jit(solution)/shard_map/ppermute | solution.py:479
  31.3 1.7 %correlate_middle.1 = (f32[4,136,128]{2,1,0:T(8,128)S(1)}, f32[4,136,128]{2,1,0:T(8,128)S(1)}) custom-call(f32[512,128]{1,0:T(8,128)S(1)} %get-tuple-element.67.refs_0_, bf16[8,320,256]{2,1,0:T(8,128)(2,1)S(1)} %get-tuple-element.68.refs_1_, bf16[1,8576,128]{2,1,0:T(8,128)(2,1)S(1)} %get-tuple-element.50.refs_2_, f32[8,128]{1,0:T(8,128)S(1)} %get-tuple-element.69.refs_3_, ...), custom_call_target="tpu_custom_call" | custom-call | flops 8589934592 | bytes 16777216 | tf_op jit(solution)/shard_map/correlate_middle/pallas_call | solution.py:300
  33.1 0.6 %collective-permute-start.12 = (f32[4,136,128]{2,1,0:T(8,128)S(1)}, f32[4,136,128]{2,1,0:T(8,128)S(1)}, u32[]{:S(2)}, u32[]{:S(2)}) collective-permute-start(f32[4,136,128]{2,1,0:T(8,128)S(1)} %get-tuple-element.72), channel_id=1, source_target_pairs={{0,3},{1,4},{2,7},{3,0},{4,1},{5,6},{6,5},{7,2},{8,13},{9,10},{10,... | collective-permute-start | bytes 835592 | tf_op jit(solution)/shard_map/ppermute | solution.py:479
  33.7 2.2 %collective-permute-done.9.got_ref = f32[4,128,128]{2,1,0:T(8,128)S(1)} collective-permute-done((f32[4,128,128]{2,1,0:T(8,128)S(1)}, f32[4,128,128]{2,1,0:T(8,128)S(1)}, u32[]{:S(2)}, u32[]{:S(2)}) %collective-permute-start.9) | collective-permute-done | bytes 262176 | tf_op jit(solution)/shard_map/ppermute | solution.py:479
  35.9 1.1 %collective-permute-start.10 = (f32[2,128,128]{2,1,0:T(8,128)S(1)}, f32[2,128,128]{2,1,0:T(8,128)S(1)}, u32[]{:S(2)}, u32[]{:S(2)}) collective-permute-start(f32[2,128,128]{2,1,0:T(8,128)S(1)} %get-tuple-element.64), channel_id=1, source_target_pairs={{0,5},{1,2},{2,1},{3,6},{4,7},{5,0},{6,3},{7,4},{8,11},{9,12},{10,... | collective-permute-start | bytes 393224 | tf_op jit(solution)/shard_map/ppermute | solution.py:479
  37.0 2.2 %collective-permute-done.12.got_ref = f32[4,136,128]{2,1,0:T(8,128)S(1)} collective-permute-done((f32[4,136,128]{2,1,0:T(8,128)S(1)}, f32[4,136,128]{2,1,0:T(8,128)S(1)}, u32[]{:S(2)}, u32[]{:S(2)}) %collective-permute-start.12) | collective-permute-done | bytes 278560 | tf_op jit(solution)/shard_map/ppermute | solution.py:479
  39.3 2.4 %collective-permute-start.13 = (f32[2,136,128]{2,1,0:T(8,128)S(1)}, f32[2,136,128]{2,1,0:T(8,128)S(1)}, u32[]{:S(2)}, u32[]{:S(2)}) collective-permute-start(f32[2,136,128]{2,1,0:T(8,128)S(1)} %get-tuple-element.74), channel_id=1, source_target_pairs={{0,5},{1,2},{2,1},{3,6},{4,7},{5,0},{6,3},{7,4},{8,11},{9,12},{10,... | collective-permute-start | bytes 417800 | tf_op jit(solution)/shard_map/ppermute | solution.py:479
  41.7 0.0 collective-permute-done.10.got_ref
  41.7 4.3 %collective-permute-start.11 = (f32[1,128,128]{2,1,0:T(8,128)S(1)}, f32[1,128,128]{2,1,0:T(8,128)S(1)}, u32[]{:S(2)}, u32[]{:S(2)}) collective-permute-start(f32[1,128,128]{2,1,0:T(8,128)S(1)} %get-tuple-element.66), channel_id=1, source_target_pairs={{0,9},{1,8},{2,11},{3,10},{4,13},{5,12},{6,15},{7,14},{8,1},{9,0},... | collective-permute-start | bytes 196616 | tf_op jit(solution)/shard_map/ppermute | solution.py:479
  45.9 0.0 collective-permute-done.13.got_ref
  46.0 3.4 %collective-permute-start.14 = (f32[1,136,128]{2,1,0:T(8,128)S(1)}, f32[1,136,128]{2,1,0:T(8,128)S(1)}, u32[]{:S(2)}, u32[]{:S(2)}) collective-permute-start(f32[1,136,128]{2,1,0:T(8,128)S(1)} %get-tuple-element.76), channel_id=1, source_target_pairs={{0,9},{1,8},{2,11},{3,10},{4,13},{5,12},{6,15},{7,14},{8,1},{9,0},... | collective-permute-start | bytes 208904 | tf_op jit(solution)/shard_map/ppermute | solution.py:479
  49.3 0.0 collective-permute-done.11.got_ref
  49.4 2.5 %collective-permute-done.14.refs_2_ = f32[1,136,128]{2,1,0:T(8,128)S(1)} collective-permute-done((f32[1,136,128]{2,1,0:T(8,128)S(1)}, f32[1,136,128]{2,1,0:T(8,128)S(1)}, u32[]{:S(2)}, u32[]{:S(2)}) %collective-permute-start.14) | collective-permute-done | bytes 69664 | tf_op jit(solution)/shard_map/ppermute | solution.py:479
  51.9 0.1 collective-permute-start.15
  52.0 1.2 %collective-permute-done.15.refs_1_ = f32[136,128]{1,0:T(8,128)S(1)} collective-permute-done((f32[136,128]{1,0:T(8,128)S(1)}, f32[136,128]{1,0:T(8,128)S(1)}, u32[]{:S(2)}, u32[]{:S(2)}) %collective-permute-start.15) | collective-permute-done | bytes 69664 | tf_op jit(solution)/shard_map/ppermute | solution.py:476
  53.2 1.0 %finish.1 = f32[256,128]{1,0:T(8,128)} custom-call(f32[136,128]{1,0:T(8,128)S(1)} %get-tuple-element.77.refs_0_, f32[136,128]{1,0:T(8,128)S(1)} %collective-permute-done.15.refs_1_), custom_call_target="tpu_custom_call" | custom-call | flops 262144 | bytes 262144 | tf_op jit(solution)/shard_map/finish/pallas_call | solution.py:388
  (12 shorter events, 0.2 us)
Async XLA Ops:
  0.0 1.2 %copy-start = (bf16[128,4096]{1,0:T(8,128)(2,1)S(1)}, bf16[128,4096]{1,0:T(8,128)(2,1)}, u32[]{:S(2)}) copy-start(bf16[128,4096]{1,0:T(8,128)(2,1)} %refs_1_.3) | copy-start | bytes 3145732
  1.2 0.7 %copy-start.2 = (s32[2]{0:T(128)S(1)}, s32[2]{0:T(128)}, u32[]{:S(2)}) copy-start(s32[2]{0:T(128)} %refs_0_.3) | copy-start | bytes 28
  1.9 3.5 %copy-start.1 = (bf16[128,4096]{1,0:T(8,128)(2,1)S(1)}, bf16[128,4096]{1,0:T(8,128)(2,1)}, u32[]{:S(2)}) copy-start(bf16[128,4096]{1,0:T(8,128)(2,1)} %refs_1_.3) | copy-start | bytes 3145732
  1.9 3.5 %copy-start.3 = (s32[2]{0:T(128)S(1)}, s32[2]{0:T(128)}, u32[]{:S(2)}) copy-start(s32[2]{0:T(128)} %refs_0_.3) | copy-start | bytes 28
  3.0 3.5 %collective-permute-start.5 = (bf16[128,2048]{1,0:T(8,128)(2,1)S(1)}, bf16[128,2048]{1,0:T(8,128)(2,1)S(1)}, u32[]{:S(2)}, u32[]{:S(2)}) collective-permute-start(bf16[128,2048]{1,0:T(8,128)(2,1)S(1)} %get-tuple-element.52), channel_id=1, source_target_pairs={{0,1},{1,0},{2,3},{3,2},{4,5},{5,4},{6,7},{7,6},{8,9},{9,8},{10,11... | collective-permute-start | bytes 1572872 | tf_op jit(solution)/shard_map/ppermute | solution.py:476
  3.5 5.7 %collective-permute-start = (bf16[128,2048]{1,0:T(8,128)(2,1)S(1)}, bf16[128,2048]{1,0:T(8,128)(2,1)S(1)}, u32[]{:S(2)}, u32[]{:S(2)}) collective-permute-start(bf16[128,2048]{1,0:T(8,128)(2,1)S(1)} %get-tuple-element.43), channel_id=1, source_target_pairs={{0,1},{1,0},{2,3},{3,2},{4,5},{5,4},{6,7},{7,6},{8,9},{9,8},{10,11... | collective-permute-start | bytes 1572872 | tf_op jit(solution)/shard_map/ppermute | solution.py:476
  4.9 4.5 %collective-permute-start.4 = (bf16[64,8,512]{2,1,0:T(8,128)(2,1)S(1)}, bf16[64,8,512]{2,1,0:T(8,128)(2,1)S(1)}, u32[]{:S(2)}, u32[]{:S(2)}) collective-permute-start(bf16[64,8,512]{2,1,0:T(8,128)(2,1)S(1)} %get-tuple-element.79), channel_id=1, source_target_pairs={{0,1},{1,0},{2,3},{3,2},{4,5},{5,4},{6,7},{7,6},{8,9},{9,8},{10,11... | collective-permute-start | bytes 1572872 | tf_op jit(solution)/shard_map/ppermute | solution.py:476
  6.5 6.7 %collective-permute-start.6 = (bf16[64,2048]{1,0:T(8,128)(2,1)S(1)}, bf16[64,2048]{1,0:T(8,128)(2,1)S(1)}, u32[]{:S(2)}, u32[]{:S(2)}) collective-permute-start(bf16[64,2048]{1,0:T(8,128)(2,1)S(1)} %get-tuple-element.54), channel_id=1, source_target_pairs={{0,3},{1,4},{2,7},{3,0},{4,1},{5,6},{6,5},{7,2},{8,13},{9,10},{10,... | collective-permute-start | bytes 786440 | tf_op jit(solution)/shard_map/ppermute | solution.py:479
  9.3 6.9 %collective-permute-start.1 = (bf16[64,2048]{1,0:T(8,128)(2,1)S(1)}, bf16[64,2048]{1,0:T(8,128)(2,1)S(1)}, u32[]{:S(2)}, u32[]{:S(2)}) collective-permute-start(bf16[64,2048]{1,0:T(8,128)(2,1)S(1)} %get-tuple-element.45), channel_id=1, source_target_pairs={{0,3},{1,4},{2,7},{3,0},{4,1},{5,6},{6,5},{7,2},{8,13},{9,10},{10,... | collective-permute-start | bytes 786440 | tf_op jit(solution)/shard_map/ppermute | solution.py:479
  13.3 5.2 %collective-permute-start.7 = (bf16[32,2048]{1,0:T(8,128)(2,1)S(1)}, bf16[32,2048]{1,0:T(8,128)(2,1)S(1)}, u32[]{:S(2)}, u32[]{:S(2)}) collective-permute-start(bf16[32,2048]{1,0:T(8,128)(2,1)S(1)} %get-tuple-element.56), channel_id=1, source_target_pairs={{0,5},{1,2},{2,1},{3,6},{4,7},{5,0},{6,3},{7,4},{8,11},{9,12},{10,... | collective-permute-start | bytes 393224 | tf_op jit(solution)/shard_map/ppermute | solution.py:479
  16.2 4.9 %collective-permute-start.2 = (bf16[32,2048]{1,0:T(8,128)(2,1)S(1)}, bf16[32,2048]{1,0:T(8,128)(2,1)S(1)}, u32[]{:S(2)}, u32[]{:S(2)}) collective-permute-start(bf16[32,2048]{1,0:T(8,128)(2,1)S(1)} %get-tuple-element.47), channel_id=1, source_target_pairs={{0,5},{1,2},{2,1},{3,6},{4,7},{5,0},{6,3},{7,4},{8,11},{9,12},{10,... | collective-permute-start | bytes 393224 | tf_op jit(solution)/shard_map/ppermute | solution.py:479
  18.5 5.9 %collective-permute-start.8 = (bf16[16,2048]{1,0:T(8,128)(2,1)S(1)}, bf16[16,2048]{1,0:T(8,128)(2,1)S(1)}, u32[]{:S(2)}, u32[]{:S(2)}) collective-permute-start(bf16[16,2048]{1,0:T(8,128)(2,1)S(1)} %get-tuple-element.58), channel_id=1, source_target_pairs={{0,9},{1,8},{2,11},{3,10},{4,13},{5,12},{6,15},{7,14},{8,1},{9,0},... | collective-permute-start | bytes 196616 | tf_op jit(solution)/shard_map/ppermute | solution.py:479
  21.1 7.0 %collective-permute-start.3 = (bf16[16,2048]{1,0:T(8,128)(2,1)S(1)}, bf16[16,2048]{1,0:T(8,128)(2,1)S(1)}, u32[]{:S(2)}, u32[]{:S(2)}) collective-permute-start(bf16[16,2048]{1,0:T(8,128)(2,1)S(1)} %get-tuple-element.49), channel_id=1, source_target_pairs={{0,9},{1,8},{2,11},{3,10},{4,13},{5,12},{6,15},{7,14},{8,1},{9,0},... | collective-permute-start | bytes 196616 | tf_op jit(solution)/shard_map/ppermute | solution.py:479
  30.0 5.9 %collective-permute-start.9 = (f32[4,128,128]{2,1,0:T(8,128)S(1)}, f32[4,128,128]{2,1,0:T(8,128)S(1)}, u32[]{:S(2)}, u32[]{:S(2)}) collective-permute-start(f32[4,128,128]{2,1,0:T(8,128)S(1)} %get-tuple-element.62), channel_id=1, source_target_pairs={{0,3},{1,4},{2,7},{3,0},{4,1},{5,6},{6,5},{7,2},{8,13},{9,10},{10,... | collective-permute-start | bytes 786440 | tf_op jit(solution)/shard_map/ppermute | solution.py:479
  33.1 6.2 %collective-permute-start.12 = (f32[4,136,128]{2,1,0:T(8,128)S(1)}, f32[4,136,128]{2,1,0:T(8,128)S(1)}, u32[]{:S(2)}, u32[]{:S(2)}) collective-permute-start(f32[4,136,128]{2,1,0:T(8,128)S(1)} %get-tuple-element.72), channel_id=1, source_target_pairs={{0,3},{1,4},{2,7},{3,0},{4,1},{5,6},{6,5},{7,2},{8,13},{9,10},{10,... | collective-permute-start | bytes 835592 | tf_op jit(solution)/shard_map/ppermute | solution.py:479
  35.9 5.7 %collective-permute-start.10 = (f32[2,128,128]{2,1,0:T(8,128)S(1)}, f32[2,128,128]{2,1,0:T(8,128)S(1)}, u32[]{:S(2)}, u32[]{:S(2)}) collective-permute-start(f32[2,128,128]{2,1,0:T(8,128)S(1)} %get-tuple-element.64), channel_id=1, source_target_pairs={{0,5},{1,2},{2,1},{3,6},{4,7},{5,0},{6,3},{7,4},{8,11},{9,12},{10,... | collective-permute-start | bytes 393224 | tf_op jit(solution)/shard_map/ppermute | solution.py:479
  39.3 6.7 %collective-permute-start.13 = (f32[2,136,128]{2,1,0:T(8,128)S(1)}, f32[2,136,128]{2,1,0:T(8,128)S(1)}, u32[]{:S(2)}, u32[]{:S(2)}) collective-permute-start(f32[2,136,128]{2,1,0:T(8,128)S(1)} %get-tuple-element.74), channel_id=1, source_target_pairs={{0,5},{1,2},{2,1},{3,6},{4,7},{5,0},{6,3},{7,4},{8,11},{9,12},{10,... | collective-permute-start | bytes 417800 | tf_op jit(solution)/shard_map/ppermute | solution.py:479
  41.7 7.7 %collective-permute-start.11 = (f32[1,128,128]{2,1,0:T(8,128)S(1)}, f32[1,128,128]{2,1,0:T(8,128)S(1)}, u32[]{:S(2)}, u32[]{:S(2)}) collective-permute-start(f32[1,128,128]{2,1,0:T(8,128)S(1)} %get-tuple-element.66), channel_id=1, source_target_pairs={{0,9},{1,8},{2,11},{3,10},{4,13},{5,12},{6,15},{7,14},{8,1},{9,0},... | collective-permute-start | bytes 196616 | tf_op jit(solution)/shard_map/ppermute | solution.py:479
  46.0 5.9 %collective-permute-start.14 = (f32[1,136,128]{2,1,0:T(8,128)S(1)}, f32[1,136,128]{2,1,0:T(8,128)S(1)}, u32[]{:S(2)}, u32[]{:S(2)}) collective-permute-start(f32[1,136,128]{2,1,0:T(8,128)S(1)} %get-tuple-element.76), channel_id=1, source_target_pairs={{0,9},{1,8},{2,11},{3,10},{4,13},{5,12},{6,15},{7,14},{8,1},{9,0},... | collective-permute-start | bytes 208904 | tf_op jit(solution)/shard_map/ppermute | solution.py:479
  51.9 1.3 %collective-permute-start.15 = (f32[136,128]{1,0:T(8,128)S(1)}, f32[136,128]{1,0:T(8,128)S(1)}, u32[]{:S(2)}, u32[]{:S(2)}) collective-permute-start(f32[136,128]{1,0:T(8,128)S(1)} %get-tuple-element.78), channel_id=1, source_target_pairs={{0,1},{1,0},{2,3},{3,2},{4,5},{5,4},{6,7},{7,6},{8,9},{9,8},{10,11... | collective-permute-start | bytes 208904 | tf_op jit(solution)/shard_map/ppermute | solution.py:476

commit v3 on v2

v3 whole, which is shorter than its diff:
```python
import math

import jax
import jax.numpy as jnp
from jax import lax
from jax.experimental import pallas as pl
from jax.experimental.pallas import tpu as pltpu
from jax.sharding import PartitionSpec as P

CT = 128
L = 512
LANES = 128
epsilon = 1e-06
f32 = jnp.float32
bf16 = jnp.bfloat16
SPARE = 12 * 2**20
IN_VMEM = pl.BlockSpec(memory_space=pltpu.VMEM)
SMALL = pltpu.CompilerParams(vmem_limit_bytes=8 * 2**20)


def iota(shape, dim):
    return lax.broadcasted_iota(jnp.int32, shape, dim)


def dot(a, b, dims=(((1,), (0,)), ((), ()))):
    return lax.dot_general(a, b, dims, preferred_element_type=f32)


def split3(v):
    high = v.astype(bf16)
    rest = v - high.astype(f32)
    middle = rest.astype(bf16)
    return high, middle, (rest - middle.astype(f32)).astype(bf16)


def pick(v, m):
    return sum(dot(part, m) for part in split3(v))


def picked(m, v):
    return sum(dot(m, part) for part in split3(v))


def shift_kernel(templates_ref, other_ref, w_ref, norm_ref, rows_ref, *, phases, devices):
    gc = other_ref.shape[0]
    panel = panel_of(lax.axis_index("win"), devices)
    groups = LANES // 2
    each = gc // groups
    channels = 2 * each
    versions, total, _ = w_ref.shape
    pad = channels * phases
    front = rows_ref.shape[0] - total
    rows_ref[pl.ds(0, front + pad), :] = jnp.zeros((front + pad, LANES), f32)
    rows_ref[pl.ds(front + pad + L * channels, total - pad - L * channels), :] = jnp.zeros(
        (total - pad - L * channels, LANES), f32
    )
    norm = jnp.zeros((1, LANES), f32)
    width = min(2, each) * LANES
    row, lane = iota((gc, width), 0), iota((gc, width), 1)
    for side, ref in enumerate((templates_ref.at[panel], other_ref)):
        for c in range(0, each, width // LANES):
            choose = (row == (lane % groups) * each + c + lane // LANES).astype(f32).astype(bf16)
            piece = dot(ref[...], choose, (((0,), (0,)), ((), ())))
            for i in range(width // LANES):
                one = piece[:, i * LANES : (i + 1) * LANES]
                norm = norm + jnp.sum(one * one, axis=0, keepdims=True)
                rows_ref[pl.ds(front + pad + side * each + c + i, L, stride=channels), :] = one
    norm_ref[...] = jnp.broadcast_to(norm, norm_ref.shape)
    low = iota((256, LANES), 1) < groups
    for v in range(versions):
        for at in range(0, total, 256):
            size = min(256, total - at)
            start = front + at - 2 * channels * v
            even = rows_ref[pl.ds(start, size), :]
            odd = rows_ref[pl.ds(start - channels, size), :]
            w_ref[v, at : at + size, :] = jnp.where(low[:size], even, odd).astype(bf16)


def shifted(templates, other, phases, pairs):
    channels = 2 * other.shape[1]
    versions = max(1, 8 // channels)
    total = 256 * pairs + channels * phases
    front = (2 * versions - 1) * channels + 8
    front = (front + 7) // 8 * 8
    gc = other.shape[0] * other.shape[1]
    return pl.pallas_call(
        lambda *refs: shift_kernel(*refs, phases=phases, devices=2 * phases),
        out_shape=(
            jax.ShapeDtypeStruct((versions, total, LANES), bf16),
            jax.ShapeDtypeStruct((8, LANES), f32),
        ),
        scratch_shapes=[pltpu.VMEM((front + total, LANES), f32)],
        compiler_params=pltpu.CompilerParams(vmem_limit_bytes=512 * (front + total) + SPARE),
        cost_estimate=pl.CostEstimate(flops=2**30, bytes_accessed=2**24, transcendentals=0),
        name="shift_templates",
    )(templates.reshape(-1, gc, L), other.reshape(gc, L))


def bits_of(devices):
    x, z, *rest = [1 << i for i in range(1, devices.bit_length() - 1)]
    return [x, z] + rest, [z, x] + rest


def panel_of(device, devices):
    return sum(device >> i & 1 for i in range(devices.bit_length() - 1)) % 2


def target_of(slot, panel, devices):
    mine, theirs = bits_of(devices)
    chip = jnp.zeros_like(slot)
    for i, (p, q) in enumerate(zip(mine, theirs)):
        chip += (slot >> (len(mine) - 1 - i) & 1) * jnp.where(panel == 0, p, q)
    return chip // 2


def spread(pieces, spread_ref, phases):
    value = sum(r[...] for r in pieces[1:]) + pieces[0][...]
    channels, t = value.shape
    repeat = (iota((channels, LANES), 0) == iota((channels, LANES), 1) % channels).astype(f32).astype(bf16)
    spread_ref[...] = dot(value, repeat, (((0,), (0,)), ((), ())))
    count = t // phases
    phase = iota((count, LANES), 1) // channels
    rows = jnp.zeros((count, LANES), f32)
    for k in range(phases):
        rows = jnp.where(phase == k, spread_ref[pl.ds(k, count, stride=phases), :], rows)
    return rows


def fill_slide(rows_ref, slide_ref):
    span = slide_ref.shape[1]
    for k in range(slide_ref.shape[0]):
        slide_ref[k, :, 0:LANES] = rows_ref[pl.ds(2 * k, span), :].astype(bf16)
        slide_ref[k, :, LANES:] = rows_ref[pl.ds(2 * k + 1, span), :].astype(bf16)


def energies(squares, m, phases):
    n = squares.shape[0]
    channels = LANES // phases
    per = L // phases
    left, right = iota((LANES, LANES), 0) // channels, iota((LANES, LANES), 1) % (2 * phases)
    inside = right < phases
    tail = (inside & (left >= right)).astype(f32).astype(bf16)
    head = (inside & (left < right)).astype(f32).astype(bf16)
    sums = jnp.broadcast_to(jnp.sum(squares, axis=1, keepdims=True), squares.shape)
    distance = iota((m, n), 1) - iota((m, n), 0)
    band = ((distance >= 1) & (distance < per)).astype(f32).astype(bf16)
    begin = pick(squares[per : min(n, per + m)], head)
    if per + m > n:
        begin = jnp.concatenate([begin, jnp.zeros((per + m - n, LANES), f32)], axis=0)
    return pick(squares[:m], tail) + picked(band, sums) + begin


def correlate_tiles(slides, w_ref, acc_ref, tiles, phases):
    versions = w_ref.shape[0]
    channels = LANES // phases
    pairs = (w_ref.shape[1] - LANES) // 256
    m = sum(count for _, count in slides)

    def shifts(q, tile):
        v = tile % versions
        return w_ref[v, pl.ds(LANES + 256 * q - 2 * channels * (tile - v), 256), :]

    for q in range(pairs):
        window = [slide[q % 8, pl.ds(16 * (q // 8), count), :] for slide, count in slides]
        window = window[0] if len(window) == 1 else jnp.concatenate(window, axis=0)
        term = dot(window, jnp.concatenate([shifts(q, tile) for tile in tiles], axis=1))
        if q == 0:
            acc_ref[pl.ds(0, m), :] = term
        else:
            acc_ref[pl.ds(0, m), :] += term


def late_kernel(*refs, phases):
    *pieces, w_ref, out_rows, out_energy, out_slide, out_acc, spread_ref, rows_ref = refs
    rows = spread(pieces, spread_ref, phases)
    count = rows.shape[0]
    out_rows[...] = rows
    rows_ref[pl.ds(0, count), :] = rows
    rows_ref[pl.ds(count, rows_ref.shape[0] - count), :] = jnp.zeros((rows_ref.shape[0] - count, LANES), f32)
    fill_slide(rows_ref, out_slide)
    out_energy[...] = energies(rows * rows, count, phases)
    correlate_tiles([(out_slide, count)], w_ref, out_acc, range(phases // 4), phases)


def write_blocks(send_ref, keep_ref, acc_ref, lead, per, devices):
    me = lax.axis_index("win")
    kept = keep_ref.shape[0]
    for slot in range(2 * kept):
        chip = jnp.bitwise_xor(me // 2, target_of(jnp.int32(slot), panel_of(me, devices), devices))
        at = pl.multiple_of(chip * per, 8)
        ref = keep_ref if slot < kept else send_ref
        for tile in range(acc_ref.shape[1] // LANES):
            ref[slot % kept, tile * per : (tile + 1) * per, :] = acc_ref[
                pl.ds(at, per), tile * LANES : (tile + 1) * LANES
            ]
        if lead is not None:
            ref[slot % kept, LANES:, :] = lead(at)


def early_kernel(*refs, phases, devices):
    *pieces, w_ref, norm_ref, rest_rows, rest_energy, rest_acc = refs[: len(refs) - 7]
    send_ref, keep_ref, slide_ref, rows_ref, spread_ref, energy_ref, acc_ref = refs[len(refs) - 7 :]
    rows = spread(pieces, spread_ref, phases)
    m = rows.shape[0]
    n = m + rest_rows.shape[0]
    rows_ref[pl.ds(0, m), :] = rows
    rows_ref[pl.ds(m, n - m), :] = rest_rows[...]
    fill_slide(rows_ref, slide_ref)
    acc_ref[pl.ds(m, n - m), :] = rest_acc[...]
    correlate_tiles([(slide_ref, m)], w_ref, acc_ref, range(phases // 4), phases)

    squares = rows_ref[...]
    energy_ref[pl.ds(0, m), :] = energies(squares * squares, m, phases)
    energy_ref[pl.ds(m, n - m), :] = rest_energy[...]
    per = L // phases
    place = iota((LANES, LANES), 1)
    wanted = (place // (2 * phases)) * phases + place % (2 * phases) - phases
    scatter = ((place % (2 * phases) >= phases) & (iota((LANES, LANES), 0) == wanted)).astype(f32).astype(bf16)
    norm = pick(norm_ref[...], scatter)
    lane = iota((8, LANES), 1)

    def extras(at):
        e = norm
        for k in range(per // 8):
            e = jnp.where(
                (lane // (2 * phases) == k) & (lane % (2 * phases) < phases), energy_ref[pl.ds(at + 8 * k, 8), :], e
            )
        return e

    write_blocks(send_ref, keep_ref, acc_ref, extras, per, devices)


def rest_kernel(early_slide, late_slide, w_ref, send_ref, keep_ref, acc_ref, *, rows, phases, devices):
    slides = list(zip((early_slide, late_slide), rows))
    correlate_tiles(slides, w_ref, acc_ref, range(phases // 4, phases // 2), phases)
    write_blocks(send_ref, keep_ref, acc_ref, None, L // phases, devices)


def grant(shapes):
    return pltpu.CompilerParams(vmem_limit_bytes=sum(math.prod(s.shape) * 4 for s in shapes) + SPARE)


def slide_shape(m, phases):
    pairs = (L // phases + 2) // 2
    return (min(8, pairs), m + 16 * ((pairs - 1) // 8), 256)


def correlate_late(pieces, w, phases):
    t = pieces[0].shape[1]
    count = t // phases
    slide = slide_shape(count, phases)
    shapes = [pltpu.VMEM((t, LANES), f32), pltpu.VMEM((slide[1] + 16, LANES), f32)]
    return pl.pallas_call(
        lambda *refs: late_kernel(*refs, phases=phases),
        out_shape=(
            jax.ShapeDtypeStruct((count, LANES), f32),
            jax.ShapeDtypeStruct((count, LANES), f32),
            jax.ShapeDtypeStruct(slide, bf16),
            jax.ShapeDtypeStruct((count, phases * 32), f32),
        ),
        in_specs=[IN_VMEM] * (len(pieces) + 1),
        out_specs=(IN_VMEM,) * 4,
        scratch_shapes=shapes,
        compiler_params=grant(shapes),
        cost_estimate=pl.CostEstimate(flops=2**31, bytes_accessed=2**22, transcendentals=0),
        name="correlate_late",
    )(*pieces, w)


def correlate_early(pieces, w, norm, rest, phases, devices):
    t = pieces[0].shape[1]
    m = t // phases
    n = m + rest[0].shape[0]
    shapes = [
        pltpu.VMEM((n, LANES), f32),
        pltpu.VMEM((t, LANES), f32),
        pltpu.VMEM((n, LANES), f32),
        pltpu.VMEM((n, phases * 32), f32),
    ]
    block = jax.ShapeDtypeStruct((devices // 4, LANES + 8, LANES), f32)
    return pl.pallas_call(
        lambda *refs: early_kernel(*refs, phases=phases, devices=devices),
        out_shape=(block, block, jax.ShapeDtypeStruct(slide_shape(m, phases), bf16)),
        in_specs=[IN_VMEM] * (len(pieces) + 5),
        out_specs=(IN_VMEM,) * 3,
        scratch_shapes=shapes,
        compiler_params=grant(shapes),
        cost_estimate=pl.CostEstimate(flops=2**32, bytes_accessed=2**24, transcendentals=0),
        name="correlate_early",
    )(*pieces, w, norm, *rest)


def correlate_rest(early_slide, late_slide, w, rows, phases, devices):
    shapes = [pltpu.VMEM((sum(rows), phases * 32), f32)]
    block = jax.ShapeDtypeStruct((devices // 4, LANES, LANES), f32)
    return pl.pallas_call(
        lambda *refs: rest_kernel(*refs, rows=rows, phases=phases, devices=devices),
        out_shape=(block, block),
        in_specs=[IN_VMEM] * 3,
        out_specs=(IN_VMEM, IN_VMEM),
        scratch_shapes=shapes,
        compiler_params=grant(shapes),
        cost_estimate=pl.CostEstimate(flops=2**33, bytes_accessed=2**24, transcendentals=0),
        name="correlate_rest",
    )(early_slide, late_slide, w)


def cut(block, phases):
    per = L // phases
    half = per // 2
    starts = range(0, LANES, per)
    return (
        jnp.concatenate([block[at : at + half] for at in starts], axis=0),
        jnp.concatenate([block[at + half : at + per] for at in starts], axis=0),
    )


def halves_kernel(kept_ref, got_ref, mine_ref, other_ref, *, phases):
    first = lax.axis_index("win") % 2 == 0
    block = kept_ref[0] + got_ref[0]
    lower, upper = cut(block, phases)
    rows = LANES // 2
    mine_ref[0:rows] = jnp.where(first, lower, upper)
    other_ref[0:rows] = jnp.where(first, upper, lower)
    if block.shape[0] > LANES:
        mine_ref[rows:] = block[LANES:]
        other_ref[rows:] = block[LANES:]


def halves(kept, got, phases):
    half = jax.ShapeDtypeStruct((kept.shape[1] - LANES // 2, LANES), f32)
    return pl.pallas_call(
        lambda *refs: halves_kernel(*refs, phases=phases),
        out_shape=(half, half),
        in_specs=[IN_VMEM, IN_VMEM],
        out_specs=(IN_VMEM, IN_VMEM),
        compiler_params=SMALL,
        cost_estimate=pl.CostEstimate(flops=2**32, bytes_accessed=2**20, transcendentals=0),
        name="halves",
    )(kept, got)


def woven(straight, mine, got):
    groups = LANES // 2
    low = iota(mine.shape, 1) < groups
    zero, one = jnp.where(straight, mine, got), jnp.where(straight, got, mine)
    return jnp.where(low, zero, pltpu.roll(one, groups, 1)), jnp.where(low, pltpu.roll(zero, groups, 1), one)


def scale_kernel(mine_ref, got_ref, even_ref, odd_ref, mine_scale, got_scale, *, phases, devices):
    groups = LANES // 2
    per = L // phases
    half = per // 2
    tiles = phases // 4
    me = lax.axis_index("win")
    first = me % 2 == 0
    straight = panel_of(me, devices) == 0
    place = iota((LANES, LANES), 0)
    wanted = (place // (2 * phases)) * phases + place % (2 * phases) - phases
    gather = (
        ((place % (2 * phases) >= phases) & (iota((LANES, LANES), 1) % groups == wanted)).astype(f32).astype(bf16)
    )
    low = iota((half, LANES), 1) < groups
    sides = []
    for ref in (mine_ref, got_ref):
        extra = ref[groups:]
        norm = math.sqrt(CT * L) * lax.rsqrt(pick(extra, gather))[:1]
        scale = lax.rsqrt(extra + epsilon)
        scales = []
        for tile in range(2 * tiles):
            columns = []
            for phase in (2 * tile, 2 * tile + 1):
                if half >= 8:
                    count = half // 8
                    pieces = [scale[:, 2 * phases * k + phase :][:, :1] for k in range(2 * count)]
                    columns.append(
                        jnp.concatenate(
                            [jnp.where(first, pieces[k], pieces[k + count]) for k in range(count)], axis=0
                        )
                    )
                else:
                    columns.append(
                        jnp.where(first, scale[:half, phase : phase + 1], scale[half : 2 * half, phase : phase + 1])
                    )
            scales.append(jnp.where(low, columns[0], columns[1]) * norm)
        sides.append(scales)
    for tile in range(tiles):
        rows = slice(tile * half, (tile + 1) * half)
        mine_scale[rows] = sides[0][tiles + tile]
        got_scale[rows] = sides[1][tiles + tile]
        even_ref[rows], odd_ref[rows] = woven(
            straight, mine_ref[rows] * sides[0][tile], got_ref[rows] * sides[1][tile]
        )


def scaled(mine, got, phases, devices):
    half = jax.ShapeDtypeStruct((LANES // 2, LANES), f32)
    return pl.pallas_call(
        lambda *refs: scale_kernel(*refs, phases=phases, devices=devices),
        out_shape=(half,) * 4,
        in_specs=[IN_VMEM, IN_VMEM],
        out_specs=(IN_VMEM,) * 4,
        compiler_params=SMALL,
        cost_estimate=pl.CostEstimate(flops=2**32, bytes_accessed=2**18, transcendentals=0),
        name="scale",
    )(mine, got)


def finish_kernel(even_ref, odd_ref, mine_scale, got_scale, mine_ref, got_ref, out_ref, *, phases, devices):
    half = L // phases // 2
    tiles = phases // 4
    straight = panel_of(lax.axis_index("win"), devices) == 0
    mine = mine_ref[...] * mine_scale[...]
    got = got_ref[...] * got_scale[...]
    even, odd = woven(straight, mine, got)
    for tile in range(tiles):
        rows = slice(tile * half, (tile + 1) * half)
        for phase, value in enumerate((even_ref[rows], odd_ref[rows])):
            out_ref[pl.ds(2 * tile + phase, half, stride=phases), :] = value
        for phase, value in enumerate((even[rows], odd[rows])):
            out_ref[pl.ds(2 * (tiles + tile) + phase, half, stride=phases), :] = value


def finish(first, second, phases, devices):
    return pl.pallas_call(
        lambda *refs: finish_kernel(*refs, phases=phases, devices=devices),
        out_shape=jax.ShapeDtypeStruct((L // 2, LANES), f32),
        in_specs=[IN_VMEM] * 6,
        out_specs=IN_VMEM,
        compiler_params=SMALL,
        cost_estimate=pl.CostEstimate(flops=2**18, bytes_accessed=2**18, transcendentals=0),
        name="finish",
    )(*first, *second)


def masks_kernel(start_hbm, routed_ref, start_ref, sem, *, devices):
    copy = pltpu.make_async_copy(start_hbm, start_ref, sem)
    copy.start()
    held = routed_ref.shape[1]
    me = lax.axis_index("win")
    mine = panel_of(me, devices)
    per_chip = 2 * CT // devices
    row = iota((CT, held), 0)
    panels = (1 - mine, mine)
    channels = []
    for panel in panels:
        target = jnp.bitwise_xor(target_of(row // per_chip, panel, devices), me // 2)
        core = jnp.bitwise_xor(panel, panel_of(2 * target, devices))
        channel = target * per_chip + (row % per_chip + per_chip // 2 * core) % per_chip
        channels.append(channel - me * held - iota((CT, held), 1))
    copy.wait()
    for i, panel in enumerate(panels):
        routed_ref[i * CT : (i + 1) * CT] = (channels[i] + start_ref[panel] == 0).astype(f32).astype(bf16)


def masks(panel_start, held, devices):
    return pl.pallas_call(
        lambda *refs: masks_kernel(*refs, devices=devices),
        out_shape=jax.ShapeDtypeStruct((2 * CT, held), bf16),
        in_specs=[pl.BlockSpec(memory_space=pltpu.HBM)],
        out_specs=IN_VMEM,
        scratch_shapes=[pltpu.SMEM(panel_start.shape, jnp.int32), pltpu.SemaphoreType.DMA],
        compiler_params=SMALL,
        cost_estimate=pl.CostEstimate(flops=2**31, bytes_accessed=2**16, transcendentals=0),
        name="masks",
    )(panel_start)


def select_kernel(records_ref, routed_ref, away_ref, home_ref, *, begin):
    both = dot(routed_ref[...], records_ref[:, begin : begin + away_ref.shape[1]]).astype(bf16)
    away_ref[...] = both[:CT]
    home_ref[...] = both[CT:]


def selected(records, routed, begin, end):
    out = jax.ShapeDtypeStruct((CT, end - begin), bf16)
    return pl.pallas_call(
        lambda *refs: select_kernel(*refs, begin=begin),
        out_shape=(out, out),
        in_specs=[IN_VMEM, IN_VMEM],
        out_specs=(IN_VMEM, IN_VMEM),
        compiler_params=pltpu.CompilerParams(vmem_limit_bytes=SPARE),
        cost_estimate=pl.CostEstimate(flops=2**27, bytes_accessed=2**21, transcendentals=0),
        name="select",
    )(records, routed)


def add_kernel(kept_ref, got_ref, *refs):
    keep_ref, send_ref = refs[-2:]
    half = keep_ref.shape[0]
    keep_ref[...] = kept_ref[:half] + got_ref[:half]
    send_ref[...] = kept_ref[half:] + got_ref[half:]


def added(kept, got, *before):
    half = kept.shape[0] // 2
    if kept.dtype == bf16 and half % 16:
        whole = kept + got
        return whole[:half], whole[half:]
    part = jax.ShapeDtypeStruct((half, *kept.shape[1:]), kept.dtype)
    return pl.pallas_call(
        add_kernel,
        out_shape=(part, part),
        in_specs=[IN_VMEM, IN_VMEM] + [pl.BlockSpec(memory_space=pl.ANY)] * len(before),
        out_specs=(IN_VMEM, IN_VMEM),
        compiler_params=SMALL,
        cost_estimate=pl.CostEstimate(flops=2**32, bytes_accessed=2**20, transcendentals=0),
        name="add",
    )(kept, got, *before)


def local(records, templates, panel_start):
    devices = lax.axis_size("win")
    panel = panel_of(lax.axis_index("win"), devices)
    phases = devices // 2
    pairs = (L // phases + 2) // 2
    orders = bits_of(devices)
    steps = len(orders[0])

    def sibling(value):
        return lax.ppermute(value, "win", [(d, d ^ 1) for d in range(devices)])

    def exchange(value, step):
        return lax.ppermute(value, "win", [(d, d ^ 1 ^ orders[panel_of(d, devices)][step]) for d in range(devices)])

    def scattered(keep, send, until, before=()):
        for step in range(until - 1):
            keep, send = added(keep, exchange(send, step), *(before if step == 0 else ()))
        return keep, exchange(send, until - 1)

    half = records.shape[1] // 2
    routed = masks(panel_start, records.shape[0], devices)
    away_late, home_late = selected(records, routed, half, 2 * half)
    got_late = sibling(away_late)
    away_early, home_early = selected(records, routed, 0, half)
    got_early = sibling(away_early)

    keep, send = added(home_late, got_late)
    late = keep, send
    got_early, templates = lax.optimization_barrier((got_early, templates))
    early = added(home_early, got_early, keep)
    given = lax.dynamic_index_in_dim(templates, 1 - panel, 0, keepdims=False)
    w, norm = shifted(templates, sibling(given), phases, pairs)
    late = scattered(*late, steps)
    early = scattered(*early, steps, [norm])
    rest_rows, rest_energy, late_slide, rest_acc = correlate_late(late, w, phases)
    send_a, keep_a, early_slide = correlate_early(early, w, norm, (rest_rows, rest_energy, rest_acc), phases, devices)
    rows = [piece[0].shape[1] // phases for piece in (early, late)]
    send_b, keep_b = correlate_rest(early_slide, late_slide, w, rows, phases, devices)

    mine, other = halves(*scattered(keep_a, send_a, steps, [send_b]), phases)
    first = scaled(mine, sibling(other), phases, devices)
    mine, other = halves(*scattered(keep_b, send_b, steps), phases)
    return finish(first, (mine, sibling(other)), phases, devices)


def solution(mesh):
    placed = (P("win", "parts"), P(None, None, "win", None), P("parts"))
    return jax.shard_map(
        local, mesh=mesh, in_specs=placed, out_specs=P(("parts", "win"), None), check_vma=False
    )
```

time: 55.2 us -> 52 us (0.942); the launches traced: 54.2 us -> 51.8 us
  waiting for transfers between devices: 11.1 us -> 18.1 us
  starting transfers between devices: 27.1 us -> 20.9 us
  local copies, waits for them, and re-layouts: 3.15 us -> 0.79 us
  Pallas kernels: 12.7 us -> 11.9 us
    ppermute x12, starting transfers between devices: 25.9 us -> 18.8 us  [exchange(): lax.ppermute(value, 'win', [(d, d ^ 1 ^ orders[panel_of(d, devices)][step...]
    ppermute x12, waiting for transfers between devices: 9.88 us -> 16.3 us  [exchange(): lax.ppermute(value, 'win', [(d, d ^ 1 ^ orders[panel_of(d, devices)][step...]
    squeeze x1, local copies, waits for them, and re-layouts: 1.27 us -> 0.03 us  [local(): given = lax.dynamic_index_in_dim(templates, 1 - panel, 0, keepdims=False)]
    pallas_call x1, Pallas kernels: 3.26 us -> 2.11 us  [correlate_late(): pl.pallas_call(lambda *refs: late_kernel(*refs, phases=phases), out_shape...]
    unnamed x8 -> x6, local copies, waits for them, and re-layouts: 1.89 us -> 0.75 us
    ppermute x4 -> x5, starting transfers between devices: 1.16 us -> 2.06 us  [sibling(): return lax.ppermute(value, 'win', [(d, d ^ 1) for d in range(devices)])]
    ppermute x4 -> x5, waiting for transfers between devices: 1.25 us -> 1.75 us  [sibling(): return lax.ppermute(value, 'win', [(d, d ^ 1) for d in range(devices)])]
    pallas_call x6 -> x8, Pallas kernels: 6.22 us -> 6.45 us  [the longest x1 2.43 us: correlate_rest(): pl.pallas_call(lambda *refs: rest_kernel(*refs, rows=rows, phases=phases,...]
  transfers between devices with their start and end apart: 16 -> 17, of which waited for: 8 -> 11; matrix products, arithmetic and copies ran while one was open for 2% -> 0% of each run, Pallas kernels for 16% -> 15%
where the time goes in v3:
time: 52 us; the launch traced here: 51.8 us
  starting transfers between devices  20.9 us (40%)
  waiting for transfers between devices  18.1 us (35%)
  Pallas kernels  11.9 us (23%)
  local copies, waits for them, and re-layouts  0.79 us (2%)
    ppermute x12, starting transfers between devices, exchange(): lax.ppermute(value, 'win', [(d, d ^ 1 ^ orders[panel_of(d, devices)][step...  18.8 us
    ppermute x12, waiting for transfers between devices, exchange(): lax.ppermute(value, 'win', [(d, d ^ 1 ^ orders[panel_of(d, devices)][step...  16.3 us
    pallas_call x1, Pallas kernels, correlate_rest(): pl.pallas_call(lambda *refs: rest_kernel(*refs, rows=rows, phases=phases,...  2.43 us
    pallas_call x1, Pallas kernels, correlate_early(): pl.pallas_call(lambda *refs: early_kernel(*refs, phases=phases, devices=d...  2.32 us
    pallas_call x1, Pallas kernels, shifted(): pl.pallas_call(lambda *refs: shift_kernel(*refs, phases=phases, devices=2...  2.26 us
    pallas_call x1, Pallas kernels, correlate_late(): pl.pallas_call(lambda *refs: late_kernel(*refs, phases=phases), out_shape...  2.11 us
    ppermute x5, starting transfers between devices, sibling(): return lax.ppermute(value, 'win', [(d, d ^ 1) for d in range(devices)])  2.06 us
    ppermute x5, waiting for transfers between devices, sibling(): return lax.ppermute(value, 'win', [(d, d ^ 1) for d in range(devices)])  1.75 us
  transfers between devices with their start and end apart: 17, of which 11 were waited for; matrix products, arithmetic and copies ran while one was open for 0% of the time, Pallas kernels for 15%

profile of v3, /device:TPU:0, one launch (start us, length us, event | category | flops | bytes accessed | tf_op | source)
XLA Modules:
  0.0 51.8 jit_solution(6811554362729157465)
XLA Ops:
  0.0 0.7 %copy-done.2 = s32[2]{0:T(128)S(1)} copy-done((s32[2]{0:T(128)S(1)}, s32[2]{0:T(128)}, u32[]{:S(2)}) %copy-start.2) | copy-done | bytes 32
  0.7 0.6 %masks.1.refs_1_ = bf16[256,128]{1,0:T(8,128)(2,1)S(1)} custom-call(s32[2]{0:T(128)S(1)} %copy-done.2), custom_call_target="tpu_custom_call" | custom-call | flops 2147483648 | bytes 65536 | tf_op jit(solution)/shard_map/masks/pallas_call | solution.py:457
  1.3 0.0 copy-done
  1.3 0.4 select.5
  1.8 0.5 %collective-permute-start.1 = (bf16[128,2048]{1,0:T(8,128)(2,1)S(1)}, bf16[128,2048]{1,0:T(8,128)(2,1)S(1)}, u32[]{:S(2)}, u32[]{:S(2)}) collective-permute-start(bf16[128,2048]{1,0:T(8,128)(2,1)S(1)} %get-tuple-element.54), channel_id=1, source_target_pairs={{0,1},{1,0},{2,3},{3,2},{4,5},{5,4},{6,7},{7,6},{8,9},{9,8},{10,11... | collective-permute-start | bytes 1572872 | tf_op jit(solution)/shard_map/ppermute | solution.py:521
  2.3 0.4 select.4
  2.7 0.1 collective-permute-start
  2.8 1.0 %collective-permute-done.1.got_ref = bf16[128,2048]{1,0:T(8,128)(2,1)S(1)} collective-permute-done((bf16[128,2048]{1,0:T(8,128)(2,1)S(1)}, bf16[128,2048]{1,0:T(8,128)(2,1)S(1)}, u32[]{:S(2)}, u32[]{:S(2)}) %collective-permute-start.1) | collective-permute-done | bytes 524320 | tf_op jit(solution)/shard_map/ppermute | solution.py:521
  3.8 0.1 add.33
  3.9 2.7 %collective-permute-start.6 = (bf16[64,2048]{1,0:T(8,128)(2,1)S(1)}, bf16[64,2048]{1,0:T(8,128)(2,1)S(1)}, u32[]{:S(2)}, u32[]{:S(2)}) collective-permute-start(bf16[64,2048]{1,0:T(8,128)(2,1)S(1)} %get-tuple-element.65), channel_id=1, source_target_pairs={{0,3},{1,4},{2,7},{3,0},{4,1},{5,6},{6,5},{7,2},{8,13},{9,10},{10,... | collective-permute-start | bytes 786440 | tf_op jit(solution)/shard_map/ppermute | solution.py:524
  6.5 0.0 collective-permute-done.got_ref
  6.5 0.0 copy-done.1
  6.6 0.5 collective-permute-start.3
  7.1 0.1 add.34
  7.2 1.3 %collective-permute-start.2 = (bf16[64,2048]{1,0:T(8,128)(2,1)S(1)}, bf16[64,2048]{1,0:T(8,128)(2,1)S(1)}, u32[]{:S(2)}, u32[]{:S(2)}) collective-permute-start(bf16[64,2048]{1,0:T(8,128)(2,1)S(1)} %get-tuple-element.57), channel_id=1, source_target_pairs={{0,3},{1,4},{2,7},{3,0},{4,1},{5,6},{6,5},{7,2},{8,13},{9,10},{10,... | collective-permute-start | bytes 786440 | tf_op jit(solution)/shard_map/ppermute | solution.py:524
  8.5 2.1 %collective-permute-done.6.got_ref = bf16[64,2048]{1,0:T(8,128)(2,1)S(1)} collective-permute-done((bf16[64,2048]{1,0:T(8,128)(2,1)S(1)}, bf16[64,2048]{1,0:T(8,128)(2,1)S(1)}, u32[]{:S(2)}, u32[]{:S(2)}) %collective-permute-start.6) | collective-permute-done | bytes 262176 | tf_op jit(solution)/shard_map/ppermute | solution.py:524
  10.6 2.2 %collective-permute-start.7 = (bf16[32,2048]{1,0:T(8,128)(2,1)S(1)}, bf16[32,2048]{1,0:T(8,128)(2,1)S(1)}, u32[]{:S(2)}, u32[]{:S(2)}) collective-permute-start(bf16[32,2048]{1,0:T(8,128)(2,1)S(1)} %get-tuple-element.67), channel_id=1, source_target_pairs={{0,5},{1,2},{2,1},{3,6},{4,7},{5,0},{6,3},{7,4},{8,11},{9,12},{10,... | collective-permute-start | bytes 393224 | tf_op jit(solution)/shard_map/ppermute | solution.py:524
  12.8 0.0 collective-permute-done.3
  12.8 2.3 %shift_templates.1 = (bf16[1,8576,128]{2,1,0:T(8,128)(2,1)S(1)}, f32[8,128]{1,0:T(8,128)S(1)}) custom-call(bf16[2,512,512]{2,1,0:T(8,128)(2,1)S(1)} %bitcast.4, bf16[512,512]{1,0:T(8,128)(2,1)S(1)} %bitcast.5), custom_call_target="tpu_custom_call" | custom-call | flops 1073741824 | bytes 16777216 | tf_op jit(solution)/shard_map/shift_templates/pallas_call | solution.py:86
  15.1 0.0 collective-permute-done.2.got_ref
  15.1 0.2 collective-permute-start.4
  15.3 0.1 collective-permute-done.7.got_ref
  15.5 2.8 %collective-permute-start.8 = (bf16[16,2048]{1,0:T(8,128)(2,1)S(1)}, bf16[16,2048]{1,0:T(8,128)(2,1)S(1)}, u32[]{:S(2)}, u32[]{:S(2)}) collective-permute-start(bf16[16,2048]{1,0:T(8,128)(2,1)S(1)} %get-tuple-element.69), channel_id=1, source_target_pairs={{0,9},{1,8},{2,11},{3,10},{4,13},{5,12},{6,15},{7,14},{8,1},{9,0},... | collective-permute-start | bytes 196616 | tf_op jit(solution)/shard_map/ppermute | solution.py:524
  18.3 1.3 %collective-permute-done.4.got_ref = bf16[32,2048]{1,0:T(8,128)(2,1)S(1)} collective-permute-done((bf16[32,2048]{1,0:T(8,128)(2,1)S(1)}, bf16[32,2048]{1,0:T(8,128)(2,1)S(1)}, u32[]{:S(2)}, u32[]{:S(2)}) %collective-permute-start.4) | collective-permute-done | bytes 131104 | tf_op jit(solution)/shard_map/ppermute | solution.py:524
  19.6 3.3 %collective-permute-start.5 = (bf16[16,2048]{1,0:T(8,128)(2,1)S(1)}, bf16[16,2048]{1,0:T(8,128)(2,1)S(1)}, u32[]{:S(2)}, u32[]{:S(2)}) collective-permute-start(bf16[16,2048]{1,0:T(8,128)(2,1)S(1)} %get-tuple-element.63), channel_id=1, source_target_pairs={{0,9},{1,8},{2,11},{3,10},{4,13},{5,12},{6,15},{7,14},{8,1},{9,0},... | collective-permute-start | bytes 196616 | tf_op jit(solution)/shard_map/ppermute | solution.py:524
  22.9 0.0 collective-permute-done.8.refs_1_
  23.0 2.1 %correlate_late.1 = (f32[256,128]{1,0:T(8,128)S(1)}, f32[256,128]{1,0:T(8,128)S(1)}, bf16[8,320,256]{2,1,0:T(8,128)(2,1)S(1)}, f32[256,256]{1,0:T(8,128)S(1)}) custom-call(bf16[16,2048]{1,0:T(8,128)(2,1)S(1)} %get-tuple-element.68.refs_0_, bf16[16,2048]{1,0:T(8,128)(2,1)S(1)} %collective-permute-done.8.refs_1_, ...), custom_call_target="tpu_custom_call" | custom-call | flops 2147483648 | bytes 4194304 | tf_op jit(solution)/shard_map/correlate_late/pallas_call | solution.py:253
  25.1 1.7 %collective-permute-done.5.refs_1_ = bf16[16,2048]{1,0:T(8,128)(2,1)S(1)} collective-permute-done((bf16[16,2048]{1,0:T(8,128)(2,1)S(1)}, bf16[16,2048]{1,0:T(8,128)(2,1)S(1)}, u32[]{:S(2)}, u32[]{:S(2)}) %collective-permute-start.5) | collective-permute-done | bytes 65568 | tf_op jit(solution)/shard_map/ppermute | solution.py:524
  26.8 2.3 %correlate_early.1 = (f32[4,136,128]{2,1,0:T(8,128)S(1)}, f32[4,136,128]{2,1,0:T(8,128)S(1)}, bf16[8,320,256]{2,1,0:T(8,128)(2,1)S(1)}) custom-call(bf16[16,2048]{1,0:T(8,128)(2,1)S(1)} %get-tuple-element.62.refs_0_, bf16[16,2048]{1,0:T(8,128)(2,1)S(1)} %collective-permute-done.5.refs_1_, bf16[1,8576,128]{2,1,0:T(8,128)(2,1)S(1)} %get-tuple-element.64.refs_2_, ...), custom_call_target="tpu_custom_call" | custom-call | flops 4294967296 | bytes 16777216 | tf_op jit(solution)/shard_map/correlate_early/pallas_call | solution.py:281
  29.1 0.1 collective-permute-start.9
  29.2 2.4 %correlate_rest.1 = (f32[4,128,128]{2,1,0:T(8,128)S(1)}, f32[4,128,128]{2,1,0:T(8,128)S(1)}) custom-call(bf16[8,320,256]{2,1,0:T(8,128)(2,1)S(1)} %get-tuple-element.75.refs_0_, bf16[8,320,256]{2,1,0:T(8,128)(2,1)S(1)} %get-tuple-element.76.refs_1_, bf16[1,8576,128]{2,1,0:T(8,128)(2,1)S(1)} %get-tuple-element.64.refs_2_), custom_call_target="tpu_custom_call" | custom-call | flops 8589934592 | bytes 16777216 | tf_op jit(solution)/shard_map/correlate_rest/pallas_call | solution.py:296
  31.7 1.8 %collective-permute-start.13 = (f32[4,128,128]{2,1,0:T(8,128)S(1)}, f32[4,128,128]{2,1,0:T(8,128)S(1)}, u32[]{:S(2)}, u32[]{:S(2)}) collective-permute-start(f32[4,128,128]{2,1,0:T(8,128)S(1)} %get-tuple-element.77.refs_0_), channel_id=1, source_target_pairs={{0,3},{1,4},{2,7},{3,0},{4,1},{5,6},{6,5},{7,2},{8,13},{9,10},{10,... | collective-permute-start | bytes 786440 | tf_op jit(solution)/shard_map/ppermute | solution.py:524
  33.4 1.7 %collective-permute-done.9.got_ref = f32[4,136,128]{2,1,0:T(8,128)S(1)} collective-permute-done((f32[4,136,128]{2,1,0:T(8,128)S(1)}, f32[4,136,128]{2,1,0:T(8,128)S(1)}, u32[]{:S(2)}, u32[]{:S(2)}) %collective-permute-start.9) | collective-permute-done | bytes 278560 | tf_op jit(solution)/shard_map/ppermute | solution.py:524
  35.2 0.1 collective-permute-start.10
  35.3 3.3 %collective-permute-done.13.got_ref = f32[4,128,128]{2,1,0:T(8,128)S(1)} collective-permute-done((f32[4,128,128]{2,1,0:T(8,128)S(1)}, f32[4,128,128]{2,1,0:T(8,128)S(1)}, u32[]{:S(2)}, u32[]{:S(2)}) %collective-permute-start.13) | collective-permute-done | bytes 262176 | tf_op jit(solution)/shard_map/ppermute | solution.py:524
  38.6 0.1 collective-permute-start.14
  38.7 1.0 %collective-permute-done.10.got_ref = f32[2,136,128]{2,1,0:T(8,128)S(1)} collective-permute-done((f32[2,136,128]{2,1,0:T(8,128)S(1)}, f32[2,136,128]{2,1,0:T(8,128)S(1)}, u32[]{:S(2)}, u32[]{:S(2)}) %collective-permute-start.10) | collective-permute-done | bytes 139296 | tf_op jit(solution)/shard_map/ppermute | solution.py:524
  39.8 1.6 %collective-permute-start.11 = (f32[1,136,128]{2,1,0:T(8,128)S(1)}, f32[1,136,128]{2,1,0:T(8,128)S(1)}, u32[]{:S(2)}, u32[]{:S(2)}) collective-permute-start(f32[1,136,128]{2,1,0:T(8,128)S(1)} %get-tuple-element.81), channel_id=1, source_target_pairs={{0,9},{1,8},{2,11},{3,10},{4,13},{5,12},{6,15},{7,14},{8,1},{9,0},... | collective-permute-start | bytes 208904 | tf_op jit(solution)/shard_map/ppermute | solution.py:524
  41.4 1.7 %collective-permute-done.14.got_ref = f32[2,128,128]{2,1,0:T(8,128)S(1)} collective-permute-done((f32[2,128,128]{2,1,0:T(8,128)S(1)}, f32[2,128,128]{2,1,0:T(8,128)S(1)}, u32[]{:S(2)}, u32[]{:S(2)}) %collective-permute-start.14) | collective-permute-done | bytes 131104 | tf_op jit(solution)/shard_map/ppermute | solution.py:524
  43.1 2.7 %collective-permute-start.15 = (f32[1,128,128]{2,1,0:T(8,128)S(1)}, f32[1,128,128]{2,1,0:T(8,128)S(1)}, u32[]{:S(2)}, u32[]{:S(2)}) collective-permute-start(f32[1,128,128]{2,1,0:T(8,128)S(1)} %get-tuple-element.92), channel_id=1, source_target_pairs={{0,9},{1,8},{2,11},{3,10},{4,13},{5,12},{6,15},{7,14},{8,1},{9,0},... | collective-permute-start | bytes 196616 | tf_op jit(solution)/shard_map/ppermute | solution.py:524
  45.7 0.0 collective-permute-done.11.refs_1_
  45.8 0.7 %collective-permute-start.12 = (f32[72,128]{1,0:T(8,128)S(1)}, f32[72,128]{1,0:T(8,128)S(1)}, u32[]{:S(2)}, u32[]{:S(2)}) collective-permute-start(f32[72,128]{1,0:T(8,128)S(1)} %get-tuple-element.83), channel_id=1, source_target_pairs={{0,1},{1,0},{2,3},{3,2},{4,5},{5,4},{6,7},{7,6},{8,9},{9,8},{10,11... | collective-permute-start | bytes 110600 | tf_op jit(solution)/shard_map/ppermute | solution.py:521
  46.5 3.3 %collective-permute-done.15.refs_1_ = f32[1,128,128]{2,1,0:T(8,128)S(1)} collective-permute-done((f32[1,128,128]{2,1,0:T(8,128)S(1)}, f32[1,128,128]{2,1,0:T(8,128)S(1)}, u32[]{:S(2)}, u32[]{:S(2)}) %collective-permute-start.15) | collective-permute-done | bytes 65568 | tf_op jit(solution)/shard_map/ppermute | solution.py:524
  49.8 0.2 collective-permute-start.16
  50.0 0.0 collective-permute-done.12.refs_1_
  50.0 0.3 scale.1
  50.3 0.7 %collective-permute-done.16.refs_5_ = f32[64,128]{1,0:T(8,128)S(1)} collective-permute-done((f32[64,128]{1,0:T(8,128)S(1)}, f32[64,128]{1,0:T(8,128)S(1)}, u32[]{:S(2)}, u32[]{:S(2)}) %collective-permute-start.16) | collective-permute-done | bytes 32800 | tf_op jit(solution)/shard_map/ppermute | solution.py:521
  51.1 0.8 %finish.1 = f32[256,128]{1,0:T(8,128)} custom-call(f32[64,128]{1,0:T(8,128)S(1)} %get-tuple-element.84.refs_0_, f32[64,128]{1,0:T(8,128)S(1)} %get-tuple-element.85.refs_1_, f32[64,128]{1,0:T(8,128)S(1)} %get-tuple-element.86.refs_2_, f32[64,128]{1,0:T(8,128)S(1)} %get-tuple-element.87.refs_3_, f32[64,128]{1,0:T(8,128)S(1)} %get-tuple-element.93.refs_4_, ...), custom_call_target="tpu_custom_call" | custom-call | flops 262144 | bytes 262144 | tf_op jit(solution)/shard_map/finish/pallas_call | solution.py:425
  (14 shorter events, 0.2 us)
Async XLA Ops:
  0.0 1.3 %copy-start = (bf16[128,4096]{1,0:T(8,128)(2,1)S(1)}, bf16[128,4096]{1,0:T(8,128)(2,1)}, u32[]{:S(2)}) copy-start(bf16[128,4096]{1,0:T(8,128)(2,1)} %refs_0_.5) | copy-start | bytes 3145732
  0.0 0.7 %copy-start.2 = (s32[2]{0:T(128)S(1)}, s32[2]{0:T(128)}, u32[]{:S(2)}) copy-start(s32[2]{0:T(128)} %refs_0_.3) | copy-start | bytes 28
  1.8 2.1 %collective-permute-start.1 = (bf16[128,2048]{1,0:T(8,128)(2,1)S(1)}, bf16[128,2048]{1,0:T(8,128)(2,1)S(1)}, u32[]{:S(2)}, u32[]{:S(2)}) collective-permute-start(bf16[128,2048]{1,0:T(8,128)(2,1)S(1)} %get-tuple-element.54), channel_id=1, source_target_pairs={{0,1},{1,0},{2,3},{3,2},{4,5},{5,4},{6,7},{7,6},{8,9},{9,8},{10,11... | collective-permute-start | bytes 1572872 | tf_op jit(solution)/shard_map/ppermute | solution.py:521
  2.7 3.8 %collective-permute-start = (bf16[128,2048]{1,0:T(8,128)(2,1)S(1)}, bf16[128,2048]{1,0:T(8,128)(2,1)S(1)}, u32[]{:S(2)}, u32[]{:S(2)}) collective-permute-start(bf16[128,2048]{1,0:T(8,128)(2,1)S(1)} %get-tuple-element.51), channel_id=1, source_target_pairs={{0,1},{1,0},{2,3},{3,2},{4,5},{5,4},{6,7},{7,6},{8,9},{9,8},{10,11... | collective-permute-start | bytes 1572872 | tf_op jit(solution)/shard_map/ppermute | solution.py:521
  3.8 2.7 %copy-start.1 = (bf16[2,64,8,512]{3,2,1,0:T(8,128)(2,1)S(1)}, bf16[2,64,8,512]{3,2,1,0:T(8,128)(2,1)}, u32[]{:S(2)}) copy-start(bf16[2,64,8,512]{3,2,1,0:T(8,128)(2,1)} %param.4) | copy-start | bytes 3145732
  3.9 6.7 %collective-permute-start.6 = (bf16[64,2048]{1,0:T(8,128)(2,1)S(1)}, bf16[64,2048]{1,0:T(8,128)(2,1)S(1)}, u32[]{:S(2)}, u32[]{:S(2)}) collective-permute-start(bf16[64,2048]{1,0:T(8,128)(2,1)S(1)} %get-tuple-element.65), channel_id=1, source_target_pairs={{0,3},{1,4},{2,7},{3,0},{4,1},{5,6},{6,5},{7,2},{8,13},{9,10},{10,... | collective-permute-start | bytes 786440 | tf_op jit(solution)/shard_map/ppermute | solution.py:524
  6.6 6.2 %collective-permute-start.3 = (bf16[64,8,512]{2,1,0:T(8,128)(2,1)S(1)}, bf16[64,8,512]{2,1,0:T(8,128)(2,1)S(1)}, u32[]{:S(2)}, u32[]{:S(2)}) collective-permute-start(bf16[64,8,512]{2,1,0:T(8,128)(2,1)S(1)} %dynamic-slice_bitcast_fusion), channel_id=1, source_target_pairs={{0,1},{1,0},{2,3},{3,2},{4,5},{5,4},{6,7},{7,6},{8,9},{9,8},{10,11... | collective-permute-start | bytes 1572872 | tf_op jit(solution)/shard_map/ppermute | solution.py:521
  7.2 7.9 %collective-permute-start.2 = (bf16[64,2048]{1,0:T(8,128)(2,1)S(1)}, bf16[64,2048]{1,0:T(8,128)(2,1)S(1)}, u32[]{:S(2)}, u32[]{:S(2)}) collective-permute-start(bf16[64,2048]{1,0:T(8,128)(2,1)S(1)} %get-tuple-element.57), channel_id=1, source_target_pairs={{0,3},{1,4},{2,7},{3,0},{4,1},{5,6},{6,5},{7,2},{8,13},{9,10},{10,... | collective-permute-start | bytes 786440 | tf_op jit(solution)/shard_map/ppermute | solution.py:524
  10.6 4.8 %collective-permute-start.7 = (bf16[32,2048]{1,0:T(8,128)(2,1)S(1)}, bf16[32,2048]{1,0:T(8,128)(2,1)S(1)}, u32[]{:S(2)}, u32[]{:S(2)}) collective-permute-start(bf16[32,2048]{1,0:T(8,128)(2,1)S(1)} %get-tuple-element.67), channel_id=1, source_target_pairs={{0,5},{1,2},{2,1},{3,6},{4,7},{5,0},{6,3},{7,4},{8,11},{9,12},{10,... | collective-permute-start | bytes 393224 | tf_op jit(solution)/shard_map/ppermute | solution.py:524
  15.1 4.5 %collective-permute-start.4 = (bf16[32,2048]{1,0:T(8,128)(2,1)S(1)}, bf16[32,2048]{1,0:T(8,128)(2,1)S(1)}, u32[]{:S(2)}, u32[]{:S(2)}) collective-permute-start(bf16[32,2048]{1,0:T(8,128)(2,1)S(1)} %get-tuple-element.61), channel_id=1, source_target_pairs={{0,5},{1,2},{2,1},{3,6},{4,7},{5,0},{6,3},{7,4},{8,11},{9,12},{10,... | collective-permute-start | bytes 393224 | tf_op jit(solution)/shard_map/ppermute | solution.py:524
  15.5 7.5 %collective-permute-start.8 = (bf16[16,2048]{1,0:T(8,128)(2,1)S(1)}, bf16[16,2048]{1,0:T(8,128)(2,1)S(1)}, u32[]{:S(2)}, u32[]{:S(2)}) collective-permute-start(bf16[16,2048]{1,0:T(8,128)(2,1)S(1)} %get-tuple-element.69), channel_id=1, source_target_pairs={{0,9},{1,8},{2,11},{3,10},{4,13},{5,12},{6,15},{7,14},{8,1},{9,0},... | collective-permute-start | bytes 196616 | tf_op jit(solution)/shard_map/ppermute | solution.py:524
  19.6 7.2 %collective-permute-start.5 = (bf16[16,2048]{1,0:T(8,128)(2,1)S(1)}, bf16[16,2048]{1,0:T(8,128)(2,1)S(1)}, u32[]{:S(2)}, u32[]{:S(2)}) collective-permute-start(bf16[16,2048]{1,0:T(8,128)(2,1)S(1)} %get-tuple-element.63), channel_id=1, source_target_pairs={{0,9},{1,8},{2,11},{3,10},{4,13},{5,12},{6,15},{7,14},{8,1},{9,0},... | collective-permute-start | bytes 196616 | tf_op jit(solution)/shard_map/ppermute | solution.py:524
  29.1 6.0 %collective-permute-start.9 = (f32[4,136,128]{2,1,0:T(8,128)S(1)}, f32[4,136,128]{2,1,0:T(8,128)S(1)}, u32[]{:S(2)}, u32[]{:S(2)}) collective-permute-start(f32[4,136,128]{2,1,0:T(8,128)S(1)} %get-tuple-element.74), channel_id=1, source_target_pairs={{0,3},{1,4},{2,7},{3,0},{4,1},{5,6},{6,5},{7,2},{8,13},{9,10},{10,... | collective-permute-start | bytes 835592 | tf_op jit(solution)/shard_map/ppermute | solution.py:524
  31.7 6.9 %collective-permute-start.13 = (f32[4,128,128]{2,1,0:T(8,128)S(1)}, f32[4,128,128]{2,1,0:T(8,128)S(1)}, u32[]{:S(2)}, u32[]{:S(2)}) collective-permute-start(f32[4,128,128]{2,1,0:T(8,128)S(1)} %get-tuple-element.77.refs_0_), channel_id=1, source_target_pairs={{0,3},{1,4},{2,7},{3,0},{4,1},{5,6},{6,5},{7,2},{8,13},{9,10},{10,... | collective-permute-start | bytes 786440 | tf_op jit(solution)/shard_map/ppermute | solution.py:524
  35.2 4.5 %collective-permute-start.10 = (f32[2,136,128]{2,1,0:T(8,128)S(1)}, f32[2,136,128]{2,1,0:T(8,128)S(1)}, u32[]{:S(2)}, u32[]{:S(2)}) collective-permute-start(f32[2,136,128]{2,1,0:T(8,128)S(1)} %get-tuple-element.79), channel_id=1, source_target_pairs={{0,5},{1,2},{2,1},{3,6},{4,7},{5,0},{6,3},{7,4},{8,11},{9,12},{10,... | collective-permute-start | bytes 417800 | tf_op jit(solution)/shard_map/ppermute | solution.py:524
  38.6 4.5 %collective-permute-start.14 = (f32[2,128,128]{2,1,0:T(8,128)S(1)}, f32[2,128,128]{2,1,0:T(8,128)S(1)}, u32[]{:S(2)}, u32[]{:S(2)}) collective-permute-start(f32[2,128,128]{2,1,0:T(8,128)S(1)} %get-tuple-element.90), channel_id=1, source_target_pairs={{0,5},{1,2},{2,1},{3,6},{4,7},{5,0},{6,3},{7,4},{8,11},{9,12},{10,... | collective-permute-start | bytes 393224 | tf_op jit(solution)/shard_map/ppermute | solution.py:524
  39.8 6.0 %collective-permute-start.11 = (f32[1,136,128]{2,1,0:T(8,128)S(1)}, f32[1,136,128]{2,1,0:T(8,128)S(1)}, u32[]{:S(2)}, u32[]{:S(2)}) collective-permute-start(f32[1,136,128]{2,1,0:T(8,128)S(1)} %get-tuple-element.81), channel_id=1, source_target_pairs={{0,9},{1,8},{2,11},{3,10},{4,13},{5,12},{6,15},{7,14},{8,1},{9,0},... | collective-permute-start | bytes 208904 | tf_op jit(solution)/shard_map/ppermute | solution.py:524
  43.1 6.7 %collective-permute-start.15 = (f32[1,128,128]{2,1,0:T(8,128)S(1)}, f32[1,128,128]{2,1,0:T(8,128)S(1)}, u32[]{:S(2)}, u32[]{:S(2)}) collective-permute-start(f32[1,128,128]{2,1,0:T(8,128)S(1)} %get-tuple-element.92), channel_id=1, source_target_pairs={{0,9},{1,8},{2,11},{3,10},{4,13},{5,12},{6,15},{7,14},{8,1},{9,0},... | collective-permute-start | bytes 196616 | tf_op jit(solution)/shard_map/ppermute | solution.py:524
  45.8 4.2 %collective-permute-start.12 = (f32[72,128]{1,0:T(8,128)S(1)}, f32[72,128]{1,0:T(8,128)S(1)}, u32[]{:S(2)}, u32[]{:S(2)}) collective-permute-start(f32[72,128]{1,0:T(8,128)S(1)} %get-tuple-element.83), channel_id=1, source_target_pairs={{0,1},{1,0},{2,3},{3,2},{4,5},{5,4},{6,7},{7,6},{8,9},{9,8},{10,11... | collective-permute-start | bytes 110600 | tf_op jit(solution)/shard_map/ppermute | solution.py:521
  49.8 1.3 %collective-permute-start.16 = (f32[64,128]{1,0:T(8,128)S(1)}, f32[64,128]{1,0:T(8,128)S(1)}, u32[]{:S(2)}, u32[]{:S(2)}) collective-permute-start(f32[64,128]{1,0:T(8,128)S(1)} %get-tuple-element.94), channel_id=1, source_target_pairs={{0,1},{1,0},{2,3},{3,2},{4,5},{5,4},{6,7},{7,6},{8,9},{9,8},{10,11... | collective-permute-start | bytes 98312 | tf_op jit(solution)/shard_map/ppermute | solution.py:521

commit v4 on v3

--- a/solution.py
+++ b/solution.py
@@ -41,7 +41,28 @@
     return sum(dot(m, part) for part in split3(v))
 
 
-def shift_kernel(templates_ref, other_ref, w_ref, norm_ref, rows_ref, *, phases, devices):
+def give_kernel(templates_hbm, before, out_ref, sem, *, devices):
+    panel = panel_of(lax.axis_index("win"), devices)
+    copy = pltpu.make_async_copy(templates_hbm.at[1 - panel], out_ref, sem)
+    copy.start()
+    copy.wait()
+
+
+def given(templates, before, devices):
+    return pl.pallas_call(
+        lambda *refs: give_kernel(*refs, devices=devices),
+        out_shape=jax.ShapeDtypeStruct(templates.shape[1:], bf16),
+        in_specs=[pl.BlockSpec(memory_space=pltpu.HBM), pl.BlockSpec(memory_space=pl.ANY)],
+        out_specs=IN_VMEM,
+        scratch_shapes=[pltpu.SemaphoreType.DMA],
+        compiler_params=SMALL,
+        cost_estimate=pl.CostEstimate(flops=2**28, bytes_accessed=2**20, transcendentals=0),
+        name="give",
+    )(templates, before)
+
+
+def shift_kernel(templates_ref, other_ref, *refs, phases, devices):
+    w_ref, norm_ref, rows_ref = refs[-3:]
     gc = other_ref.shape[0]
     panel = panel_of(lax.axis_index("win"), devices)
     groups = LANES // 2
@@ -76,24 +97,26 @@
             w_ref[v, at : at + size, :] = jnp.where(low[:size], even, odd).astype(bf16)
 
 
-def shifted(templates, other, phases, pairs):
-    channels = 2 * other.shape[1]
+def shifted(templates, other, phases, pairs, *before):
+    gc = other.shape[0]
+    channels = 2 * gc // 64
     versions = max(1, 8 // channels)
     total = 256 * pairs + channels * phases
     front = (2 * versions - 1) * channels + 8
     front = (front + 7) // 8 * 8
-    gc = other.shape[0] * other.shape[1]
     return pl.pallas_call(
         lambda *refs: shift_kernel(*refs, phases=phases, devices=2 * phases),
+        in_specs=[IN_VMEM, IN_VMEM] + [pl.BlockSpec(memory_space=pl.ANY)] * len(before),
+        out_specs=(IN_VMEM, IN_VMEM),
         out_shape=(
             jax.ShapeDtypeStruct((versions, total, LANES), bf16),
             jax.ShapeDtypeStruct((8, LANES), f32),
         ),
         scratch_shapes=[pltpu.VMEM((front + total, LANES), f32)],
         compiler_params=pltpu.CompilerParams(vmem_limit_bytes=512 * (front + total) + SPARE),
-        cost_estimate=pl.CostEstimate(flops=2**30, bytes_accessed=2**24, transcendentals=0),
+        cost_estimate=pl.CostEstimate(flops=2**28, bytes_accessed=2**20, transcendentals=0),
         name="shift_templates",
-    )(templates.reshape(-1, gc, L), other.reshape(gc, L))
+    )(templates, other, *before)
 
 
 def bits_of(devices):
@@ -171,15 +194,15 @@
 
 
 def late_kernel(*refs, phases):
-    *pieces, w_ref, out_rows, out_energy, out_slide, out_acc, spread_ref, rows_ref = refs
+    *pieces, w_ref, out_rows, out_energy, out_acc, spread_ref, rows_ref, slide_ref = refs
     rows = spread(pieces, spread_ref, phases)
     count = rows.shape[0]
     out_rows[...] = rows
     rows_ref[pl.ds(0, count), :] = rows
     rows_ref[pl.ds(count, rows_ref.shape[0] - count), :] = jnp.zeros((rows_ref.shape[0] - count, LANES), f32)
-    fill_slide(rows_ref, out_slide)
+    fill_slide(rows_ref, slide_ref)
     out_energy[...] = energies(rows * rows, count, phases)
-    correlate_tiles([(out_slide, count)], w_ref, out_acc, range(phases // 4), phases)
+    correlate_tiles([(slide_ref, count)], w_ref, out_acc, range(phases // 2), phases)
 
 
 def write_blocks(send_ref, keep_ref, acc_ref, lead, per, devices):
@@ -206,7 +229,7 @@
     rows_ref[pl.ds(0, m), :] = rows
     rows_ref[pl.ds(m, n - m), :] = rest_rows[...]
     fill_slide(rows_ref, slide_ref)
-    acc_ref[pl.ds(m, n - m), :] = rest_acc[...]
+    acc_ref[pl.ds(m, n - m), :] = rest_acc[:, : acc_ref.shape[1]]
     correlate_tiles([(slide_ref, m)], w_ref, acc_ref, range(phases // 4), phases)
 
     squares = rows_ref[...]
@@ -230,9 +253,11 @@
     write_blocks(send_ref, keep_ref, acc_ref, extras, per, devices)
 
 
-def rest_kernel(early_slide, late_slide, w_ref, send_ref, keep_ref, acc_ref, *, rows, phases, devices):
-    slides = list(zip((early_slide, late_slide), rows))
-    correlate_tiles(slides, w_ref, acc_ref, range(phases // 4, phases // 2), phases)
+def rest_kernel(slide_ref, w_ref, rest_acc, send_ref, keep_ref, acc_ref, *, phases, devices):
+    n, width = acc_ref.shape
+    m = n - rest_acc.shape[0]
+    acc_ref[pl.ds(m, n - m), :] = rest_acc[:, width:]
+    correlate_tiles([(slide_ref, m)], w_ref, acc_ref, range(phases // 4, phases // 2), phases)
     write_blocks(send_ref, keep_ref, acc_ref, None, L // phases, devices)
 
 
@@ -249,17 +274,16 @@
     t = pieces[0].shape[1]
     count = t // phases
     slide = slide_shape(count, phases)
-    shapes = [pltpu.VMEM((t, LANES), f32), pltpu.VMEM((slide[1] + 16, LANES), f32)]
+    shapes = [pltpu.VMEM((t, LANES), f32), pltpu.VMEM((slide[1] + 16, LANES), f32), pltpu.VMEM(slide, bf16)]
     return pl.pallas_call(
         lambda *refs: late_kernel(*refs, phases=phases),
         out_shape=(
             jax.ShapeDtypeStruct((count, LANES), f32),
             jax.ShapeDtypeStruct((count, LANES), f32),
-            jax.ShapeDtypeStruct(slide, bf16),
-            jax.ShapeDtypeStruct((count, phases * 32), f32),
+            jax.ShapeDtypeStruct((count, phases * 64), f32),
         ),
         in_specs=[IN_VMEM] * (len(pieces) + 1),
-        out_specs=(IN_VMEM,) * 4,
+        out_specs=(IN_VMEM,) * 3,
         scratch_shapes=shapes,
         compiler_params=grant(shapes),
         cost_estimate=pl.CostEstimate(flops=2**31, bytes_accessed=2**22, transcendentals=0),
@@ -290,11 +314,11 @@
     )(*pieces, w, norm, *rest)
 
 
-def correlate_rest(early_slide, late_slide, w, rows, phases, devices):
-    shapes = [pltpu.VMEM((sum(rows), phases * 32), f32)]
+def correlate_rest(slide, w, rest_acc, m, phases, devices):
+    shapes = [pltpu.VMEM((m + rest_acc.shape[0], phases * 32), f32)]
     block = jax.ShapeDtypeStruct((devices // 4, LANES, LANES), f32)
     return pl.pallas_call(
-        lambda *refs: rest_kernel(*refs, rows=rows, phases=phases, devices=devices),
+        lambda *refs: rest_kernel(*refs, phases=phases, devices=devices),
         out_shape=(block, block),
         in_specs=[IN_VMEM] * 3,
         out_specs=(IN_VMEM, IN_VMEM),
@@ -302,7 +326,7 @@
         compiler_params=grant(shapes),
         cost_estimate=pl.CostEstimate(flops=2**33, bytes_accessed=2**24, transcendentals=0),
         name="correlate_rest",
-    )(early_slide, late_slide, w)
+    )(slide, w, rest_acc)
 
 
 def cut(block, phases):
@@ -466,23 +490,24 @@
     )(panel_start)
 
 
-def select_kernel(records_ref, routed_ref, away_ref, home_ref, *, begin):
+def select_kernel(records_ref, routed_ref, *refs, begin):
+    away_ref, home_ref = refs[-2:]
     both = dot(routed_ref[...], records_ref[:, begin : begin + away_ref.shape[1]]).astype(bf16)
     away_ref[...] = both[:CT]
     home_ref[...] = both[CT:]
 
 
-def selected(records, routed, begin, end):
+def selected(records, routed, begin, end, *before):
     out = jax.ShapeDtypeStruct((CT, end - begin), bf16)
     return pl.pallas_call(
         lambda *refs: select_kernel(*refs, begin=begin),
         out_shape=(out, out),
-        in_specs=[IN_VMEM, IN_VMEM],
+        in_specs=[IN_VMEM, IN_VMEM] + [pl.BlockSpec(memory_space=pl.ANY)] * len(before),
         out_specs=(IN_VMEM, IN_VMEM),
         compiler_params=pltpu.CompilerParams(vmem_limit_bytes=SPARE),
         cost_estimate=pl.CostEstimate(flops=2**27, bytes_accessed=2**21, transcendentals=0),
         name="select",
-    )(records, routed)
+    )(records, routed, *before)
 
 
 def add_kernel(kept_ref, got_ref, *refs):
@@ -532,21 +557,21 @@
     routed = masks(panel_start, records.shape[0], devices)
     away_late, home_late = selected(records, routed, half, 2 * half)
     got_late = sibling(away_late)
-    away_early, home_early = selected(records, routed, 0, half)
+    away_early, home_early = selected(records, routed, 0, half, away_late)
     got_early = sibling(away_early)
 
-    keep, send = added(home_late, got_late)
-    late = keep, send
-    got_early, templates = lax.optimization_barrier((got_early, templates))
-    early = added(home_early, got_early, keep)
-    given = lax.dynamic_index_in_dim(templates, 1 - panel, 0, keepdims=False)
-    w, norm = shifted(templates, sibling(given), phases, pairs)
-    late = scattered(*late, steps)
-    early = scattered(*early, steps, [norm])
-    rest_rows, rest_energy, late_slide, rest_acc = correlate_late(late, w, phases)
-    send_a, keep_a, early_slide = correlate_early(early, w, norm, (rest_rows, rest_energy, rest_acc), phases, devices)
-    rows = [piece[0].shape[1] // phases for piece in (early, late)]
-    send_b, keep_b = correlate_rest(early_slide, late_slide, w, rows, phases, devices)
+    templates = templates.reshape(templates.shape[0], -1, L)
+    other = sibling(given(templates, away_early, devices))
+    late = added(home_late, got_late)
+    early = added(home_early, got_early, late[0])
+    w, norm = shifted(templates, other, phases, pairs, early[0])
+    for step in range(steps - 1):
+        late = added(late[0], exchange(late[1], step), *([norm] if step == 0 else []))
+        early = added(early[0], exchange(early[1], step))
+    late, early = [(keep, exchange(send, steps - 1)) for keep, send in (late, early)]
+    rest_rows, rest_energy, rest_acc = correlate_late(late, w, phases)
+    send_a, keep_a, slide = correlate_early(early, w, norm, (rest_rows, rest_energy, rest_acc), phases, devices)
+    send_b, keep_b = correlate_rest(slide, w, rest_acc, half // phases, phases, devices)
 
     mine, other = halves(*scattered(keep_a, send_a, steps, [send_b]), phases)
     first = scaled(mine, sibling(other), phases, devices)

time: 52 us -> 50.1 us (0.963)
  waiting for transfers between devices: 18.1 us -> 11.8 us
  starting transfers between devices: 20.9 us -> 25.2 us
    ppermute x12, waiting for transfers between devices: 16.3 us -> 10.8 us  [exchange(): lax.ppermute(value, 'win', [(d, d ^ 1 ^ orders[panel_of(d, devices)][step...]
    ppermute x12, starting transfers between devices: 18.8 us -> 22.4 us  [exchange(): lax.ppermute(value, 'win', [(d, d ^ 1 ^ orders[panel_of(d, devices)][step...]
    pallas_call x1, Pallas kernels: 2.11 us -> 3.23 us  [correlate_late(): pl.pallas_call(lambda *refs: late_kernel(*refs, phases=phases), out_shape...]
    pallas_call x1 -> x2, Pallas kernels: 2.43 us -> 1.39 us  [the longest x1 1.34 us: correlate_rest(): pl.pallas_call(lambda *refs: rest_kernel(*refs, phases=phases, devices=de...]
    ppermute x5, starting transfers between devices: 2.06 us -> 2.87 us  [sibling(): return lax.ppermute(value, 'win', [(d, d ^ 1) for d in range(devices)])]
    ppermute x5, waiting for transfers between devices: 1.75 us -> 0.94 us  [sibling(): return lax.ppermute(value, 'win', [(d, d ^ 1) for d in range(devices)])]
  transfers between devices with their start and end apart: 17 -> 17, of which waited for: 11 -> 11; matrix products, arithmetic and copies ran while one was open for 0% -> 0% of each run, Pallas kernels for 15% -> 16%
where the time goes in v4:
time: 50.1 us; the launch traced here: 49.9 us
  starting transfers between devices  25.2 us (50%)
  Pallas kernels  12 us (24%)
  waiting for transfers between devices  11.8 us (24%)
  local copies, waits for them, and re-layouts  0.75 us (1%)
    ppermute x12, starting transfers between devices, exchange(): lax.ppermute(value, 'win', [(d, d ^ 1 ^ orders[panel_of(d, devices)][step...  22.4 us
    ppermute x12, waiting for transfers between devices, exchange(): lax.ppermute(value, 'win', [(d, d ^ 1 ^ orders[panel_of(d, devices)][step...  10.8 us
    pallas_call x1, Pallas kernels, correlate_late(): pl.pallas_call(lambda *refs: late_kernel(*refs, phases=phases), out_shape...  3.23 us
    ppermute x5, starting transfers between devices, sibling(): return lax.ppermute(value, 'win', [(d, d ^ 1) for d in range(devices)])  2.87 us
    pallas_call x1, Pallas kernels, correlate_early(): pl.pallas_call(lambda *refs: early_kernel(*refs, phases=phases, devices=d...  2.31 us
    pallas_call x1, Pallas kernels, shifted(): pl.pallas_call(lambda *refs: shift_kernel(*refs, phases=phases, devices=2...  2.27 us
    pallas_call x1, Pallas kernels, correlate_rest(): pl.pallas_call(lambda *refs: rest_kernel(*refs, phases=phases, devices=de...  1.34 us
  transfers between devices with their start and end apart: 17, of which 11 were waited for; matrix products, arithmetic and copies ran while one was open for 0% of the time, Pallas kernels for 16%

profile of v4, /device:TPU:0, one launch (start us, length us, event | category | flops | bytes accessed | tf_op | source)
XLA Modules:
  0.0 49.9 jit_solution(13147092716950123281)
XLA Ops:
  0.0 0.7 %copy-done.2 = s32[2]{0:T(128)S(1)} copy-done((s32[2]{0:T(128)S(1)}, s32[2]{0:T(128)}, u32[]{:S(2)}) %copy-start.2) | copy-done | bytes 32
  0.7 0.6 %masks.1.refs_1_ = bf16[256,128]{1,0:T(8,128)(2,1)S(1)} custom-call(s32[2]{0:T(128)S(1)} %copy-done.2), custom_call_target="tpu_custom_call" | custom-call | flops 2147483648 | bytes 65536 | tf_op jit(solution)/shard_map/masks/pallas_call | solution.py:481
  1.3 0.0 copy-done.1
  1.3 0.0 copy-start
  1.3 0.4 select.2
  1.8 0.5 %collective-permute-start.1 = (bf16[128,2048]{1,0:T(8,128)(2,1)S(1)}, bf16[128,2048]{1,0:T(8,128)(2,1)S(1)}, u32[]{:S(2)}, u32[]{:S(2)}) collective-permute-start(bf16[128,2048]{1,0:T(8,128)(2,1)S(1)} %get-tuple-element.47.refs_2_), channel_id=1, source_target_pairs={{0,1},{1,0},{2,3},{3,2},{4,5},{5,4},{6,7},{7,6},{8,9},{9,8},{10,11... | collective-permute-start | bytes 1572872 | tf_op jit(solution)/shard_map/ppermute | solution.py:546
  2.3 0.4 select.3
  2.7 0.1 collective-permute-start
  2.9 0.5 %collective-permute-start.5 = (bf16[512,512]{1,0:T(8,128)(2,1)S(1)}, bf16[512,512]{1,0:T(8,128)(2,1)S(1)}, u32[]{:S(2)}, u32[]{:S(2)}) collective-permute-start(bf16[512,512]{1,0:T(8,128)(2,1)S(1)} %give.1), channel_id=1, source_target_pairs={{0,1},{1,0},{2,3},{3,2},{4,5},{5,4},{6,7},{7,6},{8,9},{9,8},{10,11... | collective-permute-start | bytes 1572872 | tf_op jit(solution)/shard_map/ppermute | solution.py:546
  3.4 0.4 collective-permute-done.1.got_ref
  3.8 0.1 add.10
  3.9 2.7 %collective-permute-start.6 = (bf16[64,2048]{1,0:T(8,128)(2,1)S(1)}, bf16[64,2048]{1,0:T(8,128)(2,1)S(1)}, u32[]{:S(2)}, u32[]{:S(2)}) collective-permute-start(bf16[64,2048]{1,0:T(8,128)(2,1)S(1)} %get-tuple-element.60), channel_id=1, source_target_pairs={{0,3},{1,4},{2,7},{3,0},{4,1},{5,6},{6,5},{7,2},{8,13},{9,10},{10,... | collective-permute-start | bytes 786440 | tf_op jit(solution)/shard_map/ppermute | solution.py:549
  6.5 0.0 collective-permute-done.got_ref
  6.5 0.1 add.11
  6.6 0.8 %collective-permute-start.2 = (bf16[64,2048]{1,0:T(8,128)(2,1)S(1)}, bf16[64,2048]{1,0:T(8,128)(2,1)S(1)}, u32[]{:S(2)}, u32[]{:S(2)}) collective-permute-start(bf16[64,2048]{1,0:T(8,128)(2,1)S(1)} %get-tuple-element.53), channel_id=1, source_target_pairs={{0,3},{1,4},{2,7},{3,0},{4,1},{5,6},{6,5},{7,2},{8,13},{9,10},{10,... | collective-permute-start | bytes 786440 | tf_op jit(solution)/shard_map/ppermute | solution.py:549
  7.4 0.0 collective-permute-done.5.refs_1_
  7.4 2.3 %shift_templates.1 = (bf16[1,8576,128]{2,1,0:T(8,128)(2,1)S(1)}, f32[8,128]{1,0:T(8,128)S(1)}) custom-call(bf16[2,512,512]{2,1,0:T(8,128)(2,1)S(1)} %bitcast.2, bf16[512,512]{1,0:T(8,128)(2,1)S(1)} %collective-permute-done.5.refs_1_, bf16[64,2048]{1,0:T(8,128)(2,1)S(1)} %get-tuple-element.52.kept_ref.refs_2_), custom_call_target="tpu_custom_call" | custom-call | flops 268435456 | bytes 1048576 | tf_op jit(solution)/shard_map/shift_templates/pallas_call | solution.py:107
  9.7 0.9 %collective-permute-done.6.got_ref = bf16[64,2048]{1,0:T(8,128)(2,1)S(1)} collective-permute-done((bf16[64,2048]{1,0:T(8,128)(2,1)S(1)}, bf16[64,2048]{1,0:T(8,128)(2,1)S(1)}, u32[]{:S(2)}, u32[]{:S(2)}) %collective-permute-start.6) | collective-permute-done | bytes 262176 | tf_op jit(solution)/shard_map/ppermute | solution.py:549
  10.6 2.2 %collective-permute-start.7 = (bf16[32,2048]{1,0:T(8,128)(2,1)S(1)}, bf16[32,2048]{1,0:T(8,128)(2,1)S(1)}, u32[]{:S(2)}, u32[]{:S(2)}) collective-permute-start(bf16[32,2048]{1,0:T(8,128)(2,1)S(1)} %get-tuple-element.62), channel_id=1, source_target_pairs={{0,5},{1,2},{2,1},{3,6},{4,7},{5,0},{6,3},{7,4},{8,11},{9,12},{10,... | collective-permute-start | bytes 393224 | tf_op jit(solution)/shard_map/ppermute | solution.py:549
  12.8 0.6 %collective-permute-done.2.got_ref = bf16[64,2048]{1,0:T(8,128)(2,1)S(1)} collective-permute-done((bf16[64,2048]{1,0:T(8,128)(2,1)S(1)}, bf16[64,2048]{1,0:T(8,128)(2,1)S(1)}, u32[]{:S(2)}, u32[]{:S(2)}) %collective-permute-start.2) | collective-permute-done | bytes 262176 | tf_op jit(solution)/shard_map/ppermute | solution.py:549
  13.4 1.9 %collective-permute-start.3 = (bf16[32,2048]{1,0:T(8,128)(2,1)S(1)}, bf16[32,2048]{1,0:T(8,128)(2,1)S(1)}, u32[]{:S(2)}, u32[]{:S(2)}) collective-permute-start(bf16[32,2048]{1,0:T(8,128)(2,1)S(1)} %get-tuple-element.55), channel_id=1, source_target_pairs={{0,5},{1,2},{2,1},{3,6},{4,7},{5,0},{6,3},{7,4},{8,11},{9,12},{10,... | collective-permute-start | bytes 393224 | tf_op jit(solution)/shard_map/ppermute | solution.py:549
  15.3 0.1 collective-permute-done.7.got_ref
  15.5 2.8 %collective-permute-start.8 = (bf16[16,2048]{1,0:T(8,128)(2,1)S(1)}, bf16[16,2048]{1,0:T(8,128)(2,1)S(1)}, u32[]{:S(2)}, u32[]{:S(2)}) collective-permute-start(bf16[16,2048]{1,0:T(8,128)(2,1)S(1)} %get-tuple-element.64), channel_id=1, source_target_pairs={{0,9},{1,8},{2,11},{3,10},{4,13},{5,12},{6,15},{7,14},{8,1},{9,0},... | collective-permute-start | bytes 196616 | tf_op jit(solution)/shard_map/ppermute | solution.py:549
  18.3 0.0 collective-permute-done.3.got_ref
  18.3 2.5 %collective-permute-start.4 = (bf16[16,2048]{1,0:T(8,128)(2,1)S(1)}, bf16[16,2048]{1,0:T(8,128)(2,1)S(1)}, u32[]{:S(2)}, u32[]{:S(2)}) collective-permute-start(bf16[16,2048]{1,0:T(8,128)(2,1)S(1)} %get-tuple-element.57), channel_id=1, source_target_pairs={{0,9},{1,8},{2,11},{3,10},{4,13},{5,12},{6,15},{7,14},{8,1},{9,0},... | collective-permute-start | bytes 196616 | tf_op jit(solution)/shard_map/ppermute | solution.py:549
  20.9 0.0 collective-permute-done.8.refs_1_
  20.9 3.2 %correlate_late.1 = (f32[256,128]{1,0:T(8,128)S(1)}, f32[256,128]{1,0:T(8,128)S(1)}, f32[256,512]{1,0:T(8,128)S(1)}) custom-call(bf16[16,2048]{1,0:T(8,128)(2,1)S(1)} %get-tuple-element.63.refs_0_, bf16[16,2048]{1,0:T(8,128)(2,1)S(1)} %collective-permute-done.8.refs_1_, bf16[1,8576,128]{2,1,0:T(8,128)(2,1)S(1)} %get-tuple-element.58.refs_2_.refs_1_), custom_call_target="tpu_custom_call" | custom-call | flops 2147483648 | bytes 4194304 | tf_op jit(solution)/shard_map/correlate_late/pallas_call | solution.py:278
  24.1 0.8 %collective-permute-done.4.refs_1_ = bf16[16,2048]{1,0:T(8,128)(2,1)S(1)} collective-permute-done((bf16[16,2048]{1,0:T(8,128)(2,1)S(1)}, bf16[16,2048]{1,0:T(8,128)(2,1)S(1)}, u32[]{:S(2)}, u32[]{:S(2)}) %collective-permute-start.4) | collective-permute-done | bytes 65568 | tf_op jit(solution)/shard_map/ppermute | solution.py:549
  24.9 2.3 %correlate_early.1 = (f32[4,136,128]{2,1,0:T(8,128)S(1)}, f32[4,136,128]{2,1,0:T(8,128)S(1)}, bf16[8,320,256]{2,1,0:T(8,128)(2,1)S(1)}) custom-call(bf16[16,2048]{1,0:T(8,128)(2,1)S(1)} %get-tuple-element.56.refs_0_, bf16[16,2048]{1,0:T(8,128)(2,1)S(1)} %collective-permute-done.4.refs_1_, bf16[1,8576,128]{2,1,0:T(8,128)(2,1)S(1)} %get-tuple-element.58.refs_2_.refs_1_, ...), custom_call_target="tpu_custom_call" | custom-call | flops 4294967296 | bytes 16777216 | tf_op jit(solution)/shard_map/correlate_early/pallas_call | solution.py:305
  27.2 1.8 %collective-permute-start.9 = (f32[4,136,128]{2,1,0:T(8,128)S(1)}, f32[4,136,128]{2,1,0:T(8,128)S(1)}, u32[]{:S(2)}, u32[]{:S(2)}) collective-permute-start(f32[4,136,128]{2,1,0:T(8,128)S(1)} %get-tuple-element.69), channel_id=1, source_target_pairs={{0,3},{1,4},{2,7},{3,0},{4,1},{5,6},{6,5},{7,2},{8,13},{9,10},{10,... | collective-permute-start | bytes 835592 | tf_op jit(solution)/shard_map/ppermute | solution.py:549
  29.0 1.3 %correlate_rest.1 = (f32[4,128,128]{2,1,0:T(8,128)S(1)}, f32[4,128,128]{2,1,0:T(8,128)S(1)}) custom-call(bf16[8,320,256]{2,1,0:T(8,128)(2,1)S(1)} %get-tuple-element.70.refs_0_, bf16[1,8576,128]{2,1,0:T(8,128)(2,1)S(1)} %get-tuple-element.58.refs_2_.refs_1_, f32[256,512]{1,0:T(8,128)S(1)} %get-tuple-element.67.refs_6_.refs_2_), custom_call_target="tpu_custom_call" | custom-call | flops 8589934592 | bytes 16777216 | tf_op jit(solution)/shard_map/correlate_rest/pallas_call | solution.py:320
  30.4 0.1 collective-permute-start.13
  30.5 2.8 %collective-permute-done.9.got_ref = f32[4,136,128]{2,1,0:T(8,128)S(1)} collective-permute-done((f32[4,136,128]{2,1,0:T(8,128)S(1)}, f32[4,136,128]{2,1,0:T(8,128)S(1)}, u32[]{:S(2)}, u32[]{:S(2)}) %collective-permute-start.9) | collective-permute-done | bytes 278560 | tf_op jit(solution)/shard_map/ppermute | solution.py:549
  33.3 1.5 %collective-permute-start.10 = (f32[2,136,128]{2,1,0:T(8,128)S(1)}, f32[2,136,128]{2,1,0:T(8,128)S(1)}, u32[]{:S(2)}, u32[]{:S(2)}) collective-permute-start(f32[2,136,128]{2,1,0:T(8,128)S(1)} %get-tuple-element.73), channel_id=1, source_target_pairs={{0,5},{1,2},{2,1},{3,6},{4,7},{5,0},{6,3},{7,4},{8,11},{9,12},{10,... | collective-permute-start | bytes 417800 | tf_op jit(solution)/shard_map/ppermute | solution.py:549
  34.8 1.4 %collective-permute-done.13.got_ref = f32[4,128,128]{2,1,0:T(8,128)S(1)} collective-permute-done((f32[4,128,128]{2,1,0:T(8,128)S(1)}, f32[4,128,128]{2,1,0:T(8,128)S(1)}, u32[]{:S(2)}, u32[]{:S(2)}) %collective-permute-start.13) | collective-permute-done | bytes 262176 | tf_op jit(solution)/shard_map/ppermute | solution.py:549
  36.3 1.2 %collective-permute-start.14 = (f32[2,128,128]{2,1,0:T(8,128)S(1)}, f32[2,128,128]{2,1,0:T(8,128)S(1)}, u32[]{:S(2)}, u32[]{:S(2)}) collective-permute-start(f32[2,128,128]{2,1,0:T(8,128)S(1)} %get-tuple-element.84), channel_id=1, source_target_pairs={{0,5},{1,2},{2,1},{3,6},{4,7},{5,0},{6,3},{7,4},{8,11},{9,12},{10,... | collective-permute-start | bytes 393224 | tf_op jit(solution)/shard_map/ppermute | solution.py:549
  37.5 1.1 %collective-permute-done.10.got_ref = f32[2,136,128]{2,1,0:T(8,128)S(1)} collective-permute-done((f32[2,136,128]{2,1,0:T(8,128)S(1)}, f32[2,136,128]{2,1,0:T(8,128)S(1)}, u32[]{:S(2)}, u32[]{:S(2)}) %collective-permute-start.10) | collective-permute-done | bytes 139296 | tf_op jit(solution)/shard_map/ppermute | solution.py:549
  38.6 2.2 %collective-permute-start.11 = (f32[1,136,128]{2,1,0:T(8,128)S(1)}, f32[1,136,128]{2,1,0:T(8,128)S(1)}, u32[]{:S(2)}, u32[]{:S(2)}) collective-permute-start(f32[1,136,128]{2,1,0:T(8,128)S(1)} %get-tuple-element.75), channel_id=1, source_target_pairs={{0,9},{1,8},{2,11},{3,10},{4,13},{5,12},{6,15},{7,14},{8,1},{9,0},... | collective-permute-start | bytes 208904 | tf_op jit(solution)/shard_map/ppermute | solution.py:549
  40.8 0.0 collective-permute-done.14.got_ref
  40.8 2.6 %collective-permute-start.15 = (f32[1,128,128]{2,1,0:T(8,128)S(1)}, f32[1,128,128]{2,1,0:T(8,128)S(1)}, u32[]{:S(2)}, u32[]{:S(2)}) collective-permute-start(f32[1,128,128]{2,1,0:T(8,128)S(1)} %get-tuple-element.86), channel_id=1, source_target_pairs={{0,9},{1,8},{2,11},{3,10},{4,13},{5,12},{6,15},{7,14},{8,1},{9,0},... | collective-permute-start | bytes 196616 | tf_op jit(solution)/shard_map/ppermute | solution.py:549
  43.5 1.6 %collective-permute-done.11.refs_1_ = f32[1,136,128]{2,1,0:T(8,128)S(1)} collective-permute-done((f32[1,136,128]{2,1,0:T(8,128)S(1)}, f32[1,136,128]{2,1,0:T(8,128)S(1)}, u32[]{:S(2)}, u32[]{:S(2)}) %collective-permute-start.11) | collective-permute-done | bytes 69664 | tf_op jit(solution)/shard_map/ppermute | solution.py:549
  45.1 1.1 %collective-permute-start.12 = (f32[72,128]{1,0:T(8,128)S(1)}, f32[72,128]{1,0:T(8,128)S(1)}, u32[]{:S(2)}, u32[]{:S(2)}) collective-permute-start(f32[72,128]{1,0:T(8,128)S(1)} %get-tuple-element.77), channel_id=1, source_target_pairs={{0,1},{1,0},{2,3},{3,2},{4,5},{5,4},{6,7},{7,6},{8,9},{9,8},{10,11... | collective-permute-start | bytes 110600 | tf_op jit(solution)/shard_map/ppermute | solution.py:546
  46.3 1.4 %collective-permute-done.15.refs_1_ = f32[1,128,128]{2,1,0:T(8,128)S(1)} collective-permute-done((f32[1,128,128]{2,1,0:T(8,128)S(1)}, f32[1,128,128]{2,1,0:T(8,128)S(1)}, u32[]{:S(2)}, u32[]{:S(2)}) %collective-permute-start.15) | collective-permute-done | bytes 65568 | tf_op jit(solution)/shard_map/ppermute | solution.py:549
  47.7 0.6 %collective-permute-start.16 = (f32[64,128]{1,0:T(8,128)S(1)}, f32[64,128]{1,0:T(8,128)S(1)}, u32[]{:S(2)}, u32[]{:S(2)}) collective-permute-start(f32[64,128]{1,0:T(8,128)S(1)} %get-tuple-element.88), channel_id=1, source_target_pairs={{0,1},{1,0},{2,3},{3,2},{4,5},{5,4},{6,7},{7,6},{8,9},{9,8},{10,11... | collective-permute-start | bytes 98312 | tf_op jit(solution)/shard_map/ppermute | solution.py:546
  48.3 0.0 collective-permute-done.12.refs_1_
  48.3 0.3 scale.1
  48.6 0.5 %collective-permute-done.16.refs_5_ = f32[64,128]{1,0:T(8,128)S(1)} collective-permute-done((f32[64,128]{1,0:T(8,128)S(1)}, f32[64,128]{1,0:T(8,128)S(1)}, u32[]{:S(2)}, u32[]{:S(2)}) %collective-permute-start.16) | collective-permute-done | bytes 32800 | tf_op jit(solution)/shard_map/ppermute | solution.py:546
  49.2 0.8 %finish.1 = f32[256,128]{1,0:T(8,128)} custom-call(f32[64,128]{1,0:T(8,128)S(1)} %get-tuple-element.78.refs_0_, f32[64,128]{1,0:T(8,128)S(1)} %get-tuple-element.79.refs_1_, f32[64,128]{1,0:T(8,128)S(1)} %get-tuple-element.80.refs_2_, f32[64,128]{1,0:T(8,128)S(1)} %get-tuple-element.81.refs_3_, f32[64,128]{1,0:T(8,128)S(1)} %get-tuple-element.87.refs_4_, ...), custom_call_target="tpu_custom_call" | custom-call | flops 262144 | bytes 262144 | tf_op jit(solution)/shard_map/finish/pallas_call | solution.py:449
  (14 shorter events, 0.3 us)
Async XLA Ops:
  0.0 1.3 %copy-start.1 = (bf16[128,4096]{1,0:T(8,128)(2,1)S(1)}, bf16[128,4096]{1,0:T(8,128)(2,1)}, u32[]{:S(2)}) copy-start(bf16[128,4096]{1,0:T(8,128)(2,1)} %refs_0_.5) | copy-start | bytes 3145732
  0.0 0.7 %copy-start.2 = (s32[2]{0:T(128)S(1)}, s32[2]{0:T(128)}, u32[]{:S(2)}) copy-start(s32[2]{0:T(128)} %refs_0_.3) | copy-start | bytes 28
  1.3 1.5 %copy-start = (bf16[2,64,8,512]{3,2,1,0:T(8,128)(2,1)S(1)}, bf16[2,64,8,512]{3,2,1,0:T(8,128)(2,1)}, u32[]{:S(2)}) copy-start(bf16[2,64,8,512]{3,2,1,0:T(8,128)(2,1)} %param.4) | copy-start | bytes 3145732
  1.8 2.1 %collective-permute-start.1 = (bf16[128,2048]{1,0:T(8,128)(2,1)S(1)}, bf16[128,2048]{1,0:T(8,128)(2,1)S(1)}, u32[]{:S(2)}, u32[]{:S(2)}) collective-permute-start(bf16[128,2048]{1,0:T(8,128)(2,1)S(1)} %get-tuple-element.47.refs_2_), channel_id=1, source_target_pairs={{0,1},{1,0},{2,3},{3,2},{4,5},{5,4},{6,7},{7,6},{8,9},{9,8},{10,11... | collective-permute-start | bytes 1572872 | tf_op jit(solution)/shard_map/ppermute | solution.py:546
  2.7 3.8 %collective-permute-start = (bf16[128,2048]{1,0:T(8,128)(2,1)S(1)}, bf16[128,2048]{1,0:T(8,128)(2,1)S(1)}, u32[]{:S(2)}, u32[]{:S(2)}) collective-permute-start(bf16[128,2048]{1,0:T(8,128)(2,1)S(1)} %get-tuple-element.49.refs_1_), channel_id=1, source_target_pairs={{0,1},{1,0},{2,3},{3,2},{4,5},{5,4},{6,7},{7,6},{8,9},{9,8},{10,11... | collective-permute-start | bytes 1572872 | tf_op jit(solution)/shard_map/ppermute | solution.py:546
  2.9 4.5 %collective-permute-start.5 = (bf16[512,512]{1,0:T(8,128)(2,1)S(1)}, bf16[512,512]{1,0:T(8,128)(2,1)S(1)}, u32[]{:S(2)}, u32[]{:S(2)}) collective-permute-start(bf16[512,512]{1,0:T(8,128)(2,1)S(1)} %give.1), channel_id=1, source_target_pairs={{0,1},{1,0},{2,3},{3,2},{4,5},{5,4},{6,7},{7,6},{8,9},{9,8},{10,11... | collective-permute-start | bytes 1572872 | tf_op jit(solution)/shard_map/ppermute | solution.py:546
  3.9 6.7 %collective-permute-start.6 = (bf16[64,2048]{1,0:T(8,128)(2,1)S(1)}, bf16[64,2048]{1,0:T(8,128)(2,1)S(1)}, u32[]{:S(2)}, u32[]{:S(2)}) collective-permute-start(bf16[64,2048]{1,0:T(8,128)(2,1)S(1)} %get-tuple-element.60), channel_id=1, source_target_pairs={{0,3},{1,4},{2,7},{3,0},{4,1},{5,6},{6,5},{7,2},{8,13},{9,10},{10,... | collective-permute-start | bytes 786440 | tf_op jit(solution)/shard_map/ppermute | solution.py:549
  6.6 6.8 %collective-permute-start.2 = (bf16[64,2048]{1,0:T(8,128)(2,1)S(1)}, bf16[64,2048]{1,0:T(8,128)(2,1)S(1)}, u32[]{:S(2)}, u32[]{:S(2)}) collective-permute-start(bf16[64,2048]{1,0:T(8,128)(2,1)S(1)} %get-tuple-element.53), channel_id=1, source_target_pairs={{0,3},{1,4},{2,7},{3,0},{4,1},{5,6},{6,5},{7,2},{8,13},{9,10},{10,... | collective-permute-start | bytes 786440 | tf_op jit(solution)/shard_map/ppermute | solution.py:549
  10.6 4.8 %collective-permute-start.7 = (bf16[32,2048]{1,0:T(8,128)(2,1)S(1)}, bf16[32,2048]{1,0:T(8,128)(2,1)S(1)}, u32[]{:S(2)}, u32[]{:S(2)}) collective-permute-start(bf16[32,2048]{1,0:T(8,128)(2,1)S(1)} %get-tuple-element.62), channel_id=1, source_target_pairs={{0,5},{1,2},{2,1},{3,6},{4,7},{5,0},{6,3},{7,4},{8,11},{9,12},{10,... | collective-permute-start | bytes 393224 | tf_op jit(solution)/shard_map/ppermute | solution.py:549
  13.4 4.9 %collective-permute-start.3 = (bf16[32,2048]{1,0:T(8,128)(2,1)S(1)}, bf16[32,2048]{1,0:T(8,128)(2,1)S(1)}, u32[]{:S(2)}, u32[]{:S(2)}) collective-permute-start(bf16[32,2048]{1,0:T(8,128)(2,1)S(1)} %get-tuple-element.55), channel_id=1, source_target_pairs={{0,5},{1,2},{2,1},{3,6},{4,7},{5,0},{6,3},{7,4},{8,11},{9,12},{10,... | collective-permute-start | bytes 393224 | tf_op jit(solution)/shard_map/ppermute | solution.py:549
  15.5 5.4 %collective-permute-start.8 = (bf16[16,2048]{1,0:T(8,128)(2,1)S(1)}, bf16[16,2048]{1,0:T(8,128)(2,1)S(1)}, u32[]{:S(2)}, u32[]{:S(2)}) collective-permute-start(bf16[16,2048]{1,0:T(8,128)(2,1)S(1)} %get-tuple-element.64), channel_id=1, source_target_pairs={{0,9},{1,8},{2,11},{3,10},{4,13},{5,12},{6,15},{7,14},{8,1},{9,0},... | collective-permute-start | bytes 196616 | tf_op jit(solution)/shard_map/ppermute | solution.py:549
  18.3 6.6 %collective-permute-start.4 = (bf16[16,2048]{1,0:T(8,128)(2,1)S(1)}, bf16[16,2048]{1,0:T(8,128)(2,1)S(1)}, u32[]{:S(2)}, u32[]{:S(2)}) collective-permute-start(bf16[16,2048]{1,0:T(8,128)(2,1)S(1)} %get-tuple-element.57), channel_id=1, source_target_pairs={{0,9},{1,8},{2,11},{3,10},{4,13},{5,12},{6,15},{7,14},{8,1},{9,0},... | collective-permute-start | bytes 196616 | tf_op jit(solution)/shard_map/ppermute | solution.py:549
  27.2 6.0 %collective-permute-start.9 = (f32[4,136,128]{2,1,0:T(8,128)S(1)}, f32[4,136,128]{2,1,0:T(8,128)S(1)}, u32[]{:S(2)}, u32[]{:S(2)}) collective-permute-start(f32[4,136,128]{2,1,0:T(8,128)S(1)} %get-tuple-element.69), channel_id=1, source_target_pairs={{0,3},{1,4},{2,7},{3,0},{4,1},{5,6},{6,5},{7,2},{8,13},{9,10},{10,... | collective-permute-start | bytes 835592 | tf_op jit(solution)/shard_map/ppermute | solution.py:549
  30.4 5.9 %collective-permute-start.13 = (f32[4,128,128]{2,1,0:T(8,128)S(1)}, f32[4,128,128]{2,1,0:T(8,128)S(1)}, u32[]{:S(2)}, u32[]{:S(2)}) collective-permute-start(f32[4,128,128]{2,1,0:T(8,128)S(1)} %get-tuple-element.71.refs_0_), channel_id=1, source_target_pairs={{0,3},{1,4},{2,7},{3,0},{4,1},{5,6},{6,5},{7,2},{8,13},{9,10},{10,... | collective-permute-start | bytes 786440 | tf_op jit(solution)/shard_map/ppermute | solution.py:549
  33.3 5.3 %collective-permute-start.10 = (f32[2,136,128]{2,1,0:T(8,128)S(1)}, f32[2,136,128]{2,1,0:T(8,128)S(1)}, u32[]{:S(2)}, u32[]{:S(2)}) collective-permute-start(f32[2,136,128]{2,1,0:T(8,128)S(1)} %get-tuple-element.73), channel_id=1, source_target_pairs={{0,5},{1,2},{2,1},{3,6},{4,7},{5,0},{6,3},{7,4},{8,11},{9,12},{10,... | collective-permute-start | bytes 417800 | tf_op jit(solution)/shard_map/ppermute | solution.py:549
  36.3 4.5 %collective-permute-start.14 = (f32[2,128,128]{2,1,0:T(8,128)S(1)}, f32[2,128,128]{2,1,0:T(8,128)S(1)}, u32[]{:S(2)}, u32[]{:S(2)}) collective-permute-start(f32[2,128,128]{2,1,0:T(8,128)S(1)} %get-tuple-element.84), channel_id=1, source_target_pairs={{0,5},{1,2},{2,1},{3,6},{4,7},{5,0},{6,3},{7,4},{8,11},{9,12},{10,... | collective-permute-start | bytes 393224 | tf_op jit(solution)/shard_map/ppermute | solution.py:549
  38.6 6.5 %collective-permute-start.11 = (f32[1,136,128]{2,1,0:T(8,128)S(1)}, f32[1,136,128]{2,1,0:T(8,128)S(1)}, u32[]{:S(2)}, u32[]{:S(2)}) collective-permute-start(f32[1,136,128]{2,1,0:T(8,128)S(1)} %get-tuple-element.75), channel_id=1, source_target_pairs={{0,9},{1,8},{2,11},{3,10},{4,13},{5,12},{6,15},{7,14},{8,1},{9,0},... | collective-permute-start | bytes 208904 | tf_op jit(solution)/shard_map/ppermute | solution.py:549
  40.8 6.9 %collective-permute-start.15 = (f32[1,128,128]{2,1,0:T(8,128)S(1)}, f32[1,128,128]{2,1,0:T(8,128)S(1)}, u32[]{:S(2)}, u32[]{:S(2)}) collective-permute-start(f32[1,128,128]{2,1,0:T(8,128)S(1)} %get-tuple-element.86), channel_id=1, source_target_pairs={{0,9},{1,8},{2,11},{3,10},{4,13},{5,12},{6,15},{7,14},{8,1},{9,0},... | collective-permute-start | bytes 196616 | tf_op jit(solution)/shard_map/ppermute | solution.py:549
  45.1 3.2 %collective-permute-start.12 = (f32[72,128]{1,0:T(8,128)S(1)}, f32[72,128]{1,0:T(8,128)S(1)}, u32[]{:S(2)}, u32[]{:S(2)}) collective-permute-start(f32[72,128]{1,0:T(8,128)S(1)} %get-tuple-element.77), channel_id=1, source_target_pairs={{0,1},{1,0},{2,3},{3,2},{4,5},{5,4},{6,7},{7,6},{8,9},{9,8},{10,11... | collective-permute-start | bytes 110600 | tf_op jit(solution)/shard_map/ppermute | solution.py:546
  47.7 1.4 %collective-permute-start.16 = (f32[64,128]{1,0:T(8,128)S(1)}, f32[64,128]{1,0:T(8,128)S(1)}, u32[]{:S(2)}, u32[]{:S(2)}) collective-permute-start(f32[64,128]{1,0:T(8,128)S(1)} %get-tuple-element.88), channel_id=1, source_target_pairs={{0,1},{1,0},{2,3},{3,2},{4,5},{5,4},{6,7},{7,6},{8,9},{9,8},{10,11... | collective-permute-start | bytes 98312 | tf_op jit(solution)/shard_map/ppermute | solution.py:546

commit v5 on v4

--- a/solution.py
+++ b/solution.py
@@ -136,17 +136,22 @@
     return chip // 2
 
 
-def spread(pieces, spread_ref, phases):
-    value = sum(r[...] for r in pieces[1:]) + pieces[0][...]
-    channels, t = value.shape
-    repeat = (iota((channels, LANES), 0) == iota((channels, LANES), 1) % channels).astype(f32).astype(bf16)
+def spread(value, repeat, spread_ref, phases):
+    t = value.shape[1]
     spread_ref[...] = dot(value, repeat, (((0,), (0,)), ((), ())))
     count = t // phases
-    phase = iota((count, LANES), 1) // channels
+    phase = iota((count, LANES), 1) // (LANES // phases)
     rows = jnp.zeros((count, LANES), f32)
     for k in range(phases):
         rows = jnp.where(phase == k, spread_ref[pl.ds(k, count, stride=phases), :], rows)
     return rows
+
+
+def spread_pieces(pieces, spread_ref, phases):
+    value = sum(r[...] for r in pieces[1:]) + pieces[0][...]
+    channels = value.shape[0]
+    repeat = (iota((channels, LANES), 0) == iota((channels, LANES), 1) % channels).astype(f32).astype(bf16)
+    return spread(value, repeat, spread_ref, phases)
 
 
 def fill_slide(rows_ref, slide_ref):
@@ -173,6 +178,36 @@
     return pick(squares[:m], tail) + picked(band, sums) + begin
 
 
+def energy_kernel(first_ref, second_ref, *refs, phases):
+    out_ref, squares_ref, spread_ref = refs[-3:]
+    squares = jnp.zeros((1, first_ref.shape[1]), f32)
+    for ref in (first_ref, second_ref):
+        value = ref[...].astype(f32)
+        squares = squares + jnp.sum(value * value, axis=0, keepdims=True)
+    parts = list(split3(squares)) + [jnp.zeros((13, squares.shape[1]), bf16)]
+    repeat = ((iota((16, LANES), 1) % (LANES // phases) == 0) & (iota((16, LANES), 0) < 3)).astype(f32).astype(bf16)
+    rows = spread(jnp.concatenate(parts, axis=0), repeat, spread_ref, phases)
+    squares_ref[...] = rows
+    following = [ref[...] for ref in refs[:-4]]
+    out_ref[...] = energies(jnp.concatenate([rows] + following, axis=0), rows.shape[0], phases)
+
+
+def energy_of(chunk, following, before, phases):
+    t = chunk[0].shape[1]
+    shapes = [pltpu.VMEM((t, LANES), f32)]
+    out = jax.ShapeDtypeStruct((t // phases, LANES), f32)
+    return pl.pallas_call(
+        lambda *refs: energy_kernel(*refs, phases=phases),
+        out_shape=(out, out),
+        in_specs=[IN_VMEM] * (2 + len(following)) + [pl.BlockSpec(memory_space=pl.ANY)],
+        out_specs=(IN_VMEM, IN_VMEM),
+        scratch_shapes=shapes,
+        compiler_params=grant(shapes),
+        cost_estimate=pl.CostEstimate(flops=2**28, bytes_accessed=2**20, transcendentals=0),
+        name="energy",
+    )(*chunk, *following, before)
+
+
 def correlate_tiles(slides, w_ref, acc_ref, tiles, phases):
     versions = w_ref.shape[0]
     channels = LANES // phases
@@ -194,14 +229,13 @@
 
 
 def late_kernel(*refs, phases):
-    *pieces, w_ref, out_rows, out_energy, out_acc, spread_ref, rows_ref, slide_ref = refs
-    rows = spread(pieces, spread_ref, phases)
+    *pieces, w_ref, out_rows, out_acc, spread_ref, rows_ref, slide_ref = refs
+    rows = spread_pieces(pieces, spread_ref, phases)
     count = rows.shape[0]
     out_rows[...] = rows
     rows_ref[pl.ds(0, count), :] = rows
     rows_ref[pl.ds(count, rows_ref.shape[0] - count), :] = jnp.zeros((rows_ref.shape[0] - count, LANES), f32)
     fill_slide(rows_ref, slide_ref)
-    out_energy[...] = energies(rows * rows, count, phases)
     correlate_tiles([(slide_ref, count)], w_ref, out_acc, range(phases // 2), phases)
 
 
@@ -221,9 +255,9 @@
 
 
 def early_kernel(*refs, phases, devices):
-    *pieces, w_ref, norm_ref, rest_rows, rest_energy, rest_acc = refs[: len(refs) - 7]
+    *pieces, w_ref, norm_ref, early_energy, late_energy, rest_rows, rest_acc = refs[: len(refs) - 7]
     send_ref, keep_ref, slide_ref, rows_ref, spread_ref, energy_ref, acc_ref = refs[len(refs) - 7 :]
-    rows = spread(pieces, spread_ref, phases)
+    rows = spread_pieces(pieces, spread_ref, phases)
     m = rows.shape[0]
     n = m + rest_rows.shape[0]
     rows_ref[pl.ds(0, m), :] = rows
@@ -232,9 +266,8 @@
     acc_ref[pl.ds(m, n - m), :] = rest_acc[:, : acc_ref.shape[1]]
     correlate_tiles([(slide_ref, m)], w_ref, acc_ref, range(phases // 4), phases)
 
-    squares = rows_ref[...]
-    energy_ref[pl.ds(0, m), :] = energies(squares * squares, m, phases)
-    energy_ref[pl.ds(m, n - m), :] = rest_energy[...]
+    energy_ref[pl.ds(0, m), :] = early_energy[...]
+    energy_ref[pl.ds(m, n - m), :] = late_energy[...]
     per = L // phases
     place = iota((LANES, LANES), 1)
     wanted = (place // (2 * phases)) * phases + place % (2 * phases) - phases
@@ -279,11 +312,10 @@
         lambda *refs: late_kernel(*refs, phases=phases),
         out_shape=(
             jax.ShapeDtypeStruct((count, LANES), f32),
-            jax.ShapeDtypeStruct((count, LANES), f32),
             jax.ShapeDtypeStruct((count, phases * 64), f32),
         ),
         in_specs=[IN_VMEM] * (len(pieces) + 1),
-        out_specs=(IN_VMEM,) * 3,
+        out_specs=(IN_VMEM,) * 2,
         scratch_shapes=shapes,
         compiler_params=grant(shapes),
         cost_estimate=pl.CostEstimate(flops=2**31, bytes_accessed=2**22, transcendentals=0),
@@ -291,7 +323,7 @@
     )(*pieces, w)
 
 
-def correlate_early(pieces, w, norm, rest, phases, devices):
+def correlate_early(pieces, w, norm, energy, rest, phases, devices):
     t = pieces[0].shape[1]
     m = t // phases
     n = m + rest[0].shape[0]
@@ -305,13 +337,13 @@
     return pl.pallas_call(
         lambda *refs: early_kernel(*refs, phases=phases, devices=devices),
         out_shape=(block, block, jax.ShapeDtypeStruct(slide_shape(m, phases), bf16)),
-        in_specs=[IN_VMEM] * (len(pieces) + 5),
+        in_specs=[IN_VMEM] * (len(pieces) + 6),
         out_specs=(IN_VMEM,) * 3,
         scratch_shapes=shapes,
         compiler_params=grant(shapes),
         cost_estimate=pl.CostEstimate(flops=2**32, bytes_accessed=2**24, transcendentals=0),
         name="correlate_early",
-    )(*pieces, w, norm, *rest)
+    )(*pieces, w, norm, *energy, *rest)
 
 
 def correlate_rest(slide, w, rest_acc, m, phases, devices):
@@ -565,12 +597,18 @@
     late = added(home_late, got_late)
     early = added(home_early, got_early, late[0])
     w, norm = shifted(templates, other, phases, pairs, early[0])
+    held = late, early
     for step in range(steps - 1):
-        late = added(late[0], exchange(late[1], step), *([norm] if step == 0 else []))
-        early = added(early[0], exchange(early[1], step))
+        if step == 0:
+            late_energy, squares = energy_of(held[0], [], norm, phases)
+        late = added(late[0], exchange(late[1], step), *([late_energy] if step == 0 else []))
+        if step == 0:
+            early_energy, _ = energy_of(held[1], [squares], late[0], phases)
+        early = added(early[0], exchange(early[1], step), *([early_energy] if step == 0 else []))
     late, early = [(keep, exchange(send, steps - 1)) for keep, send in (late, early)]
-    rest_rows, rest_energy, rest_acc = correlate_late(late, w, phases)
-    send_a, keep_a, slide = correlate_early(early, w, norm, (rest_rows, rest_energy, rest_acc), phases, devices)
+    rest_rows, rest_acc = correlate_late(late, w, phases)
+    energy = early_energy, late_energy
+    send_a, keep_a, slide = correlate_early(early, w, norm, energy, (rest_rows, rest_acc), phases, devices)
     send_b, keep_b = correlate_rest(slide, w, rest_acc, half // phases, phases, devices)
 
     mine, other = halves(*scattered(keep_a, send_a, steps, [send_b]), phases)

time: 50.1 us -> 49.4 us (0.986)
  waiting for transfers between devices: 11.8 us -> 9.84 us
  Pallas kernels: 12 us -> 13.6 us
    pallas_call x0 -> x2, Pallas kernels: none -> 2.17 us  [energy_of(): pl.pallas_call(lambda *refs: energy_kernel(*refs, phases=phases), out_sha...]
    ppermute x12, waiting for transfers between devices: 10.8 us -> 8.72 us  [exchange(): lax.ppermute(value, 'win', [(d, d ^ 1 ^ orders[panel_of(d, devices)][step...]
    ppermute x12, starting transfers between devices: 22.4 us -> 21.3 us  [exchange(): lax.ppermute(value, 'win', [(d, d ^ 1 ^ orders[panel_of(d, devices)][step...]
    ppermute x5, starting transfers between devices: 2.87 us -> 3.55 us  [sibling(): return lax.ppermute(value, 'win', [(d, d ^ 1) for d in range(devices)])]
  transfers between devices with their start and end apart: 17 -> 17, of which waited for: 11 -> 10; matrix products, arithmetic and copies ran while one was open for 0% -> 0% of each run, Pallas kernels for 16% -> 20%
where the time goes in v5:
time: 49.4 us; the launch traced here: 49.2 us
  starting transfers between devices  24.9 us (50%)
  Pallas kernels  13.6 us (28%)
  waiting for transfers between devices  9.84 us (20%)
  local copies, waits for them, and re-layouts  0.75 us (2%)
    ppermute x12, starting transfers between devices, exchange(): lax.ppermute(value, 'win', [(d, d ^ 1 ^ orders[panel_of(d, devices)][step...  21.3 us
    ppermute x12, waiting for transfers between devices, exchange(): lax.ppermute(value, 'win', [(d, d ^ 1 ^ orders[panel_of(d, devices)][step...  8.72 us
    ppermute x5, starting transfers between devices, sibling(): return lax.ppermute(value, 'win', [(d, d ^ 1) for d in range(devices)])  3.55 us
    pallas_call x1, Pallas kernels, correlate_late(): pl.pallas_call(lambda *refs: late_kernel(*refs, phases=phases), out_shape...  2.99 us
    pallas_call x1, Pallas kernels, shifted(): pl.pallas_call(lambda *refs: shift_kernel(*refs, phases=phases, devices=2...  2.27 us
    pallas_call x2, Pallas kernels, energy_of(): pl.pallas_call(lambda *refs: energy_kernel(*refs, phases=phases), out_sha...  2.17 us
    pallas_call x1, Pallas kernels, correlate_early(): pl.pallas_call(lambda *refs: early_kernel(*refs, phases=phases, devices=d...  1.99 us
    pallas_call x1, Pallas kernels, correlate_rest(): pl.pallas_call(lambda *refs: rest_kernel(*refs, phases=phases, devices=de...  1.34 us
  transfers between devices with their start and end apart: 17, of which 10 were waited for; matrix products, arithmetic and copies ran while one was open for 0% of the time, Pallas kernels for 20%

profile of v5, /device:TPU:0, one launch (start us, length us, event | category | flops | bytes accessed | tf_op | source)
XLA Modules:
  0.0 49.2 jit_solution(6042312667348399037)
XLA Ops:
  0.0 0.7 %copy-done.2 = s32[2]{0:T(128)S(1)} copy-done((s32[2]{0:T(128)S(1)}, s32[2]{0:T(128)}, u32[]{:S(2)}) %copy-start.2) | copy-done | bytes 32
  0.7 0.6 %masks.1.refs_1_ = bf16[256,128]{1,0:T(8,128)(2,1)S(1)} custom-call(s32[2]{0:T(128)S(1)} %copy-done.2), custom_call_target="tpu_custom_call" | custom-call | flops 2147483648 | bytes 65536 | tf_op jit(solution)/shard_map/masks/pallas_call | solution.py:513
  1.3 0.0 copy-start
  1.3 0.4 select.2
  1.8 0.5 %collective-permute-start.1 = (bf16[128,2048]{1,0:T(8,128)(2,1)S(1)}, bf16[128,2048]{1,0:T(8,128)(2,1)S(1)}, u32[]{:S(2)}, u32[]{:S(2)}) collective-permute-start(bf16[128,2048]{1,0:T(8,128)(2,1)S(1)} %get-tuple-element.49.refs_2_), channel_id=1, source_target_pairs={{0,1},{1,0},{2,3},{3,2},{4,5},{5,4},{6,7},{7,6},{8,9},{9,8},{10,11... | collective-permute-start | bytes 1572872 | tf_op jit(solution)/shard_map/ppermute | solution.py:578
  2.3 0.4 select.3
  2.7 0.1 collective-permute-start
  2.9 0.5 %collective-permute-start.3 = (bf16[512,512]{1,0:T(8,128)(2,1)S(1)}, bf16[512,512]{1,0:T(8,128)(2,1)S(1)}, u32[]{:S(2)}, u32[]{:S(2)}) collective-permute-start(bf16[512,512]{1,0:T(8,128)(2,1)S(1)} %give.1), channel_id=1, source_target_pairs={{0,1},{1,0},{2,3},{3,2},{4,5},{5,4},{6,7},{7,6},{8,9},{9,8},{10,11... | collective-permute-start | bytes 1572872 | tf_op jit(solution)/shard_map/ppermute | solution.py:578
  3.4 0.4 collective-permute-done.1.got_ref
  3.8 0.1 add.10
  3.9 2.7 %collective-permute-start.4 = (bf16[64,2048]{1,0:T(8,128)(2,1)S(1)}, bf16[64,2048]{1,0:T(8,128)(2,1)S(1)}, u32[]{:S(2)}, u32[]{:S(2)}) collective-permute-start(bf16[64,2048]{1,0:T(8,128)(2,1)S(1)} %get-tuple-element.56.refs_1_), channel_id=1, source_target_pairs={{0,3},{1,4},{2,7},{3,0},{4,1},{5,6},{6,5},{7,2},{8,13},{9,10},{10,... | collective-permute-start | bytes 786440 | tf_op jit(solution)/shard_map/ppermute | solution.py:581
  6.5 0.0 collective-permute-done.got_ref
  6.5 0.1 add.11
  6.6 0.8 %collective-permute-start.2 = (bf16[64,2048]{1,0:T(8,128)(2,1)S(1)}, bf16[64,2048]{1,0:T(8,128)(2,1)S(1)}, u32[]{:S(2)}, u32[]{:S(2)}) collective-permute-start(bf16[64,2048]{1,0:T(8,128)(2,1)S(1)} %get-tuple-element.55.refs_1_), channel_id=1, source_target_pairs={{0,3},{1,4},{2,7},{3,0},{4,1},{5,6},{6,5},{7,2},{8,13},{9,10},{10,... | collective-permute-start | bytes 786440 | tf_op jit(solution)/shard_map/ppermute | solution.py:581
  7.4 0.0 collective-permute-done.3.refs_1_
  7.4 2.3 %shift_templates.1 = (bf16[1,8576,128]{2,1,0:T(8,128)(2,1)S(1)}, f32[8,128]{1,0:T(8,128)S(1)}) custom-call(bf16[2,512,512]{2,1,0:T(8,128)(2,1)S(1)} %bitcast.2, bf16[512,512]{1,0:T(8,128)(2,1)S(1)} %collective-permute-done.3.refs_1_, bf16[64,2048]{1,0:T(8,128)(2,1)S(1)} %get-tuple-element.54.refs_2_.refs_0_.kept_ref), custom_call_target="tpu_custom_call" | custom-call | flops 268435456 | bytes 1048576 | tf_op jit(solution)/shard_map/shift_templates/pallas_call | solution.py:107
  9.7 1.0 %energy.2 = (f32[256,128]{1,0:T(8,128)S(1)}, f32[256,128]{1,0:T(8,128)S(1)}) custom-call(bf16[64,2048]{1,0:T(8,128)(2,1)S(1)} %get-tuple-element.53.refs_0_.kept_ref, bf16[64,2048]{1,0:T(8,128)(2,1)S(1)} %get-tuple-element.56.refs_1_, f32[8,128]{1,0:T(8,128)S(1)} %get-tuple-element.57.refs_2_.refs_3_), custom_call_target="tpu_custom_call" | custom-call | flops 268435456 | bytes 1048576 | tf_op jit(solution)/shard_map/energy/pallas_call | solution.py:199
  10.7 0.0 collective-permute-done.4.got_ref
  10.7 2.1 %collective-permute-start.7 = (bf16[32,2048]{1,0:T(8,128)(2,1)S(1)}, bf16[32,2048]{1,0:T(8,128)(2,1)S(1)}, u32[]{:S(2)}, u32[]{:S(2)}) collective-permute-start(bf16[32,2048]{1,0:T(8,128)(2,1)S(1)} %get-tuple-element.67), channel_id=1, source_target_pairs={{0,5},{1,2},{2,1},{3,6},{4,7},{5,0},{6,3},{7,4},{8,11},{9,12},{10,... | collective-permute-start | bytes 393224 | tf_op jit(solution)/shard_map/ppermute | solution.py:581
  12.8 1.2 %energy.3 = (f32[256,128]{1,0:T(8,128)S(1)}, f32[256,128]{1,0:T(8,128)}) custom-call(bf16[64,2048]{1,0:T(8,128)(2,1)S(1)} %get-tuple-element.54.refs_2_.refs_0_.kept_ref, bf16[64,2048]{1,0:T(8,128)(2,1)S(1)} %get-tuple-element.55.refs_1_, f32[256,128]{1,0:T(8,128)S(1)} %get-tuple-element.58.refs_2_, bf16[32,2048]{1,0:T(8,128)(2,1)S(1)} %get-tuple-element.60.refs_3_.kept_ref), custom_call_target="tpu_custom_call" | custom-call | flops 268435456 | bytes 1048576 | tf_op jit(solution)/shard_map/energy/pallas_call | solution.py:199
  14.0 0.0 collective-permute-done.2.got_ref
  14.0 1.3 %collective-permute-start.5 = (bf16[32,2048]{1,0:T(8,128)(2,1)S(1)}, bf16[32,2048]{1,0:T(8,128)(2,1)S(1)}, u32[]{:S(2)}, u32[]{:S(2)}) collective-permute-start(bf16[32,2048]{1,0:T(8,128)(2,1)S(1)} %get-tuple-element.63), channel_id=1, source_target_pairs={{0,5},{1,2},{2,1},{3,6},{4,7},{5,0},{6,3},{7,4},{8,11},{9,12},{10,... | collective-permute-start | bytes 393224 | tf_op jit(solution)/shard_map/ppermute | solution.py:581
  15.3 0.1 collective-permute-done.7.got_ref
  15.5 2.8 %collective-permute-start.8 = (bf16[16,2048]{1,0:T(8,128)(2,1)S(1)}, bf16[16,2048]{1,0:T(8,128)(2,1)S(1)}, u32[]{:S(2)}, u32[]{:S(2)}) collective-permute-start(bf16[16,2048]{1,0:T(8,128)(2,1)S(1)} %get-tuple-element.69), channel_id=1, source_target_pairs={{0,9},{1,8},{2,11},{3,10},{4,13},{5,12},{6,15},{7,14},{8,1},{9,0},... | collective-permute-start | bytes 196616 | tf_op jit(solution)/shard_map/ppermute | solution.py:581
  18.3 0.2 collective-permute-done.5.got_ref
  18.5 2.4 %collective-permute-start.6 = (bf16[16,2048]{1,0:T(8,128)(2,1)S(1)}, bf16[16,2048]{1,0:T(8,128)(2,1)S(1)}, u32[]{:S(2)}, u32[]{:S(2)}) collective-permute-start(bf16[16,2048]{1,0:T(8,128)(2,1)S(1)} %get-tuple-element.65), channel_id=1, source_target_pairs={{0,9},{1,8},{2,11},{3,10},{4,13},{5,12},{6,15},{7,14},{8,1},{9,0},... | collective-permute-start | bytes 196616 | tf_op jit(solution)/shard_map/ppermute | solution.py:581
  20.9 0.0 collective-permute-done.8.refs_1_
  20.9 3.0 %correlate_late.1 = (f32[256,128]{1,0:T(8,128)S(1)}, f32[256,512]{1,0:T(8,128)S(1)}) custom-call(bf16[16,2048]{1,0:T(8,128)(2,1)S(1)} %get-tuple-element.68.refs_0_, bf16[16,2048]{1,0:T(8,128)(2,1)S(1)} %collective-permute-done.8.refs_1_, bf16[1,8576,128]{2,1,0:T(8,128)(2,1)S(1)} %get-tuple-element.66.refs_2_.refs_1_), custom_call_target="tpu_custom_call" | custom-call | flops 2147483648 | bytes 4194304 | tf_op jit(solution)/shard_map/correlate_late/pallas_call | solution.py:311
  23.9 1.1 %collective-permute-done.6.refs_1_ = bf16[16,2048]{1,0:T(8,128)(2,1)S(1)} collective-permute-done((bf16[16,2048]{1,0:T(8,128)(2,1)S(1)}, bf16[16,2048]{1,0:T(8,128)(2,1)S(1)}, u32[]{:S(2)}, u32[]{:S(2)}) %collective-permute-start.6) | collective-permute-done | bytes 65568 | tf_op jit(solution)/shard_map/ppermute | solution.py:581
  25.0 2.0 %correlate_early.1 = (f32[4,136,128]{2,1,0:T(8,128)S(1)}, f32[4,136,128]{2,1,0:T(8,128)S(1)}, bf16[8,320,256]{2,1,0:T(8,128)(2,1)S(1)}) custom-call(bf16[16,2048]{1,0:T(8,128)(2,1)S(1)} %get-tuple-element.64.refs_0_, bf16[16,2048]{1,0:T(8,128)(2,1)S(1)} %collective-permute-done.6.refs_1_, bf16[1,8576,128]{2,1,0:T(8,128)(2,1)S(1)} %get-tuple-element.66.refs_2_.refs_1_, ...), custom_call_target="tpu_custom_call" | custom-call | flops 4294967296 | bytes 16777216 | tf_op jit(solution)/shard_map/correlate_early/pallas_call | solution.py:337
  27.0 1.5 %collective-permute-start.9 = (f32[4,136,128]{2,1,0:T(8,128)S(1)}, f32[4,136,128]{2,1,0:T(8,128)S(1)}, u32[]{:S(2)}, u32[]{:S(2)}) collective-permute-start(f32[4,136,128]{2,1,0:T(8,128)S(1)} %get-tuple-element.73), channel_id=1, source_target_pairs={{0,3},{1,4},{2,7},{3,0},{4,1},{5,6},{6,5},{7,2},{8,13},{9,10},{10,... | collective-permute-start | bytes 835592 | tf_op jit(solution)/shard_map/ppermute | solution.py:581
  28.4 1.3 %correlate_rest.1 = (f32[4,128,128]{2,1,0:T(8,128)S(1)}, f32[4,128,128]{2,1,0:T(8,128)S(1)}) custom-call(bf16[8,320,256]{2,1,0:T(8,128)(2,1)S(1)} %get-tuple-element.74.refs_0_, bf16[1,8576,128]{2,1,0:T(8,128)(2,1)S(1)} %get-tuple-element.66.refs_2_.refs_1_, f32[256,512]{1,0:T(8,128)S(1)} %get-tuple-element.71.refs_7_.refs_2_), custom_call_target="tpu_custom_call" | custom-call | flops 8589934592 | bytes 16777216 | tf_op jit(solution)/shard_map/correlate_rest/pallas_call | solution.py:352
  29.8 0.4 collective-permute-start.13
  30.2 2.8 %collective-permute-done.9.got_ref = f32[4,136,128]{2,1,0:T(8,128)S(1)} collective-permute-done((f32[4,136,128]{2,1,0:T(8,128)S(1)}, f32[4,136,128]{2,1,0:T(8,128)S(1)}, u32[]{:S(2)}, u32[]{:S(2)}) %collective-permute-start.9) | collective-permute-done | bytes 278560 | tf_op jit(solution)/shard_map/ppermute | solution.py:581
  33.0 1.2 %collective-permute-start.10 = (f32[2,136,128]{2,1,0:T(8,128)S(1)}, f32[2,136,128]{2,1,0:T(8,128)S(1)}, u32[]{:S(2)}, u32[]{:S(2)}) collective-permute-start(f32[2,136,128]{2,1,0:T(8,128)S(1)} %get-tuple-element.77), channel_id=1, source_target_pairs={{0,5},{1,2},{2,1},{3,6},{4,7},{5,0},{6,3},{7,4},{8,11},{9,12},{10,... | collective-permute-start | bytes 417800 | tf_op jit(solution)/shard_map/ppermute | solution.py:581
  34.2 1.6 %collective-permute-done.13.got_ref = f32[4,128,128]{2,1,0:T(8,128)S(1)} collective-permute-done((f32[4,128,128]{2,1,0:T(8,128)S(1)}, f32[4,128,128]{2,1,0:T(8,128)S(1)}, u32[]{:S(2)}, u32[]{:S(2)}) %collective-permute-start.13) | collective-permute-done | bytes 262176 | tf_op jit(solution)/shard_map/ppermute | solution.py:581
  35.9 1.1 %collective-permute-start.14 = (f32[2,128,128]{2,1,0:T(8,128)S(1)}, f32[2,128,128]{2,1,0:T(8,128)S(1)}, u32[]{:S(2)}, u32[]{:S(2)}) collective-permute-start(f32[2,128,128]{2,1,0:T(8,128)S(1)} %get-tuple-element.88), channel_id=1, source_target_pairs={{0,5},{1,2},{2,1},{3,6},{4,7},{5,0},{6,3},{7,4},{8,11},{9,12},{10,... | collective-permute-start | bytes 393224 | tf_op jit(solution)/shard_map/ppermute | solution.py:581
  36.9 0.8 %collective-permute-done.10.got_ref = f32[2,136,128]{2,1,0:T(8,128)S(1)} collective-permute-done((f32[2,136,128]{2,1,0:T(8,128)S(1)}, f32[2,136,128]{2,1,0:T(8,128)S(1)}, u32[]{:S(2)}, u32[]{:S(2)}) %collective-permute-start.10) | collective-permute-done | bytes 139296 | tf_op jit(solution)/shard_map/ppermute | solution.py:581
  37.7 2.5 %collective-permute-start.11 = (f32[1,136,128]{2,1,0:T(8,128)S(1)}, f32[1,136,128]{2,1,0:T(8,128)S(1)}, u32[]{:S(2)}, u32[]{:S(2)}) collective-permute-start(f32[1,136,128]{2,1,0:T(8,128)S(1)} %get-tuple-element.79), channel_id=1, source_target_pairs={{0,9},{1,8},{2,11},{3,10},{4,13},{5,12},{6,15},{7,14},{8,1},{9,0},... | collective-permute-start | bytes 208904 | tf_op jit(solution)/shard_map/ppermute | solution.py:581
  40.2 0.1 collective-permute-done.14.got_ref
  40.3 2.6 %collective-permute-start.15 = (f32[1,128,128]{2,1,0:T(8,128)S(1)}, f32[1,128,128]{2,1,0:T(8,128)S(1)}, u32[]{:S(2)}, u32[]{:S(2)}) collective-permute-start(f32[1,128,128]{2,1,0:T(8,128)S(1)} %get-tuple-element.90), channel_id=1, source_target_pairs={{0,9},{1,8},{2,11},{3,10},{4,13},{5,12},{6,15},{7,14},{8,1},{9,0},... | collective-permute-start | bytes 196616 | tf_op jit(solution)/shard_map/ppermute | solution.py:581
  42.9 0.0 collective-permute-done.11.refs_1_
  42.9 2.2 %collective-permute-start.12 = (f32[72,128]{1,0:T(8,128)S(1)}, f32[72,128]{1,0:T(8,128)S(1)}, u32[]{:S(2)}, u32[]{:S(2)}) collective-permute-start(f32[72,128]{1,0:T(8,128)S(1)} %get-tuple-element.81), channel_id=1, source_target_pairs={{0,1},{1,0},{2,3},{3,2},{4,5},{5,4},{6,7},{7,6},{8,9},{9,8},{10,11... | collective-permute-start | bytes 110600 | tf_op jit(solution)/shard_map/ppermute | solution.py:578
  45.1 2.1 %collective-permute-done.15.refs_1_ = f32[1,128,128]{2,1,0:T(8,128)S(1)} collective-permute-done((f32[1,128,128]{2,1,0:T(8,128)S(1)}, f32[1,128,128]{2,1,0:T(8,128)S(1)}, u32[]{:S(2)}, u32[]{:S(2)}) %collective-permute-start.15) | collective-permute-done | bytes 65568 | tf_op jit(solution)/shard_map/ppermute | solution.py:581
  47.2 0.2 collective-permute-start.16
  47.4 0.3 scale.1
  47.8 0.7 %collective-permute-done.16.refs_5_ = f32[64,128]{1,0:T(8,128)S(1)} collective-permute-done((f32[64,128]{1,0:T(8,128)S(1)}, f32[64,128]{1,0:T(8,128)S(1)}, u32[]{:S(2)}, u32[]{:S(2)}) %collective-permute-start.16) | collective-permute-done | bytes 32800 | tf_op jit(solution)/shard_map/ppermute | solution.py:578
  48.5 0.8 %finish.1 = f32[256,128]{1,0:T(8,128)} custom-call(f32[64,128]{1,0:T(8,128)S(1)} %get-tuple-element.82.refs_0_, f32[64,128]{1,0:T(8,128)S(1)} %get-tuple-element.83.refs_1_, f32[64,128]{1,0:T(8,128)S(1)} %get-tuple-element.84.refs_2_, f32[64,128]{1,0:T(8,128)S(1)} %get-tuple-element.85.refs_3_, f32[64,128]{1,0:T(8,128)S(1)} %get-tuple-element.91.refs_4_, ...), custom_call_target="tpu_custom_call" | custom-call | flops 262144 | bytes 262144 | tf_op jit(solution)/shard_map/finish/pallas_call | solution.py:481
  (16 shorter events, 0.3 us)
Async XLA Ops:
  0.0 1.3 %copy-start.1 = (bf16[128,4096]{1,0:T(8,128)(2,1)S(1)}, bf16[128,4096]{1,0:T(8,128)(2,1)}, u32[]{:S(2)}) copy-start(bf16[128,4096]{1,0:T(8,128)(2,1)} %refs_0_.5) | copy-start | bytes 3145732
  0.0 0.7 %copy-start.2 = (s32[2]{0:T(128)S(1)}, s32[2]{0:T(128)}, u32[]{:S(2)}) copy-start(s32[2]{0:T(128)} %refs_0_.3) | copy-start | bytes 28
  1.3 1.5 %copy-start = (bf16[2,64,8,512]{3,2,1,0:T(8,128)(2,1)S(1)}, bf16[2,64,8,512]{3,2,1,0:T(8,128)(2,1)}, u32[]{:S(2)}) copy-start(bf16[2,64,8,512]{3,2,1,0:T(8,128)(2,1)} %param.4) | copy-start | bytes 3145732
  1.8 2.1 %collective-permute-start.1 = (bf16[128,2048]{1,0:T(8,128)(2,1)S(1)}, bf16[128,2048]{1,0:T(8,128)(2,1)S(1)}, u32[]{:S(2)}, u32[]{:S(2)}) collective-permute-start(bf16[128,2048]{1,0:T(8,128)(2,1)S(1)} %get-tuple-element.49.refs_2_), channel_id=1, source_target_pairs={{0,1},{1,0},{2,3},{3,2},{4,5},{5,4},{6,7},{7,6},{8,9},{9,8},{10,11... | collective-permute-start | bytes 1572872 | tf_op jit(solution)/shard_map/ppermute | solution.py:578
  2.7 3.8 %collective-permute-start = (bf16[128,2048]{1,0:T(8,128)(2,1)S(1)}, bf16[128,2048]{1,0:T(8,128)(2,1)S(1)}, u32[]{:S(2)}, u32[]{:S(2)}) collective-permute-start(bf16[128,2048]{1,0:T(8,128)(2,1)S(1)} %get-tuple-element.51.refs_1_), channel_id=1, source_target_pairs={{0,1},{1,0},{2,3},{3,2},{4,5},{5,4},{6,7},{7,6},{8,9},{9,8},{10,11... | collective-permute-start | bytes 1572872 | tf_op jit(solution)/shard_map/ppermute | solution.py:578
  2.9 4.5 %collective-permute-start.3 = (bf16[512,512]{1,0:T(8,128)(2,1)S(1)}, bf16[512,512]{1,0:T(8,128)(2,1)S(1)}, u32[]{:S(2)}, u32[]{:S(2)}) collective-permute-start(bf16[512,512]{1,0:T(8,128)(2,1)S(1)} %give.1), channel_id=1, source_target_pairs={{0,1},{1,0},{2,3},{3,2},{4,5},{5,4},{6,7},{7,6},{8,9},{9,8},{10,11... | collective-permute-start | bytes 1572872 | tf_op jit(solution)/shard_map/ppermute | solution.py:578
  3.9 6.8 %collective-permute-start.4 = (bf16[64,2048]{1,0:T(8,128)(2,1)S(1)}, bf16[64,2048]{1,0:T(8,128)(2,1)S(1)}, u32[]{:S(2)}, u32[]{:S(2)}) collective-permute-start(bf16[64,2048]{1,0:T(8,128)(2,1)S(1)} %get-tuple-element.56.refs_1_), channel_id=1, source_target_pairs={{0,3},{1,4},{2,7},{3,0},{4,1},{5,6},{6,5},{7,2},{8,13},{9,10},{10,... | collective-permute-start | bytes 786440 | tf_op jit(solution)/shard_map/ppermute | solution.py:581
  6.6 7.4 %collective-permute-start.2 = (bf16[64,2048]{1,0:T(8,128)(2,1)S(1)}, bf16[64,2048]{1,0:T(8,128)(2,1)S(1)}, u32[]{:S(2)}, u32[]{:S(2)}) collective-permute-start(bf16[64,2048]{1,0:T(8,128)(2,1)S(1)} %get-tuple-element.55.refs_1_), channel_id=1, source_target_pairs={{0,3},{1,4},{2,7},{3,0},{4,1},{5,6},{6,5},{7,2},{8,13},{9,10},{10,... | collective-permute-start | bytes 786440 | tf_op jit(solution)/shard_map/ppermute | solution.py:581
  10.7 4.7 %collective-permute-start.7 = (bf16[32,2048]{1,0:T(8,128)(2,1)S(1)}, bf16[32,2048]{1,0:T(8,128)(2,1)S(1)}, u32[]{:S(2)}, u32[]{:S(2)}) collective-permute-start(bf16[32,2048]{1,0:T(8,128)(2,1)S(1)} %get-tuple-element.67), channel_id=1, source_target_pairs={{0,5},{1,2},{2,1},{3,6},{4,7},{5,0},{6,3},{7,4},{8,11},{9,12},{10,... | collective-permute-start | bytes 393224 | tf_op jit(solution)/shard_map/ppermute | solution.py:581
  14.0 4.5 %collective-permute-start.5 = (bf16[32,2048]{1,0:T(8,128)(2,1)S(1)}, bf16[32,2048]{1,0:T(8,128)(2,1)S(1)}, u32[]{:S(2)}, u32[]{:S(2)}) collective-permute-start(bf16[32,2048]{1,0:T(8,128)(2,1)S(1)} %get-tuple-element.63), channel_id=1, source_target_pairs={{0,5},{1,2},{2,1},{3,6},{4,7},{5,0},{6,3},{7,4},{8,11},{9,12},{10,... | collective-permute-start | bytes 393224 | tf_op jit(solution)/shard_map/ppermute | solution.py:581
  15.5 5.4 %collective-permute-start.8 = (bf16[16,2048]{1,0:T(8,128)(2,1)S(1)}, bf16[16,2048]{1,0:T(8,128)(2,1)S(1)}, u32[]{:S(2)}, u32[]{:S(2)}) collective-permute-start(bf16[16,2048]{1,0:T(8,128)(2,1)S(1)} %get-tuple-element.69), channel_id=1, source_target_pairs={{0,9},{1,8},{2,11},{3,10},{4,13},{5,12},{6,15},{7,14},{8,1},{9,0},... | collective-permute-start | bytes 196616 | tf_op jit(solution)/shard_map/ppermute | solution.py:581
  18.5 6.5 %collective-permute-start.6 = (bf16[16,2048]{1,0:T(8,128)(2,1)S(1)}, bf16[16,2048]{1,0:T(8,128)(2,1)S(1)}, u32[]{:S(2)}, u32[]{:S(2)}) collective-permute-start(bf16[16,2048]{1,0:T(8,128)(2,1)S(1)} %get-tuple-element.65), channel_id=1, source_target_pairs={{0,9},{1,8},{2,11},{3,10},{4,13},{5,12},{6,15},{7,14},{8,1},{9,0},... | collective-permute-start | bytes 196616 | tf_op jit(solution)/shard_map/ppermute | solution.py:581
  27.0 6.0 %collective-permute-start.9 = (f32[4,136,128]{2,1,0:T(8,128)S(1)}, f32[4,136,128]{2,1,0:T(8,128)S(1)}, u32[]{:S(2)}, u32[]{:S(2)}) collective-permute-start(f32[4,136,128]{2,1,0:T(8,128)S(1)} %get-tuple-element.73), channel_id=1, source_target_pairs={{0,3},{1,4},{2,7},{3,0},{4,1},{5,6},{6,5},{7,2},{8,13},{9,10},{10,... | collective-permute-start | bytes 835592 | tf_op jit(solution)/shard_map/ppermute | solution.py:581
  29.8 6.0 %collective-permute-start.13 = (f32[4,128,128]{2,1,0:T(8,128)S(1)}, f32[4,128,128]{2,1,0:T(8,128)S(1)}, u32[]{:S(2)}, u32[]{:S(2)}) collective-permute-start(f32[4,128,128]{2,1,0:T(8,128)S(1)} %get-tuple-element.75.refs_0_), channel_id=1, source_target_pairs={{0,3},{1,4},{2,7},{3,0},{4,1},{5,6},{6,5},{7,2},{8,13},{9,10},{10,... | collective-permute-start | bytes 786440 | tf_op jit(solution)/shard_map/ppermute | solution.py:581
  33.0 4.7 %collective-permute-start.10 = (f32[2,136,128]{2,1,0:T(8,128)S(1)}, f32[2,136,128]{2,1,0:T(8,128)S(1)}, u32[]{:S(2)}, u32[]{:S(2)}) collective-permute-start(f32[2,136,128]{2,1,0:T(8,128)S(1)} %get-tuple-element.77), channel_id=1, source_target_pairs={{0,5},{1,2},{2,1},{3,6},{4,7},{5,0},{6,3},{7,4},{8,11},{9,12},{10,... | collective-permute-start | bytes 417800 | tf_op jit(solution)/shard_map/ppermute | solution.py:581
  35.9 4.5 %collective-permute-start.14 = (f32[2,128,128]{2,1,0:T(8,128)S(1)}, f32[2,128,128]{2,1,0:T(8,128)S(1)}, u32[]{:S(2)}, u32[]{:S(2)}) collective-permute-start(f32[2,128,128]{2,1,0:T(8,128)S(1)} %get-tuple-element.88), channel_id=1, source_target_pairs={{0,5},{1,2},{2,1},{3,6},{4,7},{5,0},{6,3},{7,4},{8,11},{9,12},{10,... | collective-permute-start | bytes 393224 | tf_op jit(solution)/shard_map/ppermute | solution.py:581
  37.7 5.2 %collective-permute-start.11 = (f32[1,136,128]{2,1,0:T(8,128)S(1)}, f32[1,136,128]{2,1,0:T(8,128)S(1)}, u32[]{:S(2)}, u32[]{:S(2)}) collective-permute-start(f32[1,136,128]{2,1,0:T(8,128)S(1)} %get-tuple-element.79), channel_id=1, source_target_pairs={{0,9},{1,8},{2,11},{3,10},{4,13},{5,12},{6,15},{7,14},{8,1},{9,0},... | collective-permute-start | bytes 208904 | tf_op jit(solution)/shard_map/ppermute | solution.py:581
  40.3 6.8 %collective-permute-start.15 = (f32[1,128,128]{2,1,0:T(8,128)S(1)}, f32[1,128,128]{2,1,0:T(8,128)S(1)}, u32[]{:S(2)}, u32[]{:S(2)}) collective-permute-start(f32[1,128,128]{2,1,0:T(8,128)S(1)} %get-tuple-element.90), channel_id=1, source_target_pairs={{0,9},{1,8},{2,11},{3,10},{4,13},{5,12},{6,15},{7,14},{8,1},{9,0},... | collective-permute-start | bytes 196616 | tf_op jit(solution)/shard_map/ppermute | solution.py:581
  42.9 4.5 %collective-permute-start.12 = (f32[72,128]{1,0:T(8,128)S(1)}, f32[72,128]{1,0:T(8,128)S(1)}, u32[]{:S(2)}, u32[]{:S(2)}) collective-permute-start(f32[72,128]{1,0:T(8,128)S(1)} %get-tuple-element.81), channel_id=1, source_target_pairs={{0,1},{1,0},{2,3},{3,2},{4,5},{5,4},{6,7},{7,6},{8,9},{9,8},{10,11... | collective-permute-start | bytes 110600 | tf_op jit(solution)/shard_map/ppermute | solution.py:578
  47.2 1.3 %collective-permute-start.16 = (f32[64,128]{1,0:T(8,128)S(1)}, f32[64,128]{1,0:T(8,128)S(1)}, u32[]{:S(2)}, u32[]{:S(2)}) collective-permute-start(f32[64,128]{1,0:T(8,128)S(1)} %get-tuple-element.92), channel_id=1, source_target_pairs={{0,1},{1,0},{2,3},{3,2},{4,5},{5,4},{6,7},{7,6},{8,9},{9,8},{10,11... | collective-permute-start | bytes 98312 | tf_op jit(solution)/shard_map/ppermute | solution.py:578

commit v6 on v5

--- a/solution.py
+++ b/solution.py
@@ -77,10 +77,11 @@
     )
     norm = jnp.zeros((1, LANES), f32)
     width = min(2, each) * LANES
-    row, lane = iota((gc, width), 0), iota((gc, width), 1)
+    lane = iota((gc, width), 1)
+    offset = iota((gc, width), 0) - lane % groups * each - lane // LANES
     for side, ref in enumerate((templates_ref.at[panel], other_ref)):
         for c in range(0, each, width // LANES):
-            choose = (row == (lane % groups) * each + c + lane // LANES).astype(f32).astype(bf16)
+            choose = (offset == c).astype(f32).astype(bf16)
             piece = dot(ref[...], choose, (((0,), (0,)), ((), ())))
             for i in range(width // LANES):
                 one = piece[:, i * LANES : (i + 1) * LANES]

time: 49.4 us -> 49.4 us (level)
  no operation moved by 1% of the time
where the time goes in v6:
time: 49.4 us; the launch traced here: 49.2 us
  starting transfers between devices  24.9 us (50%)
  Pallas kernels  13.6 us (28%)
  waiting for transfers between devices  9.84 us (20%)
  local copies, waits for them, and re-layouts  0.75 us (2%)
    ppermute x12, starting transfers between devices, exchange(): lax.ppermute(value, 'win', [(d, d ^ 1 ^ orders[panel_of(d, devices)][step...  21.3 us
    ppermute x12, waiting for transfers between devices, exchange(): lax.ppermute(value, 'win', [(d, d ^ 1 ^ orders[panel_of(d, devices)][step...  8.72 us
    ppermute x5, starting transfers between devices, sibling(): return lax.ppermute(value, 'win', [(d, d ^ 1) for d in range(devices)])  3.55 us
    pallas_call x1, Pallas kernels, correlate_late(): pl.pallas_call(lambda *refs: late_kernel(*refs, phases=phases), out_shape...  2.99 us
    pallas_call x1, Pallas kernels, shifted(): pl.pallas_call(lambda *refs: shift_kernel(*refs, phases=phases, devices=2...  2.24 us
    pallas_call x2, Pallas kernels, energy_of(): pl.pallas_call(lambda *refs: energy_kernel(*refs, phases=phases), out_sha...  2.17 us
    pallas_call x1, Pallas kernels, correlate_early(): pl.pallas_call(lambda *refs: early_kernel(*refs, phases=phases, devices=d...  1.99 us
    pallas_call x1, Pallas kernels, correlate_rest(): pl.pallas_call(lambda *refs: rest_kernel(*refs, phases=phases, devices=de...  1.34 us
  transfers between devices with their start and end apart: 17, of which 10 were waited for; matrix products, arithmetic and copies ran while one was open for 0% of the time, Pallas kernels for 20%

profile of v6, /device:TPU:0, one launch (start us, length us, event | category | flops | bytes accessed | tf_op | source)
XLA Modules:
  0.0 49.2 jit_solution(2663846476898809127)
XLA Ops:
  0.0 0.7 %copy-done.2 = s32[2]{0:T(128)S(1)} copy-done((s32[2]{0:T(128)S(1)}, s32[2]{0:T(128)}, u32[]{:S(2)}) %copy-start.2) | copy-done | bytes 32
  0.7 0.6 %masks.1.refs_1_ = bf16[256,128]{1,0:T(8,128)(2,1)S(1)} custom-call(s32[2]{0:T(128)S(1)} %copy-done.2), custom_call_target="tpu_custom_call" | custom-call | flops 2147483648 | bytes 65536 | tf_op jit(solution)/shard_map/masks/pallas_call | solution.py:514
  1.3 0.0 copy-start
  1.3 0.4 select.2
  1.8 0.5 %collective-permute-start.1 = (bf16[128,2048]{1,0:T(8,128)(2,1)S(1)}, bf16[128,2048]{1,0:T(8,128)(2,1)S(1)}, u32[]{:S(2)}, u32[]{:S(2)}) collective-permute-start(bf16[128,2048]{1,0:T(8,128)(2,1)S(1)} %get-tuple-element.49.refs_2_), channel_id=1, source_target_pairs={{0,1},{1,0},{2,3},{3,2},{4,5},{5,4},{6,7},{7,6},{8,9},{9,8},{10,11... | collective-permute-start | bytes 1572872 | tf_op jit(solution)/shard_map/ppermute | solution.py:579
  2.3 0.4 select.3
  2.7 0.1 collective-permute-start
  2.9 0.5 %collective-permute-start.3 = (bf16[512,512]{1,0:T(8,128)(2,1)S(1)}, bf16[512,512]{1,0:T(8,128)(2,1)S(1)}, u32[]{:S(2)}, u32[]{:S(2)}) collective-permute-start(bf16[512,512]{1,0:T(8,128)(2,1)S(1)} %give.1), channel_id=1, source_target_pairs={{0,1},{1,0},{2,3},{3,2},{4,5},{5,4},{6,7},{7,6},{8,9},{9,8},{10,11... | collective-permute-start | bytes 1572872 | tf_op jit(solution)/shard_map/ppermute | solution.py:579
  3.4 0.4 collective-permute-done.1.got_ref
  3.8 0.1 add.10
  3.9 2.7 %collective-permute-start.4 = (bf16[64,2048]{1,0:T(8,128)(2,1)S(1)}, bf16[64,2048]{1,0:T(8,128)(2,1)S(1)}, u32[]{:S(2)}, u32[]{:S(2)}) collective-permute-start(bf16[64,2048]{1,0:T(8,128)(2,1)S(1)} %get-tuple-element.56.refs_1_), channel_id=1, source_target_pairs={{0,3},{1,4},{2,7},{3,0},{4,1},{5,6},{6,5},{7,2},{8,13},{9,10},{10,... | collective-permute-start | bytes 786440 | tf_op jit(solution)/shard_map/ppermute | solution.py:582
  6.5 0.0 collective-permute-done.got_ref
  6.5 0.1 add.11
  6.6 0.8 %collective-permute-start.2 = (bf16[64,2048]{1,0:T(8,128)(2,1)S(1)}, bf16[64,2048]{1,0:T(8,128)(2,1)S(1)}, u32[]{:S(2)}, u32[]{:S(2)}) collective-permute-start(bf16[64,2048]{1,0:T(8,128)(2,1)S(1)} %get-tuple-element.55.refs_1_), channel_id=1, source_target_pairs={{0,3},{1,4},{2,7},{3,0},{4,1},{5,6},{6,5},{7,2},{8,13},{9,10},{10,... | collective-permute-start | bytes 786440 | tf_op jit(solution)/shard_map/ppermute | solution.py:582
  7.4 0.0 collective-permute-done.3.refs_1_
  7.4 2.2 %shift_templates.1 = (bf16[1,8576,128]{2,1,0:T(8,128)(2,1)S(1)}, f32[8,128]{1,0:T(8,128)S(1)}) custom-call(bf16[2,512,512]{2,1,0:T(8,128)(2,1)S(1)} %bitcast.2, bf16[512,512]{1,0:T(8,128)(2,1)S(1)} %collective-permute-done.3.refs_1_, bf16[64,2048]{1,0:T(8,128)(2,1)S(1)} %get-tuple-element.54.refs_2_.refs_0_.kept_ref), custom_call_target="tpu_custom_call" | custom-call | flops 268435456 | bytes 1048576 | tf_op jit(solution)/shard_map/shift_templates/pallas_call | solution.py:108
  9.7 1.0 %energy.2 = (f32[256,128]{1,0:T(8,128)S(1)}, f32[256,128]{1,0:T(8,128)S(1)}) custom-call(bf16[64,2048]{1,0:T(8,128)(2,1)S(1)} %get-tuple-element.53.refs_0_.kept_ref, bf16[64,2048]{1,0:T(8,128)(2,1)S(1)} %get-tuple-element.56.refs_1_, f32[8,128]{1,0:T(8,128)S(1)} %get-tuple-element.57.refs_2_.refs_3_), custom_call_target="tpu_custom_call" | custom-call | flops 268435456 | bytes 1048576 | tf_op jit(solution)/shard_map/energy/pallas_call | solution.py:200
  10.7 0.0 collective-permute-done.4.got_ref
  10.7 2.1 %collective-permute-start.7 = (bf16[32,2048]{1,0:T(8,128)(2,1)S(1)}, bf16[32,2048]{1,0:T(8,128)(2,1)S(1)}, u32[]{:S(2)}, u32[]{:S(2)}) collective-permute-start(bf16[32,2048]{1,0:T(8,128)(2,1)S(1)} %get-tuple-element.67), channel_id=1, source_target_pairs={{0,5},{1,2},{2,1},{3,6},{4,7},{5,0},{6,3},{7,4},{8,11},{9,12},{10,... | collective-permute-start | bytes 393224 | tf_op jit(solution)/shard_map/ppermute | solution.py:582
  12.8 1.2 %energy.3 = (f32[256,128]{1,0:T(8,128)S(1)}, f32[256,128]{1,0:T(8,128)}) custom-call(bf16[64,2048]{1,0:T(8,128)(2,1)S(1)} %get-tuple-element.54.refs_2_.refs_0_.kept_ref, bf16[64,2048]{1,0:T(8,128)(2,1)S(1)} %get-tuple-element.55.refs_1_, f32[256,128]{1,0:T(8,128)S(1)} %get-tuple-element.58.refs_2_, bf16[32,2048]{1,0:T(8,128)(2,1)S(1)} %get-tuple-element.60.refs_3_.kept_ref), custom_call_target="tpu_custom_call" | custom-call | flops 268435456 | bytes 1048576 | tf_op jit(solution)/shard_map/energy/pallas_call | solution.py:200
  14.0 0.0 collective-permute-done.2.got_ref
  14.0 1.3 %collective-permute-start.5 = (bf16[32,2048]{1,0:T(8,128)(2,1)S(1)}, bf16[32,2048]{1,0:T(8,128)(2,1)S(1)}, u32[]{:S(2)}, u32[]{:S(2)}) collective-permute-start(bf16[32,2048]{1,0:T(8,128)(2,1)S(1)} %get-tuple-element.63), channel_id=1, source_target_pairs={{0,5},{1,2},{2,1},{3,6},{4,7},{5,0},{6,3},{7,4},{8,11},{9,12},{10,... | collective-permute-start | bytes 393224 | tf_op jit(solution)/shard_map/ppermute | solution.py:582
  15.3 0.1 collective-permute-done.7.got_ref
  15.5 2.8 %collective-permute-start.8 = (bf16[16,2048]{1,0:T(8,128)(2,1)S(1)}, bf16[16,2048]{1,0:T(8,128)(2,1)S(1)}, u32[]{:S(2)}, u32[]{:S(2)}) collective-permute-start(bf16[16,2048]{1,0:T(8,128)(2,1)S(1)} %get-tuple-element.69), channel_id=1, source_target_pairs={{0,9},{1,8},{2,11},{3,10},{4,13},{5,12},{6,15},{7,14},{8,1},{9,0},... | collective-permute-start | bytes 196616 | tf_op jit(solution)/shard_map/ppermute | solution.py:582
  18.3 0.2 collective-permute-done.5.got_ref
  18.5 2.4 %collective-permute-start.6 = (bf16[16,2048]{1,0:T(8,128)(2,1)S(1)}, bf16[16,2048]{1,0:T(8,128)(2,1)S(1)}, u32[]{:S(2)}, u32[]{:S(2)}) collective-permute-start(bf16[16,2048]{1,0:T(8,128)(2,1)S(1)} %get-tuple-element.65), channel_id=1, source_target_pairs={{0,9},{1,8},{2,11},{3,10},{4,13},{5,12},{6,15},{7,14},{8,1},{9,0},... | collective-permute-start | bytes 196616 | tf_op jit(solution)/shard_map/ppermute | solution.py:582
  20.9 0.0 collective-permute-done.8.refs_1_
  20.9 3.0 %correlate_late.1 = (f32[256,128]{1,0:T(8,128)S(1)}, f32[256,512]{1,0:T(8,128)S(1)}) custom-call(bf16[16,2048]{1,0:T(8,128)(2,1)S(1)} %get-tuple-element.68.refs_0_, bf16[16,2048]{1,0:T(8,128)(2,1)S(1)} %collective-permute-done.8.refs_1_, bf16[1,8576,128]{2,1,0:T(8,128)(2,1)S(1)} %get-tuple-element.66.refs_2_.refs_1_), custom_call_target="tpu_custom_call" | custom-call | flops 2147483648 | bytes 4194304 | tf_op jit(solution)/shard_map/correlate_late/pallas_call | solution.py:312
  23.9 1.1 %collective-permute-done.6.refs_1_ = bf16[16,2048]{1,0:T(8,128)(2,1)S(1)} collective-permute-done((bf16[16,2048]{1,0:T(8,128)(2,1)S(1)}, bf16[16,2048]{1,0:T(8,128)(2,1)S(1)}, u32[]{:S(2)}, u32[]{:S(2)}) %collective-permute-start.6) | collective-permute-done | bytes 65568 | tf_op jit(solution)/shard_map/ppermute | solution.py:582
  25.0 2.0 %correlate_early.1 = (f32[4,136,128]{2,1,0:T(8,128)S(1)}, f32[4,136,128]{2,1,0:T(8,128)S(1)}, bf16[8,320,256]{2,1,0:T(8,128)(2,1)S(1)}) custom-call(bf16[16,2048]{1,0:T(8,128)(2,1)S(1)} %get-tuple-element.64.refs_0_, bf16[16,2048]{1,0:T(8,128)(2,1)S(1)} %collective-permute-done.6.refs_1_, bf16[1,8576,128]{2,1,0:T(8,128)(2,1)S(1)} %get-tuple-element.66.refs_2_.refs_1_, ...), custom_call_target="tpu_custom_call" | custom-call | flops 4294967296 | bytes 16777216 | tf_op jit(solution)/shard_map/correlate_early/pallas_call | solution.py:338
  27.0 1.5 %collective-permute-start.9 = (f32[4,136,128]{2,1,0:T(8,128)S(1)}, f32[4,136,128]{2,1,0:T(8,128)S(1)}, u32[]{:S(2)}, u32[]{:S(2)}) collective-permute-start(f32[4,136,128]{2,1,0:T(8,128)S(1)} %get-tuple-element.73), channel_id=1, source_target_pairs={{0,3},{1,4},{2,7},{3,0},{4,1},{5,6},{6,5},{7,2},{8,13},{9,10},{10,... | collective-permute-start | bytes 835592 | tf_op jit(solution)/shard_map/ppermute | solution.py:582
  28.4 1.3 %correlate_rest.1 = (f32[4,128,128]{2,1,0:T(8,128)S(1)}, f32[4,128,128]{2,1,0:T(8,128)S(1)}) custom-call(bf16[8,320,256]{2,1,0:T(8,128)(2,1)S(1)} %get-tuple-element.74.refs_0_, bf16[1,8576,128]{2,1,0:T(8,128)(2,1)S(1)} %get-tuple-element.66.refs_2_.refs_1_, f32[256,512]{1,0:T(8,128)S(1)} %get-tuple-element.71.refs_7_.refs_2_), custom_call_target="tpu_custom_call" | custom-call | flops 8589934592 | bytes 16777216 | tf_op jit(solution)/shard_map/correlate_rest/pallas_call | solution.py:353
  29.8 0.4 collective-permute-start.13
  30.2 2.8 %collective-permute-done.9.got_ref = f32[4,136,128]{2,1,0:T(8,128)S(1)} collective-permute-done((f32[4,136,128]{2,1,0:T(8,128)S(1)}, f32[4,136,128]{2,1,0:T(8,128)S(1)}, u32[]{:S(2)}, u32[]{:S(2)}) %collective-permute-start.9) | collective-permute-done | bytes 278560 | tf_op jit(solution)/shard_map/ppermute | solution.py:582
  33.0 1.2 %collective-permute-start.10 = (f32[2,136,128]{2,1,0:T(8,128)S(1)}, f32[2,136,128]{2,1,0:T(8,128)S(1)}, u32[]{:S(2)}, u32[]{:S(2)}) collective-permute-start(f32[2,136,128]{2,1,0:T(8,128)S(1)} %get-tuple-element.77), channel_id=1, source_target_pairs={{0,5},{1,2},{2,1},{3,6},{4,7},{5,0},{6,3},{7,4},{8,11},{9,12},{10,... | collective-permute-start | bytes 417800 | tf_op jit(solution)/shard_map/ppermute | solution.py:582
  34.2 1.6 %collective-permute-done.13.got_ref = f32[4,128,128]{2,1,0:T(8,128)S(1)} collective-permute-done((f32[4,128,128]{2,1,0:T(8,128)S(1)}, f32[4,128,128]{2,1,0:T(8,128)S(1)}, u32[]{:S(2)}, u32[]{:S(2)}) %collective-permute-start.13) | collective-permute-done | bytes 262176 | tf_op jit(solution)/shard_map/ppermute | solution.py:582
  35.9 1.1 %collective-permute-start.14 = (f32[2,128,128]{2,1,0:T(8,128)S(1)}, f32[2,128,128]{2,1,0:T(8,128)S(1)}, u32[]{:S(2)}, u32[]{:S(2)}) collective-permute-start(f32[2,128,128]{2,1,0:T(8,128)S(1)} %get-tuple-element.88), channel_id=1, source_target_pairs={{0,5},{1,2},{2,1},{3,6},{4,7},{5,0},{6,3},{7,4},{8,11},{9,12},{10,... | collective-permute-start | bytes 393224 | tf_op jit(solution)/shard_map/ppermute | solution.py:582
  36.9 0.8 %collective-permute-done.10.got_ref = f32[2,136,128]{2,1,0:T(8,128)S(1)} collective-permute-done((f32[2,136,128]{2,1,0:T(8,128)S(1)}, f32[2,136,128]{2,1,0:T(8,128)S(1)}, u32[]{:S(2)}, u32[]{:S(2)}) %collective-permute-start.10) | collective-permute-done | bytes 139296 | tf_op jit(solution)/shard_map/ppermute | solution.py:582
  37.7 2.5 %collective-permute-start.11 = (f32[1,136,128]{2,1,0:T(8,128)S(1)}, f32[1,136,128]{2,1,0:T(8,128)S(1)}, u32[]{:S(2)}, u32[]{:S(2)}) collective-permute-start(f32[1,136,128]{2,1,0:T(8,128)S(1)} %get-tuple-element.79), channel_id=1, source_target_pairs={{0,9},{1,8},{2,11},{3,10},{4,13},{5,12},{6,15},{7,14},{8,1},{9,0},... | collective-permute-start | bytes 208904 | tf_op jit(solution)/shard_map/ppermute | solution.py:582
  40.2 0.1 collective-permute-done.14.got_ref
  40.3 2.6 %collective-permute-start.15 = (f32[1,128,128]{2,1,0:T(8,128)S(1)}, f32[1,128,128]{2,1,0:T(8,128)S(1)}, u32[]{:S(2)}, u32[]{:S(2)}) collective-permute-start(f32[1,128,128]{2,1,0:T(8,128)S(1)} %get-tuple-element.90), channel_id=1, source_target_pairs={{0,9},{1,8},{2,11},{3,10},{4,13},{5,12},{6,15},{7,14},{8,1},{9,0},... | collective-permute-start | bytes 196616 | tf_op jit(solution)/shard_map/ppermute | solution.py:582
  42.9 0.0 collective-permute-done.11.refs_1_
  42.9 2.2 %collective-permute-start.12 = (f32[72,128]{1,0:T(8,128)S(1)}, f32[72,128]{1,0:T(8,128)S(1)}, u32[]{:S(2)}, u32[]{:S(2)}) collective-permute-start(f32[72,128]{1,0:T(8,128)S(1)} %get-tuple-element.81), channel_id=1, source_target_pairs={{0,1},{1,0},{2,3},{3,2},{4,5},{5,4},{6,7},{7,6},{8,9},{9,8},{10,11... | collective-permute-start | bytes 110600 | tf_op jit(solution)/shard_map/ppermute | solution.py:579
  45.1 2.1 %collective-permute-done.15.refs_1_ = f32[1,128,128]{2,1,0:T(8,128)S(1)} collective-permute-done((f32[1,128,128]{2,1,0:T(8,128)S(1)}, f32[1,128,128]{2,1,0:T(8,128)S(1)}, u32[]{:S(2)}, u32[]{:S(2)}) %collective-permute-start.15) | collective-permute-done | bytes 65568 | tf_op jit(solution)/shard_map/ppermute | solution.py:582
  47.2 0.2 collective-permute-start.16
  47.4 0.3 scale.1
  47.8 0.7 %collective-permute-done.16.refs_5_ = f32[64,128]{1,0:T(8,128)S(1)} collective-permute-done((f32[64,128]{1,0:T(8,128)S(1)}, f32[64,128]{1,0:T(8,128)S(1)}, u32[]{:S(2)}, u32[]{:S(2)}) %collective-permute-start.16) | collective-permute-done | bytes 32800 | tf_op jit(solution)/shard_map/ppermute | solution.py:579
  48.5 0.8 %finish.1 = f32[256,128]{1,0:T(8,128)} custom-call(f32[64,128]{1,0:T(8,128)S(1)} %get-tuple-element.82.refs_0_, f32[64,128]{1,0:T(8,128)S(1)} %get-tuple-element.83.refs_1_, f32[64,128]{1,0:T(8,128)S(1)} %get-tuple-element.84.refs_2_, f32[64,128]{1,0:T(8,128)S(1)} %get-tuple-element.85.refs_3_, f32[64,128]{1,0:T(8,128)S(1)} %get-tuple-element.91.refs_4_, ...), custom_call_target="tpu_custom_call" | custom-call | flops 262144 | bytes 262144 | tf_op jit(solution)/shard_map/finish/pallas_call | solution.py:482
  (16 shorter events, 0.3 us)
Async XLA Ops:
  0.0 1.3 %copy-start.1 = (bf16[128,4096]{1,0:T(8,128)(2,1)S(1)}, bf16[128,4096]{1,0:T(8,128)(2,1)}, u32[]{:S(2)}) copy-start(bf16[128,4096]{1,0:T(8,128)(2,1)} %refs_0_.5) | copy-start | bytes 3145732
  0.0 0.7 %copy-start.2 = (s32[2]{0:T(128)S(1)}, s32[2]{0:T(128)}, u32[]{:S(2)}) copy-start(s32[2]{0:T(128)} %refs_0_.3) | copy-start | bytes 28
  1.3 1.5 %copy-start = (bf16[2,64,8,512]{3,2,1,0:T(8,128)(2,1)S(1)}, bf16[2,64,8,512]{3,2,1,0:T(8,128)(2,1)}, u32[]{:S(2)}) copy-start(bf16[2,64,8,512]{3,2,1,0:T(8,128)(2,1)} %param.4) | copy-start | bytes 3145732
  1.8 2.1 %collective-permute-start.1 = (bf16[128,2048]{1,0:T(8,128)(2,1)S(1)}, bf16[128,2048]{1,0:T(8,128)(2,1)S(1)}, u32[]{:S(2)}, u32[]{:S(2)}) collective-permute-start(bf16[128,2048]{1,0:T(8,128)(2,1)S(1)} %get-tuple-element.49.refs_2_), channel_id=1, source_target_pairs={{0,1},{1,0},{2,3},{3,2},{4,5},{5,4},{6,7},{7,6},{8,9},{9,8},{10,11... | collective-permute-start | bytes 1572872 | tf_op jit(solution)/shard_map/ppermute | solution.py:579
  2.7 3.8 %collective-permute-start = (bf16[128,2048]{1,0:T(8,128)(2,1)S(1)}, bf16[128,2048]{1,0:T(8,128)(2,1)S(1)}, u32[]{:S(2)}, u32[]{:S(2)}) collective-permute-start(bf16[128,2048]{1,0:T(8,128)(2,1)S(1)} %get-tuple-element.51.refs_1_), channel_id=1, source_target_pairs={{0,1},{1,0},{2,3},{3,2},{4,5},{5,4},{6,7},{7,6},{8,9},{9,8},{10,11... | collective-permute-start | bytes 1572872 | tf_op jit(solution)/shard_map/ppermute | solution.py:579
  2.9 4.5 %collective-permute-start.3 = (bf16[512,512]{1,0:T(8,128)(2,1)S(1)}, bf16[512,512]{1,0:T(8,128)(2,1)S(1)}, u32[]{:S(2)}, u32[]{:S(2)}) collective-permute-start(bf16[512,512]{1,0:T(8,128)(2,1)S(1)} %give.1), channel_id=1, source_target_pairs={{0,1},{1,0},{2,3},{3,2},{4,5},{5,4},{6,7},{7,6},{8,9},{9,8},{10,11... | collective-permute-start | bytes 1572872 | tf_op jit(solution)/shard_map/ppermute | solution.py:579
  3.9 6.8 %collective-permute-start.4 = (bf16[64,2048]{1,0:T(8,128)(2,1)S(1)}, bf16[64,2048]{1,0:T(8,128)(2,1)S(1)}, u32[]{:S(2)}, u32[]{:S(2)}) collective-permute-start(bf16[64,2048]{1,0:T(8,128)(2,1)S(1)} %get-tuple-element.56.refs_1_), channel_id=1, source_target_pairs={{0,3},{1,4},{2,7},{3,0},{4,1},{5,6},{6,5},{7,2},{8,13},{9,10},{10,... | collective-permute-start | bytes 786440 | tf_op jit(solution)/shard_map/ppermute | solution.py:582
  6.6 7.4 %collective-permute-start.2 = (bf16[64,2048]{1,0:T(8,128)(2,1)S(1)}, bf16[64,2048]{1,0:T(8,128)(2,1)S(1)}, u32[]{:S(2)}, u32[]{:S(2)}) collective-permute-start(bf16[64,2048]{1,0:T(8,128)(2,1)S(1)} %get-tuple-element.55.refs_1_), channel_id=1, source_target_pairs={{0,3},{1,4},{2,7},{3,0},{4,1},{5,6},{6,5},{7,2},{8,13},{9,10},{10,... | collective-permute-start | bytes 786440 | tf_op jit(solution)/shard_map/ppermute | solution.py:582
  10.7 4.8 %collective-permute-start.7 = (bf16[32,2048]{1,0:T(8,128)(2,1)S(1)}, bf16[32,2048]{1,0:T(8,128)(2,1)S(1)}, u32[]{:S(2)}, u32[]{:S(2)}) collective-permute-start(bf16[32,2048]{1,0:T(8,128)(2,1)S(1)} %get-tuple-element.67), channel_id=1, source_target_pairs={{0,5},{1,2},{2,1},{3,6},{4,7},{5,0},{6,3},{7,4},{8,11},{9,12},{10,... | collective-permute-start | bytes 393224 | tf_op jit(solution)/shard_map/ppermute | solution.py:582
  14.0 4.5 %collective-permute-start.5 = (bf16[32,2048]{1,0:T(8,128)(2,1)S(1)}, bf16[32,2048]{1,0:T(8,128)(2,1)S(1)}, u32[]{:S(2)}, u32[]{:S(2)}) collective-permute-start(bf16[32,2048]{1,0:T(8,128)(2,1)S(1)} %get-tuple-element.63), channel_id=1, source_target_pairs={{0,5},{1,2},{2,1},{3,6},{4,7},{5,0},{6,3},{7,4},{8,11},{9,12},{10,... | collective-permute-start | bytes 393224 | tf_op jit(solution)/shard_map/ppermute | solution.py:582
  15.5 5.4 %collective-permute-start.8 = (bf16[16,2048]{1,0:T(8,128)(2,1)S(1)}, bf16[16,2048]{1,0:T(8,128)(2,1)S(1)}, u32[]{:S(2)}, u32[]{:S(2)}) collective-permute-start(bf16[16,2048]{1,0:T(8,128)(2,1)S(1)} %get-tuple-element.69), channel_id=1, source_target_pairs={{0,9},{1,8},{2,11},{3,10},{4,13},{5,12},{6,15},{7,14},{8,1},{9,0},... | collective-permute-start | bytes 196616 | tf_op jit(solution)/shard_map/ppermute | solution.py:582
  18.5 6.5 %collective-permute-start.6 = (bf16[16,2048]{1,0:T(8,128)(2,1)S(1)}, bf16[16,2048]{1,0:T(8,128)(2,1)S(1)}, u32[]{:S(2)}, u32[]{:S(2)}) collective-permute-start(bf16[16,2048]{1,0:T(8,128)(2,1)S(1)} %get-tuple-element.65), channel_id=1, source_target_pairs={{0,9},{1,8},{2,11},{3,10},{4,13},{5,12},{6,15},{7,14},{8,1},{9,0},... | collective-permute-start | bytes 196616 | tf_op jit(solution)/shard_map/ppermute | solution.py:582
  27.0 6.0 %collective-permute-start.9 = (f32[4,136,128]{2,1,0:T(8,128)S(1)}, f32[4,136,128]{2,1,0:T(8,128)S(1)}, u32[]{:S(2)}, u32[]{:S(2)}) collective-permute-start(f32[4,136,128]{2,1,0:T(8,128)S(1)} %get-tuple-element.73), channel_id=1, source_target_pairs={{0,3},{1,4},{2,7},{3,0},{4,1},{5,6},{6,5},{7,2},{8,13},{9,10},{10,... | collective-permute-start | bytes 835592 | tf_op jit(solution)/shard_map/ppermute | solution.py:582
  29.8 6.0 %collective-permute-start.13 = (f32[4,128,128]{2,1,0:T(8,128)S(1)}, f32[4,128,128]{2,1,0:T(8,128)S(1)}, u32[]{:S(2)}, u32[]{:S(2)}) collective-permute-start(f32[4,128,128]{2,1,0:T(8,128)S(1)} %get-tuple-element.75.refs_0_), channel_id=1, source_target_pairs={{0,3},{1,4},{2,7},{3,0},{4,1},{5,6},{6,5},{7,2},{8,13},{9,10},{10,... | collective-permute-start | bytes 786440 | tf_op jit(solution)/shard_map/ppermute | solution.py:582
  33.0 4.7 %collective-permute-start.10 = (f32[2,136,128]{2,1,0:T(8,128)S(1)}, f32[2,136,128]{2,1,0:T(8,128)S(1)}, u32[]{:S(2)}, u32[]{:S(2)}) collective-permute-start(f32[2,136,128]{2,1,0:T(8,128)S(1)} %get-tuple-element.77), channel_id=1, source_target_pairs={{0,5},{1,2},{2,1},{3,6},{4,7},{5,0},{6,3},{7,4},{8,11},{9,12},{10,... | collective-permute-start | bytes 417800 | tf_op jit(solution)/shard_map/ppermute | solution.py:582
  35.9 4.5 %collective-permute-start.14 = (f32[2,128,128]{2,1,0:T(8,128)S(1)}, f32[2,128,128]{2,1,0:T(8,128)S(1)}, u32[]{:S(2)}, u32[]{:S(2)}) collective-permute-start(f32[2,128,128]{2,1,0:T(8,128)S(1)} %get-tuple-element.88), channel_id=1, source_target_pairs={{0,5},{1,2},{2,1},{3,6},{4,7},{5,0},{6,3},{7,4},{8,11},{9,12},{10,... | collective-permute-start | bytes 393224 | tf_op jit(solution)/shard_map/ppermute | solution.py:582
  37.7 5.2 %collective-permute-start.11 = (f32[1,136,128]{2,1,0:T(8,128)S(1)}, f32[1,136,128]{2,1,0:T(8,128)S(1)}, u32[]{:S(2)}, u32[]{:S(2)}) collective-permute-start(f32[1,136,128]{2,1,0:T(8,128)S(1)} %get-tuple-element.79), channel_id=1, source_target_pairs={{0,9},{1,8},{2,11},{3,10},{4,13},{5,12},{6,15},{7,14},{8,1},{9,0},... | collective-permute-start | bytes 208904 | tf_op jit(solution)/shard_map/ppermute | solution.py:582
  40.3 6.8 %collective-permute-start.15 = (f32[1,128,128]{2,1,0:T(8,128)S(1)}, f32[1,128,128]{2,1,0:T(8,128)S(1)}, u32[]{:S(2)}, u32[]{:S(2)}) collective-permute-start(f32[1,128,128]{2,1,0:T(8,128)S(1)} %get-tuple-element.90), channel_id=1, source_target_pairs={{0,9},{1,8},{2,11},{3,10},{4,13},{5,12},{6,15},{7,14},{8,1},{9,0},... | collective-permute-start | bytes 196616 | tf_op jit(solution)/shard_map/ppermute | solution.py:582
  42.9 4.5 %collective-permute-start.12 = (f32[72,128]{1,0:T(8,128)S(1)}, f32[72,128]{1,0:T(8,128)S(1)}, u32[]{:S(2)}, u32[]{:S(2)}) collective-permute-start(f32[72,128]{1,0:T(8,128)S(1)} %get-tuple-element.81), channel_id=1, source_target_pairs={{0,1},{1,0},{2,3},{3,2},{4,5},{5,4},{6,7},{7,6},{8,9},{9,8},{10,11... | collective-permute-start | bytes 110600 | tf_op jit(solution)/shard_map/ppermute | solution.py:579
  47.2 1.3 %collective-permute-start.16 = (f32[64,128]{1,0:T(8,128)S(1)}, f32[64,128]{1,0:T(8,128)S(1)}, u32[]{:S(2)}, u32[]{:S(2)}) collective-permute-start(f32[64,128]{1,0:T(8,128)S(1)} %get-tuple-element.92), channel_id=1, source_target_pairs={{0,1},{1,0},{2,3},{3,2},{4,5},{5,4},{6,7},{7,6},{8,9},{9,8},{10,11... | collective-permute-start | bytes 98312 | tf_op jit(solution)/shard_map/ppermute | solution.py:579

commit v7 on v6

--- a/solution.py
+++ b/solution.py
@@ -122,7 +122,7 @@
 
 def bits_of(devices):
     x, z, *rest = [1 << i for i in range(1, devices.bit_length() - 1)]
-    return [x, z] + rest, [z, x] + rest
+    return [z, x] + rest, [x, z] + rest
 
 
 def panel_of(device, devices):

time: 49.4 us -> 49.4 us (level)
  starting transfers between devices: 24.9 us -> 26 us
  waiting for transfers between devices: 9.84 us -> 8.84 us
    ppermute x12, starting transfers between devices: 21.3 us -> 23.4 us  [exchange(): lax.ppermute(value, 'win', [(d, d ^ 1 ^ orders[panel_of(d, devices)][step...]
    ppermute x12, waiting for transfers between devices: 8.72 us -> 7.67 us  [exchange(): lax.ppermute(value, 'win', [(d, d ^ 1 ^ orders[panel_of(d, devices)][step...]
    ppermute x5, starting transfers between devices: 3.55 us -> 2.52 us  [sibling(): return lax.ppermute(value, 'win', [(d, d ^ 1) for d in range(devices)])]
  transfers between devices with their start and end apart: 17 -> 17, of which waited for: 10 -> 8; matrix products, arithmetic and copies ran while one was open for 0% -> 0% of each run, Pallas kernels for 20% -> 20%
where the time goes in v7:
time: 49.4 us; the launch traced here: 49.3 us
  starting transfers between devices  26 us (53%)
  Pallas kernels  13.6 us (28%)
  waiting for transfers between devices  8.84 us (18%)
  local copies, waits for them, and re-layouts  0.75 us (2%)
    ppermute x12, starting transfers between devices, exchange(): lax.ppermute(value, 'win', [(d, d ^ 1 ^ orders[panel_of(d, devices)][step...  23.4 us
    ppermute x12, waiting for transfers between devices, exchange(): lax.ppermute(value, 'win', [(d, d ^ 1 ^ orders[panel_of(d, devices)][step...  7.67 us
    pallas_call x1, Pallas kernels, correlate_late(): pl.pallas_call(lambda *refs: late_kernel(*refs, phases=phases), out_shape...  2.99 us
    ppermute x5, starting transfers between devices, sibling(): return lax.ppermute(value, 'win', [(d, d ^ 1) for d in range(devices)])  2.52 us
    pallas_call x1, Pallas kernels, shifted(): pl.pallas_call(lambda *refs: shift_kernel(*refs, phases=phases, devices=2...  2.24 us
    pallas_call x2, Pallas kernels, energy_of(): pl.pallas_call(lambda *refs: energy_kernel(*refs, phases=phases), out_sha...  2.17 us
    pallas_call x1, Pallas kernels, correlate_early(): pl.pallas_call(lambda *refs: early_kernel(*refs, phases=phases, devices=d...  1.99 us
    pallas_call x1, Pallas kernels, correlate_rest(): pl.pallas_call(lambda *refs: rest_kernel(*refs, phases=phases, devices=de...  1.33 us
  transfers between devices with their start and end apart: 17, of which 8 were waited for; matrix products, arithmetic and copies ran while one was open for 0% of the time, Pallas kernels for 20%

profile of v7, /device:TPU:0, one launch (start us, length us, event | category | flops | bytes accessed | tf_op | source)
XLA Modules:
  0.0 49.3 jit_solution(9988806244199859131)
XLA Ops:
  0.0 0.7 %copy-done.2 = s32[2]{0:T(128)S(1)} copy-done((s32[2]{0:T(128)S(1)}, s32[2]{0:T(128)}, u32[]{:S(2)}) %copy-start.2) | copy-done | bytes 32
  0.7 0.6 %masks.1.refs_1_ = bf16[256,128]{1,0:T(8,128)(2,1)S(1)} custom-call(s32[2]{0:T(128)S(1)} %copy-done.2), custom_call_target="tpu_custom_call" | custom-call | flops 2147483648 | bytes 65536 | tf_op jit(solution)/shard_map/masks/pallas_call | solution.py:514
  1.3 0.0 copy-start
  1.3 0.4 select.2
  1.8 0.5 %collective-permute-start.1 = (bf16[128,2048]{1,0:T(8,128)(2,1)S(1)}, bf16[128,2048]{1,0:T(8,128)(2,1)S(1)}, u32[]{:S(2)}, u32[]{:S(2)}) collective-permute-start(bf16[128,2048]{1,0:T(8,128)(2,1)S(1)} %get-tuple-element.49.refs_2_), channel_id=1, source_target_pairs={{0,1},{1,0},{2,3},{3,2},{4,5},{5,4},{6,7},{7,6},{8,9},{9,8},{10,11... | collective-permute-start | bytes 1572872 | tf_op jit(solution)/shard_map/ppermute | solution.py:579
  2.3 0.4 select.3
  2.7 0.1 collective-permute-start
  2.9 0.5 %collective-permute-start.3 = (bf16[512,512]{1,0:T(8,128)(2,1)S(1)}, bf16[512,512]{1,0:T(8,128)(2,1)S(1)}, u32[]{:S(2)}, u32[]{:S(2)}) collective-permute-start(bf16[512,512]{1,0:T(8,128)(2,1)S(1)} %give.1), channel_id=1, source_target_pairs={{0,1},{1,0},{2,3},{3,2},{4,5},{5,4},{6,7},{7,6},{8,9},{9,8},{10,11... | collective-permute-start | bytes 1572872 | tf_op jit(solution)/shard_map/ppermute | solution.py:579
  3.4 0.4 collective-permute-done.1.got_ref
  3.8 0.1 add.10
  3.9 2.8 %collective-permute-start.4 = (bf16[64,2048]{1,0:T(8,128)(2,1)S(1)}, bf16[64,2048]{1,0:T(8,128)(2,1)S(1)}, u32[]{:S(2)}, u32[]{:S(2)}) collective-permute-start(bf16[64,2048]{1,0:T(8,128)(2,1)S(1)} %get-tuple-element.56.refs_1_), channel_id=1, source_target_pairs={{0,5},{1,2},{2,1},{3,6},{4,7},{5,0},{6,3},{7,4},{8,11},{9,12},{10,... | collective-permute-start | bytes 786440 | tf_op jit(solution)/shard_map/ppermute | solution.py:582
  6.6 0.0 collective-permute-done.got_ref
  6.6 0.1 add.11
  6.7 0.8 %collective-permute-start.2 = (bf16[64,2048]{1,0:T(8,128)(2,1)S(1)}, bf16[64,2048]{1,0:T(8,128)(2,1)S(1)}, u32[]{:S(2)}, u32[]{:S(2)}) collective-permute-start(bf16[64,2048]{1,0:T(8,128)(2,1)S(1)} %get-tuple-element.55.refs_1_), channel_id=1, source_target_pairs={{0,5},{1,2},{2,1},{3,6},{4,7},{5,0},{6,3},{7,4},{8,11},{9,12},{10,... | collective-permute-start | bytes 786440 | tf_op jit(solution)/shard_map/ppermute | solution.py:582
  7.5 2.2 %shift_templates.1 = (bf16[1,8576,128]{2,1,0:T(8,128)(2,1)S(1)}, f32[8,128]{1,0:T(8,128)S(1)}) custom-call(bf16[2,512,512]{2,1,0:T(8,128)(2,1)S(1)} %bitcast.2, bf16[512,512]{1,0:T(8,128)(2,1)S(1)} %collective-permute-done.3.refs_1_, bf16[64,2048]{1,0:T(8,128)(2,1)S(1)} %get-tuple-element.54.refs_2_.refs_0_.kept_ref), custom_call_target="tpu_custom_call" | custom-call | flops 268435456 | bytes 1048576 | tf_op jit(solution)/shard_map/shift_templates/pallas_call | solution.py:108
  9.7 1.0 %energy.2 = (f32[256,128]{1,0:T(8,128)S(1)}, f32[256,128]{1,0:T(8,128)S(1)}) custom-call(bf16[64,2048]{1,0:T(8,128)(2,1)S(1)} %get-tuple-element.53.refs_0_.kept_ref, bf16[64,2048]{1,0:T(8,128)(2,1)S(1)} %get-tuple-element.56.refs_1_, f32[8,128]{1,0:T(8,128)S(1)} %get-tuple-element.57.refs_2_.refs_3_), custom_call_target="tpu_custom_call" | custom-call | flops 268435456 | bytes 1048576 | tf_op jit(solution)/shard_map/energy/pallas_call | solution.py:200
  10.7 0.0 collective-permute-done.4.got_ref
  10.8 1.9 %collective-permute-start.7 = (bf16[32,2048]{1,0:T(8,128)(2,1)S(1)}, bf16[32,2048]{1,0:T(8,128)(2,1)S(1)}, u32[]{:S(2)}, u32[]{:S(2)}) collective-permute-start(bf16[32,2048]{1,0:T(8,128)(2,1)S(1)} %get-tuple-element.67), channel_id=1, source_target_pairs={{0,3},{1,4},{2,7},{3,0},{4,1},{5,6},{6,5},{7,2},{8,13},{9,10},{10,... | collective-permute-start | bytes 393224 | tf_op jit(solution)/shard_map/ppermute | solution.py:582
  12.7 1.2 %energy.3 = (f32[256,128]{1,0:T(8,128)S(1)}, f32[256,128]{1,0:T(8,128)}) custom-call(bf16[64,2048]{1,0:T(8,128)(2,1)S(1)} %get-tuple-element.54.refs_2_.refs_0_.kept_ref, bf16[64,2048]{1,0:T(8,128)(2,1)S(1)} %get-tuple-element.55.refs_1_, f32[256,128]{1,0:T(8,128)S(1)} %get-tuple-element.58.refs_2_, bf16[32,2048]{1,0:T(8,128)(2,1)S(1)} %get-tuple-element.60.refs_3_.kept_ref), custom_call_target="tpu_custom_call" | custom-call | flops 268435456 | bytes 1048576 | tf_op jit(solution)/shard_map/energy/pallas_call | solution.py:200
  13.9 0.0 collective-permute-done.2.got_ref
  13.9 1.3 %collective-permute-start.5 = (bf16[32,2048]{1,0:T(8,128)(2,1)S(1)}, bf16[32,2048]{1,0:T(8,128)(2,1)S(1)}, u32[]{:S(2)}, u32[]{:S(2)}) collective-permute-start(bf16[32,2048]{1,0:T(8,128)(2,1)S(1)} %get-tuple-element.63), channel_id=1, source_target_pairs={{0,3},{1,4},{2,7},{3,0},{4,1},{5,6},{6,5},{7,2},{8,13},{9,10},{10,... | collective-permute-start | bytes 393224 | tf_op jit(solution)/shard_map/ppermute | solution.py:582
  15.2 0.1 collective-permute-done.7.got_ref
  15.4 2.9 %collective-permute-start.8 = (bf16[16,2048]{1,0:T(8,128)(2,1)S(1)}, bf16[16,2048]{1,0:T(8,128)(2,1)S(1)}, u32[]{:S(2)}, u32[]{:S(2)}) collective-permute-start(bf16[16,2048]{1,0:T(8,128)(2,1)S(1)} %get-tuple-element.69), channel_id=1, source_target_pairs={{0,9},{1,8},{2,11},{3,10},{4,13},{5,12},{6,15},{7,14},{8,1},{9,0},... | collective-permute-start | bytes 196616 | tf_op jit(solution)/shard_map/ppermute | solution.py:582
  18.3 0.1 collective-permute-done.5.got_ref
  18.4 2.5 %collective-permute-start.6 = (bf16[16,2048]{1,0:T(8,128)(2,1)S(1)}, bf16[16,2048]{1,0:T(8,128)(2,1)S(1)}, u32[]{:S(2)}, u32[]{:S(2)}) collective-permute-start(bf16[16,2048]{1,0:T(8,128)(2,1)S(1)} %get-tuple-element.65), channel_id=1, source_target_pairs={{0,9},{1,8},{2,11},{3,10},{4,13},{5,12},{6,15},{7,14},{8,1},{9,0},... | collective-permute-start | bytes 196616 | tf_op jit(solution)/shard_map/ppermute | solution.py:582
  20.9 0.0 collective-permute-done.8.refs_1_
  20.9 3.0 %correlate_late.1 = (f32[256,128]{1,0:T(8,128)S(1)}, f32[256,512]{1,0:T(8,128)S(1)}) custom-call(bf16[16,2048]{1,0:T(8,128)(2,1)S(1)} %get-tuple-element.68.refs_0_, bf16[16,2048]{1,0:T(8,128)(2,1)S(1)} %collective-permute-done.8.refs_1_, bf16[1,8576,128]{2,1,0:T(8,128)(2,1)S(1)} %get-tuple-element.66.refs_2_.refs_1_), custom_call_target="tpu_custom_call" | custom-call | flops 2147483648 | bytes 4194304 | tf_op jit(solution)/shard_map/correlate_late/pallas_call | solution.py:312
  23.9 1.0 %collective-permute-done.6.refs_1_ = bf16[16,2048]{1,0:T(8,128)(2,1)S(1)} collective-permute-done((bf16[16,2048]{1,0:T(8,128)(2,1)S(1)}, bf16[16,2048]{1,0:T(8,128)(2,1)S(1)}, u32[]{:S(2)}, u32[]{:S(2)}) %collective-permute-start.6) | collective-permute-done | bytes 65568 | tf_op jit(solution)/shard_map/ppermute | solution.py:582
  24.9 2.0 %correlate_early.1 = (f32[4,136,128]{2,1,0:T(8,128)S(1)}, f32[4,136,128]{2,1,0:T(8,128)S(1)}, bf16[8,320,256]{2,1,0:T(8,128)(2,1)S(1)}) custom-call(bf16[16,2048]{1,0:T(8,128)(2,1)S(1)} %get-tuple-element.64.refs_0_, bf16[16,2048]{1,0:T(8,128)(2,1)S(1)} %collective-permute-done.6.refs_1_, bf16[1,8576,128]{2,1,0:T(8,128)(2,1)S(1)} %get-tuple-element.66.refs_2_.refs_1_, ...), custom_call_target="tpu_custom_call" | custom-call | flops 4294967296 | bytes 16777216 | tf_op jit(solution)/shard_map/correlate_early/pallas_call | solution.py:338
  26.9 1.0 %collective-permute-start.9 = (f32[4,136,128]{2,1,0:T(8,128)S(1)}, f32[4,136,128]{2,1,0:T(8,128)S(1)}, u32[]{:S(2)}, u32[]{:S(2)}) collective-permute-start(f32[4,136,128]{2,1,0:T(8,128)S(1)} %get-tuple-element.73), channel_id=1, source_target_pairs={{0,5},{1,2},{2,1},{3,6},{4,7},{5,0},{6,3},{7,4},{8,11},{9,12},{10,... | collective-permute-start | bytes 835592 | tf_op jit(solution)/shard_map/ppermute | solution.py:582
  27.9 1.3 %correlate_rest.1 = (f32[4,128,128]{2,1,0:T(8,128)S(1)}, f32[4,128,128]{2,1,0:T(8,128)S(1)}) custom-call(bf16[8,320,256]{2,1,0:T(8,128)(2,1)S(1)} %get-tuple-element.74.refs_0_, bf16[1,8576,128]{2,1,0:T(8,128)(2,1)S(1)} %get-tuple-element.66.refs_2_.refs_1_, f32[256,512]{1,0:T(8,128)S(1)} %get-tuple-element.71.refs_7_.refs_2_), custom_call_target="tpu_custom_call" | custom-call | flops 8589934592 | bytes 16777216 | tf_op jit(solution)/shard_map/correlate_rest/pallas_call | solution.py:353
  29.2 0.9 %collective-permute-start.13 = (f32[4,128,128]{2,1,0:T(8,128)S(1)}, f32[4,128,128]{2,1,0:T(8,128)S(1)}, u32[]{:S(2)}, u32[]{:S(2)}) collective-permute-start(f32[4,128,128]{2,1,0:T(8,128)S(1)} %get-tuple-element.75.refs_0_), channel_id=1, source_target_pairs={{0,5},{1,2},{2,1},{3,6},{4,7},{5,0},{6,3},{7,4},{8,11},{9,12},{10,... | collective-permute-start | bytes 786440 | tf_op jit(solution)/shard_map/ppermute | solution.py:582
  30.1 2.8 %collective-permute-done.9.got_ref = f32[4,136,128]{2,1,0:T(8,128)S(1)} collective-permute-done((f32[4,136,128]{2,1,0:T(8,128)S(1)}, f32[4,136,128]{2,1,0:T(8,128)S(1)}, u32[]{:S(2)}, u32[]{:S(2)}) %collective-permute-start.9) | collective-permute-done | bytes 278560 | tf_op jit(solution)/shard_map/ppermute | solution.py:582
  33.0 1.8 %collective-permute-start.10 = (f32[2,136,128]{2,1,0:T(8,128)S(1)}, f32[2,136,128]{2,1,0:T(8,128)S(1)}, u32[]{:S(2)}, u32[]{:S(2)}) collective-permute-start(f32[2,136,128]{2,1,0:T(8,128)S(1)} %get-tuple-element.77), channel_id=1, source_target_pairs={{0,3},{1,4},{2,7},{3,0},{4,1},{5,6},{6,5},{7,2},{8,13},{9,10},{10,... | collective-permute-start | bytes 417800 | tf_op jit(solution)/shard_map/ppermute | solution.py:582
  34.8 1.0 %collective-permute-done.13.got_ref = f32[4,128,128]{2,1,0:T(8,128)S(1)} collective-permute-done((f32[4,128,128]{2,1,0:T(8,128)S(1)}, f32[4,128,128]{2,1,0:T(8,128)S(1)}, u32[]{:S(2)}, u32[]{:S(2)}) %collective-permute-start.13) | collective-permute-done | bytes 262176 | tf_op jit(solution)/shard_map/ppermute | solution.py:582
  35.8 2.0 %collective-permute-start.14 = (f32[2,128,128]{2,1,0:T(8,128)S(1)}, f32[2,128,128]{2,1,0:T(8,128)S(1)}, u32[]{:S(2)}, u32[]{:S(2)}) collective-permute-start(f32[2,128,128]{2,1,0:T(8,128)S(1)} %get-tuple-element.88), channel_id=1, source_target_pairs={{0,3},{1,4},{2,7},{3,0},{4,1},{5,6},{6,5},{7,2},{8,13},{9,10},{10,... | collective-permute-start | bytes 393224 | tf_op jit(solution)/shard_map/ppermute | solution.py:582
  37.8 0.0 collective-permute-done.10.got_ref
  37.8 2.7 %collective-permute-start.11 = (f32[1,136,128]{2,1,0:T(8,128)S(1)}, f32[1,136,128]{2,1,0:T(8,128)S(1)}, u32[]{:S(2)}, u32[]{:S(2)}) collective-permute-start(f32[1,136,128]{2,1,0:T(8,128)S(1)} %get-tuple-element.79), channel_id=1, source_target_pairs={{0,9},{1,8},{2,11},{3,10},{4,13},{5,12},{6,15},{7,14},{8,1},{9,0},... | collective-permute-start | bytes 208904 | tf_op jit(solution)/shard_map/ppermute | solution.py:582
  40.4 0.0 collective-permute-done.14.got_ref
  40.5 3.0 %collective-permute-start.15 = (f32[1,128,128]{2,1,0:T(8,128)S(1)}, f32[1,128,128]{2,1,0:T(8,128)S(1)}, u32[]{:S(2)}, u32[]{:S(2)}) collective-permute-start(f32[1,128,128]{2,1,0:T(8,128)S(1)} %get-tuple-element.90), channel_id=1, source_target_pairs={{0,9},{1,8},{2,11},{3,10},{4,13},{5,12},{6,15},{7,14},{8,1},{9,0},... | collective-permute-start | bytes 196616 | tf_op jit(solution)/shard_map/ppermute | solution.py:582
  43.4 0.0 collective-permute-done.11.refs_1_
  43.4 1.2 %collective-permute-start.12 = (f32[72,128]{1,0:T(8,128)S(1)}, f32[72,128]{1,0:T(8,128)S(1)}, u32[]{:S(2)}, u32[]{:S(2)}) collective-permute-start(f32[72,128]{1,0:T(8,128)S(1)} %get-tuple-element.81), channel_id=1, source_target_pairs={{0,1},{1,0},{2,3},{3,2},{4,5},{5,4},{6,7},{7,6},{8,9},{9,8},{10,11... | collective-permute-start | bytes 110600 | tf_op jit(solution)/shard_map/ppermute | solution.py:579
  44.6 2.6 %collective-permute-done.15.refs_1_ = f32[1,128,128]{2,1,0:T(8,128)S(1)} collective-permute-done((f32[1,128,128]{2,1,0:T(8,128)S(1)}, f32[1,128,128]{2,1,0:T(8,128)S(1)}, u32[]{:S(2)}, u32[]{:S(2)}) %collective-permute-start.15) | collective-permute-done | bytes 65568 | tf_op jit(solution)/shard_map/ppermute | solution.py:582
  47.3 0.2 collective-permute-start.16
  47.4 0.0 collective-permute-done.12.refs_1_
  47.4 0.3 scale.1
  47.8 0.7 %collective-permute-done.16.refs_5_ = f32[64,128]{1,0:T(8,128)S(1)} collective-permute-done((f32[64,128]{1,0:T(8,128)S(1)}, f32[64,128]{1,0:T(8,128)S(1)}, u32[]{:S(2)}, u32[]{:S(2)}) %collective-permute-start.16) | collective-permute-done | bytes 32800 | tf_op jit(solution)/shard_map/ppermute | solution.py:579
  48.5 0.8 %finish.1 = f32[256,128]{1,0:T(8,128)} custom-call(f32[64,128]{1,0:T(8,128)S(1)} %get-tuple-element.82.refs_0_, f32[64,128]{1,0:T(8,128)S(1)} %get-tuple-element.83.refs_1_, f32[64,128]{1,0:T(8,128)S(1)} %get-tuple-element.84.refs_2_, f32[64,128]{1,0:T(8,128)S(1)} %get-tuple-element.85.refs_3_, f32[64,128]{1,0:T(8,128)S(1)} %get-tuple-element.91.refs_4_, ...), custom_call_target="tpu_custom_call" | custom-call | flops 262144 | bytes 262144 | tf_op jit(solution)/shard_map/finish/pallas_call | solution.py:482
  (16 shorter events, 0.3 us)
Async XLA Ops:
  0.0 1.3 %copy-start.1 = (bf16[128,4096]{1,0:T(8,128)(2,1)S(1)}, bf16[128,4096]{1,0:T(8,128)(2,1)}, u32[]{:S(2)}) copy-start(bf16[128,4096]{1,0:T(8,128)(2,1)} %refs_0_.5) | copy-start | bytes 3145732
  0.0 0.7 %copy-start.2 = (s32[2]{0:T(128)S(1)}, s32[2]{0:T(128)}, u32[]{:S(2)}) copy-start(s32[2]{0:T(128)} %refs_0_.3) | copy-start | bytes 28
  1.3 1.5 %copy-start = (bf16[2,64,8,512]{3,2,1,0:T(8,128)(2,1)S(1)}, bf16[2,64,8,512]{3,2,1,0:T(8,128)(2,1)}, u32[]{:S(2)}) copy-start(bf16[2,64,8,512]{3,2,1,0:T(8,128)(2,1)} %param.4) | copy-start | bytes 3145732
  1.8 2.1 %collective-permute-start.1 = (bf16[128,2048]{1,0:T(8,128)(2,1)S(1)}, bf16[128,2048]{1,0:T(8,128)(2,1)S(1)}, u32[]{:S(2)}, u32[]{:S(2)}) collective-permute-start(bf16[128,2048]{1,0:T(8,128)(2,1)S(1)} %get-tuple-element.49.refs_2_), channel_id=1, source_target_pairs={{0,1},{1,0},{2,3},{3,2},{4,5},{5,4},{6,7},{7,6},{8,9},{9,8},{10,11... | collective-permute-start | bytes 1572872 | tf_op jit(solution)/shard_map/ppermute | solution.py:579
  2.7 3.9 %collective-permute-start = (bf16[128,2048]{1,0:T(8,128)(2,1)S(1)}, bf16[128,2048]{1,0:T(8,128)(2,1)S(1)}, u32[]{:S(2)}, u32[]{:S(2)}) collective-permute-start(bf16[128,2048]{1,0:T(8,128)(2,1)S(1)} %get-tuple-element.51.refs_1_), channel_id=1, source_target_pairs={{0,1},{1,0},{2,3},{3,2},{4,5},{5,4},{6,7},{7,6},{8,9},{9,8},{10,11... | collective-permute-start | bytes 1572872 | tf_op jit(solution)/shard_map/ppermute | solution.py:579
  2.9 4.6 %collective-permute-start.3 = (bf16[512,512]{1,0:T(8,128)(2,1)S(1)}, bf16[512,512]{1,0:T(8,128)(2,1)S(1)}, u32[]{:S(2)}, u32[]{:S(2)}) collective-permute-start(bf16[512,512]{1,0:T(8,128)(2,1)S(1)} %give.1), channel_id=1, source_target_pairs={{0,1},{1,0},{2,3},{3,2},{4,5},{5,4},{6,7},{7,6},{8,9},{9,8},{10,11... | collective-permute-start | bytes 1572872 | tf_op jit(solution)/shard_map/ppermute | solution.py:579
  3.9 6.9 %collective-permute-start.4 = (bf16[64,2048]{1,0:T(8,128)(2,1)S(1)}, bf16[64,2048]{1,0:T(8,128)(2,1)S(1)}, u32[]{:S(2)}, u32[]{:S(2)}) collective-permute-start(bf16[64,2048]{1,0:T(8,128)(2,1)S(1)} %get-tuple-element.56.refs_1_), channel_id=1, source_target_pairs={{0,5},{1,2},{2,1},{3,6},{4,7},{5,0},{6,3},{7,4},{8,11},{9,12},{10,... | collective-permute-start | bytes 786440 | tf_op jit(solution)/shard_map/ppermute | solution.py:582
  6.7 7.2 %collective-permute-start.2 = (bf16[64,2048]{1,0:T(8,128)(2,1)S(1)}, bf16[64,2048]{1,0:T(8,128)(2,1)S(1)}, u32[]{:S(2)}, u32[]{:S(2)}) collective-permute-start(bf16[64,2048]{1,0:T(8,128)(2,1)S(1)} %get-tuple-element.55.refs_1_), channel_id=1, source_target_pairs={{0,5},{1,2},{2,1},{3,6},{4,7},{5,0},{6,3},{7,4},{8,11},{9,12},{10,... | collective-permute-start | bytes 786440 | tf_op jit(solution)/shard_map/ppermute | solution.py:582
  10.8 4.6 %collective-permute-start.7 = (bf16[32,2048]{1,0:T(8,128)(2,1)S(1)}, bf16[32,2048]{1,0:T(8,128)(2,1)S(1)}, u32[]{:S(2)}, u32[]{:S(2)}) collective-permute-start(bf16[32,2048]{1,0:T(8,128)(2,1)S(1)} %get-tuple-element.67), channel_id=1, source_target_pairs={{0,3},{1,4},{2,7},{3,0},{4,1},{5,6},{6,5},{7,2},{8,13},{9,10},{10,... | collective-permute-start | bytes 393224 | tf_op jit(solution)/shard_map/ppermute | solution.py:582
  13.9 4.5 %collective-permute-start.5 = (bf16[32,2048]{1,0:T(8,128)(2,1)S(1)}, bf16[32,2048]{1,0:T(8,128)(2,1)S(1)}, u32[]{:S(2)}, u32[]{:S(2)}) collective-permute-start(bf16[32,2048]{1,0:T(8,128)(2,1)S(1)} %get-tuple-element.63), channel_id=1, source_target_pairs={{0,3},{1,4},{2,7},{3,0},{4,1},{5,6},{6,5},{7,2},{8,13},{9,10},{10,... | collective-permute-start | bytes 393224 | tf_op jit(solution)/shard_map/ppermute | solution.py:582
  15.4 5.5 %collective-permute-start.8 = (bf16[16,2048]{1,0:T(8,128)(2,1)S(1)}, bf16[16,2048]{1,0:T(8,128)(2,1)S(1)}, u32[]{:S(2)}, u32[]{:S(2)}) collective-permute-start(bf16[16,2048]{1,0:T(8,128)(2,1)S(1)} %get-tuple-element.69), channel_id=1, source_target_pairs={{0,9},{1,8},{2,11},{3,10},{4,13},{5,12},{6,15},{7,14},{8,1},{9,0},... | collective-permute-start | bytes 196616 | tf_op jit(solution)/shard_map/ppermute | solution.py:582
  18.4 6.5 %collective-permute-start.6 = (bf16[16,2048]{1,0:T(8,128)(2,1)S(1)}, bf16[16,2048]{1,0:T(8,128)(2,1)S(1)}, u32[]{:S(2)}, u32[]{:S(2)}) collective-permute-start(bf16[16,2048]{1,0:T(8,128)(2,1)S(1)} %get-tuple-element.65), channel_id=1, source_target_pairs={{0,9},{1,8},{2,11},{3,10},{4,13},{5,12},{6,15},{7,14},{8,1},{9,0},... | collective-permute-start | bytes 196616 | tf_op jit(solution)/shard_map/ppermute | solution.py:582
  26.9 6.0 %collective-permute-start.9 = (f32[4,136,128]{2,1,0:T(8,128)S(1)}, f32[4,136,128]{2,1,0:T(8,128)S(1)}, u32[]{:S(2)}, u32[]{:S(2)}) collective-permute-start(f32[4,136,128]{2,1,0:T(8,128)S(1)} %get-tuple-element.73), channel_id=1, source_target_pairs={{0,5},{1,2},{2,1},{3,6},{4,7},{5,0},{6,3},{7,4},{8,11},{9,12},{10,... | collective-permute-start | bytes 835592 | tf_op jit(solution)/shard_map/ppermute | solution.py:582
  29.2 6.6 %collective-permute-start.13 = (f32[4,128,128]{2,1,0:T(8,128)S(1)}, f32[4,128,128]{2,1,0:T(8,128)S(1)}, u32[]{:S(2)}, u32[]{:S(2)}) collective-permute-start(f32[4,128,128]{2,1,0:T(8,128)S(1)} %get-tuple-element.75.refs_0_), channel_id=1, source_target_pairs={{0,5},{1,2},{2,1},{3,6},{4,7},{5,0},{6,3},{7,4},{8,11},{9,12},{10,... | collective-permute-start | bytes 786440 | tf_op jit(solution)/shard_map/ppermute | solution.py:582
  33.0 4.8 %collective-permute-start.10 = (f32[2,136,128]{2,1,0:T(8,128)S(1)}, f32[2,136,128]{2,1,0:T(8,128)S(1)}, u32[]{:S(2)}, u32[]{:S(2)}) collective-permute-start(f32[2,136,128]{2,1,0:T(8,128)S(1)} %get-tuple-element.77), channel_id=1, source_target_pairs={{0,3},{1,4},{2,7},{3,0},{4,1},{5,6},{6,5},{7,2},{8,13},{9,10},{10,... | collective-permute-start | bytes 417800 | tf_op jit(solution)/shard_map/ppermute | solution.py:582
  35.8 4.6 %collective-permute-start.14 = (f32[2,128,128]{2,1,0:T(8,128)S(1)}, f32[2,128,128]{2,1,0:T(8,128)S(1)}, u32[]{:S(2)}, u32[]{:S(2)}) collective-permute-start(f32[2,128,128]{2,1,0:T(8,128)S(1)} %get-tuple-element.88), channel_id=1, source_target_pairs={{0,3},{1,4},{2,7},{3,0},{4,1},{5,6},{6,5},{7,2},{8,13},{9,10},{10,... | collective-permute-start | bytes 393224 | tf_op jit(solution)/shard_map/ppermute | solution.py:582
  37.8 5.6 %collective-permute-start.11 = (f32[1,136,128]{2,1,0:T(8,128)S(1)}, f32[1,136,128]{2,1,0:T(8,128)S(1)}, u32[]{:S(2)}, u32[]{:S(2)}) collective-permute-start(f32[1,136,128]{2,1,0:T(8,128)S(1)} %get-tuple-element.79), channel_id=1, source_target_pairs={{0,9},{1,8},{2,11},{3,10},{4,13},{5,12},{6,15},{7,14},{8,1},{9,0},... | collective-permute-start | bytes 208904 | tf_op jit(solution)/shard_map/ppermute | solution.py:582
  40.5 6.8 %collective-permute-start.15 = (f32[1,128,128]{2,1,0:T(8,128)S(1)}, f32[1,128,128]{2,1,0:T(8,128)S(1)}, u32[]{:S(2)}, u32[]{:S(2)}) collective-permute-start(f32[1,128,128]{2,1,0:T(8,128)S(1)} %get-tuple-element.90), channel_id=1, source_target_pairs={{0,9},{1,8},{2,11},{3,10},{4,13},{5,12},{6,15},{7,14},{8,1},{9,0},... | collective-permute-start | bytes 196616 | tf_op jit(solution)/shard_map/ppermute | solution.py:582
  43.4 4.0 %collective-permute-start.12 = (f32[72,128]{1,0:T(8,128)S(1)}, f32[72,128]{1,0:T(8,128)S(1)}, u32[]{:S(2)}, u32[]{:S(2)}) collective-permute-start(f32[72,128]{1,0:T(8,128)S(1)} %get-tuple-element.81), channel_id=1, source_target_pairs={{0,1},{1,0},{2,3},{3,2},{4,5},{5,4},{6,7},{7,6},{8,9},{9,8},{10,11... | collective-permute-start | bytes 110600 | tf_op jit(solution)/shard_map/ppermute | solution.py:579
  47.3 1.3 %collective-permute-start.16 = (f32[64,128]{1,0:T(8,128)S(1)}, f32[64,128]{1,0:T(8,128)S(1)}, u32[]{:S(2)}, u32[]{:S(2)}) collective-permute-start(f32[64,128]{1,0:T(8,128)S(1)} %get-tuple-element.92), channel_id=1, source_target_pairs={{0,1},{1,0},{2,3},{3,2},{4,5},{5,4},{6,7},{7,6},{8,9},{9,8},{10,11... | collective-permute-start | bytes 98312 | tf_op jit(solution)/shard_map/ppermute | solution.py:579
